TPU v7x, 512 devices: a whole 4x4x16 slice. The times are simulated.
512 devices in a mesh: row: 16 (over y, x), col: 32 (over z, core).
Axes of the slice: x: 4, y: 4, z: 16, core: 2. Of those that a mesh axis runs over, the one named last changes fastest.
Arguments:
- src_feat: bfloat16 [64, 65536], P(None, ('row', 'col')), may hold values from -1 to 1
- tgt_feat: bfloat16 [64, 32768], P(None, 'col'), may hold values from -1 to 1
Outputs:
- src_potential: float32 [65536], P('row')
- tgt_potential: float32 [32768], P('col')
All inputs are finite; a program needn't handle non-finite values.
Results may differ from a plain program's by a relative error of at most 0.0003.
Values may be sent and summed in bfloat16 or wider, within the bound.
No kernel may reach another device: no remote copies, remote signals or barrier semaphores. Data moves between devices by JAX's collectives and lax.ppermute only.
A program may use at most 64 MiB of HBM per device.

v0:
```python
import math

import jax
import jax.numpy as jnp
from jax import lax
from jax.sharding import PartitionSpec as P

ITERS = 2


INV_EPS = 20.0
EPS = 0.05


def squares(feats):
    return jnp.sum(jnp.square(feats.astype(jnp.float32)), axis=0)


def pair_costs(xs, xsq, ys, ysq):
    inner = lax.dot_general(xs, ys, (((0,), (0,)), ((), ())), preferred_element_type=jnp.float32)
    return xsq[:, None] + ysq[None, :] - 2.0 * inner


def blocked(xs, xsq):
    width, count = xs.shape
    size = math.gcd(count, 512)
    number = count // size
    return (xs.reshape(width, number, size).transpose(1, 0, 2), xsq.reshape(number, size))


def row_partials(xs, xsq, tgt_feat, tgt_sq, tgt_pot):
    feat_blocks, sq_blocks = blocked(xs, xsq)

    def row_one_block(args):
        feats, sq = args
        scores = (tgt_pot[None, :] - pair_costs(feats, sq, tgt_feat, tgt_sq)) * INV_EPS
        peak = jnp.max(scores, axis=1)
        return (peak, jnp.sum(jnp.exp(scores - peak[:, None]), axis=1))

    peaks, totals = lax.map(row_one_block, (feat_blocks, sq_blocks))
    return (peaks.reshape(xs.shape[1]), totals.reshape(xs.shape[1]))


def col_partials(xs, xsq, src_pot, tgt_feat, tgt_sq):
    feat_blocks, sq_blocks = blocked(xs, xsq)
    pot_blocks = src_pot.reshape(sq_blocks.shape)

    def col_one_block(args):
        feats, sq, pots = args
        scores = (pots[:, None] - pair_costs(feats, sq, tgt_feat, tgt_sq)) * INV_EPS
        peak = jnp.max(scores, axis=0)
        return (peak, jnp.sum(jnp.exp(scores - peak[None, :]), axis=0))

    peaks, totals = lax.map(col_one_block, (feat_blocks, sq_blocks, pot_blocks))
    peak = jnp.max(peaks, axis=0)
    return (peak, jnp.sum(totals * jnp.exp(peaks - peak[None, :]), axis=0))


def finish(peak, total, count):
    return -EPS * (peak + jnp.log(total) - math.log(count))


def per_device(src_feat, tgt_feat):
    n_col = lax.axis_size("col")
    n_row = lax.axis_size("row")
    tgt_count = tgt_feat.shape[1]
    targets = tgt_count * n_col
    src_count = src_feat.shape[1] * n_col
    sources = src_count * n_row
    tgt_sq = squares(tgt_feat)
    src_block = lax.all_gather(src_feat, "col", axis=1, tiled=True)
    src_sq = squares(src_block)
    tgt_pot = jnp.zeros((tgt_count,), jnp.float32)
    src_pot = jnp.zeros((src_count,), jnp.float32)
    for step in range(ITERS):
        row_peak, row_total = row_partials(src_block, src_sq, tgt_feat, tgt_sq, tgt_pot)
        shared_peak = lax.pmax(row_peak, "col")
        row_total = lax.psum(row_total * jnp.exp(row_peak - shared_peak), "col")
        row_peak = shared_peak
        src_pot = finish(row_peak, row_total, targets)
        col_peak, col_total = col_partials(src_block, src_sq, src_pot, tgt_feat, tgt_sq)
        shared_top = lax.pmax(col_peak, "row")
        col_total = lax.psum(col_total * jnp.exp(col_peak - shared_top), "row")
        col_peak = shared_top
        tgt_pot = finish(col_peak, col_total, sources)
    return (src_pot, tgt_pot)


def solution(mesh):
    return jax.shard_map(
        per_device,
        mesh=mesh,
        in_specs=(P(None, ("row", "col")), P(None, "col")),
        out_specs=(P("row"), P("col")),
        check_vma=False,
    )
```

profile of v0, /device:TPU:2, one launch (start us, length us, event | category | flops | bytes accessed | tf_op | source)
XLA Modules:
  0.0 592.4 jit_solution(7874260443332699380)
XLA Ops:
  0.6 38.0 %all_gather.3 = bf16[64,4096]{1,0:T(8,128)(2,1)S(1)} all-gather(bf16[64,128]{1,0:T(8,128)(2,1)} %param.10), channel_id=1, replica_groups=mesh['row'=16,'col'=32] {'col'}, dimensions={1}, use_global_device_ids=true | all-gather | bytes 540672 | tf_op jit(solution)/shard_map/all_gather | solution.py:71
  39.3 11.0 %while.48 = (s32[]{:T(128)}, f32[8,512]{1,0:T(8,128)S(1)}, f32[8,512]{1,0:T(8,128)S(1)}, f32[8,512]{1,0:T(8,128)S(1)}, f32[1024]{0:T(1024)S(1)}, /*index=5*/bf16...) while((s32[]{:T(128)}, f32[8,512]{1,0:T(8,128)S(1)}, ...), condition=%wide.region_5.6_spmd, body=%wide.region_2.5_spmd.sunk | while | flops 71302144 | bytes 4415597 | solution.py:40
  39.3 0.7 fusion.29
  43.4 0.7 fusion.29
  46.1 0.7 fusion.29
  50.2 90.3 %pmax.28 = f32[4096]{0:T(1024)S(1)} all-reduce(f32[4096]{0:T(1024)S(1)} %bitcast.104), channel_id=1, replica_groups=mesh['row'=16,'col'=32] {'col'}, use_global_device_ids=true, to_apply=%region_6.7 | all-reduce | flops 4096 | bytes 32768 | tf_op jit(solution)/shard_map/pmax | solution.py:77
  140.6 90.0 %psum.28 = f32[4096]{0:T(1024)S(1)} all-reduce(f32[4096]{0:T(1024)S(1)} %exponential_multiply_fusion.1), channel_id=1, replica_groups=mesh['row'=16,'col'=32] {'col'}, use_global_device_ids=true, to_apply=%region_7.8 | all-reduce | flops 4096 | bytes 32768 | tf_op jit(solution)/shard_map/psum | solution.py:78
  230.7 9.8 %while.49 = (s32[]{:T(128)}, f32[8,1024]{1,0:T(8,128)S(1)}, f32[8,1024]{1,0:T(8,128)S(1)}, f32[8,512]{1,0:T(8,128)S(1)}, f32[8,512]{1,0:T(8,128)S(1)}, /*index=5...) while((s32[]{:T(128)}, f32[8,1024]{1,0:T(8,128)S(1)}, ...), condition=%wide.region_11.12_spmd, body=%wide.region_8.11_spmd.sunk | while | flops 71301120 | bytes 4436085 | solution.py:54
  240.5 36.7 %pmax.29 = f32[1024]{0:T(1024)S(1)} all-reduce(f32[1024]{0:T(1024)S(1)} %reduce_max.54), channel_id=1, replica_groups=mesh['row'=16,'col'=32] {'row'}, use_global_device_ids=true, to_apply=%region_13.14 | all-reduce | flops 1024 | bytes 8192 | tf_op jit(solution)/shard_map/pmax | solution.py:82
  277.2 40.0 %psum.29 = f32[1024]{0:T(1024)S(1)} all-reduce(f32[1024]{0:T(1024)S(1)} %exponential_multiply_fusion.3), channel_id=1, replica_groups=mesh['row'=16,'col'=32] {'row'}, use_global_device_ids=true, to_apply=%region_15.16 | all-reduce | flops 1024 | bytes 8192 | tf_op jit(solution)/shard_map/psum | solution.py:83
  317.2 11.0 %while.50 = (s32[]{:T(128)}, f32[8,512]{1,0:T(8,128)S(1)}, f32[8,512]{1,0:T(8,128)S(1)}, f32[1024]{0:T(1024)S(1)}, f32[8,512]{1,0:T(8,128)S(1)}, /*index=5*/f32[...) while((s32[]{:T(128)}, f32[8,512]{1,0:T(8,128)S(1)}, ...), condition=%wide.region_19.20_spmd, body=%wide.region_16.19_spmd.sunk | while | flops 71302144 | bytes 4419701 | solution.py:40
  317.3 0.7 fusion.33
  318.6 0.7 fusion.33
  320.0 0.7 fusion.33
  321.4 0.7 fusion.33
  322.8 0.7 fusion.33
  324.1 0.7 fusion.33
  325.5 0.7 fusion.33
  326.9 0.7 fusion.33
  328.2 90.0 %pmax.30 = f32[4096]{0:T(1024)S(1)} all-reduce(f32[4096]{0:T(1024)S(1)} %bitcast.106), channel_id=1, replica_groups=mesh['row'=16,'col'=32] {'col'}, use_global_device_ids=true, to_apply=%region_20.21 | all-reduce | flops 4096 | bytes 32768 | tf_op jit(solution)/shard_map/pmax | solution.py:77
  418.3 90.0 %psum.30 = f32[4096]{0:T(1024)S(1)} all-reduce(f32[4096]{0:T(1024)S(1)} %exponential_multiply_fusion), channel_id=1, replica_groups=mesh['row'=16,'col'=32] {'col'}, use_global_device_ids=true, to_apply=%region_21.22 | all-reduce | flops 4096 | bytes 32768 | tf_op jit(solution)/shard_map/psum | solution.py:78
  508.9 9.8 %while.51 = (s32[]{:T(128)}, f32[8,1024]{1,0:T(8,128)S(1)}, f32[8,1024]{1,0:T(8,128)S(1)}, f32[8,512]{1,0:T(8,128)S(1)}, f32[8,512]{1,0:T(8,128)S(1)}, /*index=5...) while((s32[]{:T(128)}, f32[8,1024]{1,0:T(8,128)S(1)}, ...), condition=%wide.region_25.26_spmd, body=%wide.region_22.25_spmd.sunk | while | flops 71301120 | bytes 4436085 | solution.py:54
  518.8 35.5 %pmax.31 = f32[1024]{0:T(1024)S(1)} all-reduce(f32[1024]{0:T(1024)S(1)} %reduce_max.55), channel_id=1, replica_groups=mesh['row'=16,'col'=32] {'row'}, use_global_device_ids=true, to_apply=%region_27.28 | all-reduce | flops 1024 | bytes 8192 | tf_op jit(solution)/shard_map/pmax | solution.py:82
  554.3 37.4 %psum.31 = f32[1024]{0:T(1024)S(1)} all-reduce(f32[1024]{0:T(1024)S(1)} %exponential_multiply_fusion.2), channel_id=1, replica_groups=mesh['row'=16,'col'=32] {'row'}, use_global_device_ids=true, to_apply=%region_29.30 | all-reduce | flops 1024 | bytes 8192 | tf_op jit(solution)/shard_map/psum | solution.py:83
  (184 shorter events, 34.5 us)
Async XLA Ops:
  0.6 38.6 %copy-start = (bf16[64,1024]{1,0:T(8,128)(2,1)S(1)}, bf16[64,1024]{1,0:T(8,128)(2,1)}, u32[]{:S(2)}) copy-start(bf16[64,1024]{1,0:T(8,128)(2,1)} %param.11) | copy-start | bytes 393220
  508.3 0.6 copy-start.1
where the time goes:
time: 593 us; the launch traced here: 592 us
  blocking collectives  548 us (92%)
  matrix products  21 us (4%)
  other arithmetic  14.6 us (2%)
  local copies, waits for them, and re-layouts  6.5 us (1%)
    pmax x2, blocking collectives, per_device(): shared_peak = lax.pmax(row_peak, 'col')  180 us
    psum x2, blocking collectives, per_device(): row_total = lax.psum(row_total * jnp.exp(row_peak - shared_peak), 'col')  180 us
    psum x2, blocking collectives, per_device(): col_total = lax.psum(col_total * jnp.exp(col_peak - shared_top), 'row')  77.4 us
    pmax x2, blocking collectives, per_device(): shared_top = lax.pmax(col_peak, 'row')  72.2 us
    all_gather x1, blocking collectives, per_device(): src_block = lax.all_gather(src_feat, 'col', axis=1, tiled=True)  38 us
    dot_general x32, matrix products, pair_costs(): lax.dot_general(xs, ys, (((0,), (0,)), ((), ())), preferred_element_type=...  21 us

commit v1 on v0

v1 whole, which is shorter than its diff:
```python
import math

import jax
import jax.numpy as jnp
from jax import lax
from jax.sharding import Mesh, PartitionSpec as P

ITERS = 2
INV_EPS = 20.0
EPS = 0.05
BLOCK = 512


def squares(feats):
    return jnp.sum(jnp.square(feats.astype(jnp.float32)), axis=-2)


def share(value, axis, size):
    spread = jnp.broadcast_to(value[None], (size,) + value.shape)
    return lax.all_to_all(spread, axis, 0, 0, tiled=False)


def merge(parts):
    peak = jnp.max(parts, axis=0)
    return peak + jnp.log(jnp.sum(jnp.exp(parts - peak[None]), axis=0))


def partial_lse(over, over_sq, over_pot, kept, kept_sq):
    def one(args):
        feats, sq, pot = args
        inner = lax.dot_general(feats, kept, (((0,), (0,)), ((), ())), preferred_element_type=jnp.float32)
        scores = (pot[:, None] - ((sq[:, None] + kept_sq[None, :]) - 2.0 * inner)) * INV_EPS
        peak = jnp.max(scores, axis=0)
        return peak, jnp.sum(jnp.exp(scores - peak[None, :]), axis=0)

    peaks, totals = lax.map(one, (over, over_sq, over_pot))
    peak = jnp.max(peaks, axis=0)
    return peak + jnp.log(jnp.sum(totals * jnp.exp(peaks - peak[None]), axis=0))


def per_device(n_row, n_z, n_core, src_feat, tgt_feat):
    sources = src_feat.shape[1] * n_row * n_z * n_core
    targets = tgt_feat.shape[1] * n_z * n_core
    width, tgt_own = tgt_feat.shape
    tgt = lax.all_gather(tgt_feat, "core")
    src = share(src_feat, "z", n_z)
    tgt_sq, src_sq = squares(tgt), squares(src)
    n_src, n_tgt = src.shape[0] * src.shape[2], n_core * tgt_own
    src_flat = src.transpose(1, 0, 2).reshape(width, n_src)
    tgt_flat = tgt.transpose(1, 0, 2).reshape(width, n_tgt)
    sq_s, sq_t = src_sq.reshape(n_src), tgt_sq.reshape(n_tgt)
    tgt_pot = jnp.zeros((n_tgt,), jnp.float32)

    def blocks(flat):
        return flat.reshape(width, -1, BLOCK).transpose(1, 0, 2)

    for step in range(ITERS):
        part = partial_lse(blocks(tgt_flat), sq_t.reshape(-1, BLOCK), tgt_pot.reshape(-1, BLOCK), src_flat, sq_s)
        src_pot = -EPS * (merge(share(part, "z", n_z)) - math.log(targets))
        part = partial_lse(blocks(src_flat), sq_s.reshape(-1, BLOCK), src_pot.reshape(-1, BLOCK), tgt_flat, sq_t)
        if step < ITERS - 1:
            tgt_pot = -EPS * (merge(share(part, ("row", "core"), n_row * n_core)) - math.log(sources))
        else:
            send = jnp.broadcast_to(part.reshape(1, n_core, tgt_own), (n_row, n_core, tgt_own))
            got = lax.all_to_all(send.reshape(n_row * n_core, tgt_own), ("row", "core"), 0, 0, tiled=True)
            tgt_out = -EPS * (merge(got) - math.log(sources))
    both = lax.all_gather(src_pot.reshape(n_z, -1), "core", axis=1)
    return both.reshape(n_core * n_src), tgt_out


def solution(mesh):
    n_row, n_col = mesh.shape["row"], mesh.shape["col"]
    n_core = 2
    n_z = n_col // n_core
    fine = Mesh(mesh.devices.reshape(n_row, n_z, n_core), ("row", "z", "core"))

    def body(src_feat, tgt_feat):
        return per_device(n_row, n_z, n_core, src_feat, tgt_feat)

    return jax.shard_map(
        body,
        mesh=fine,
        in_specs=(P(None, ("row", "z", "core")), P(None, ("z", "core"))),
        out_specs=(P("row"), P(("z", "core"))),
        check_vma=False,
    )
```

time: 593 us -> 142 us (0.24)
  the two profiles are of different devices: /device:TPU:2 before, /device:TPU:1 now
where the time goes in v1:
time: 142 us
  starting transfers between devices  47.6 us (34%)
  waiting for transfers between devices  47.6 us (34%)
  matrix products  17.7 us (12%)
  other arithmetic  12 us (8%)
  local copies, waits for them, and re-layouts  10.4 us (7%)
  blocking collectives  4.61 us (3%)
    all_to_all x4, waiting for transfers between devices, share(): return lax.all_to_all(spread, axis, 0, 0, tiled=False)  42.4 us
    all_to_all x4, starting transfers between devices, share(): return lax.all_to_all(spread, axis, 0, 0, tiled=False)  41 us
    dot_general x16, matrix products, one(): lax.dot_general(feats, kept, (((0,), (0,)), ((), ())), preferred_element_...  17.7 us
    reduce_sum x16, other arithmetic, one(): return (peak, jnp.sum(jnp.exp(scores - peak[None, :]), axis=0))  10.3 us
    all_to_all x1, starting transfers between devices, per_device(): lax.all_to_all(send.reshape(n_row * n_core, tgt_own), ('row', 'core'), 0,...  6.53 us
    all_to_all x1, waiting for transfers between devices, per_device(): lax.all_to_all(send.reshape(n_row * n_core, tgt_own), ('row', 'core'), 0,...  5.2 us
    dynamic_update_slice x32, local copies, waits for them, and re-layouts, partial_lse(): peaks, totals = lax.map(one, (over, over_sq, over_pot))  4.08 us
    broadcast_in_dim x4, local copies, waits for them, and re-layouts, share(): spread = jnp.broadcast_to(value[None], (size,) + value.shape)  3.7 us
  transfers between devices with their start and end apart: 5, of which 5 were waited for; matrix products, arithmetic and copies ran while one was open for 1% of the time, Pallas kernels for 0%

profile of v1, /device:TPU:1, one launch (start us, length us, event | category | flops | bytes accessed | tf_op | source)
XLA Modules:
  0.0 141.7 jit_solution(13519195854246548326)
XLA Ops:
  0.6 1.5 %broadcast_in_dim.44 = bf16[16,64,128]{2,1,0:T(8,128)(2,1)} broadcast(bf16[64,128]{1,0:T(8,128)(2,1)} %param.10), dimensions={1,2} | broadcast | bytes 278528 | tf_op jit(solution)/shard_map/broadcast_in_dim | solution.py:19
  2.1 15.7 %all-to-all-start = ((bf16[16,64,128]{2,1,0:T(8,128)(2,1)}), bf16[16,64,128]{2,1,0:T(8,128)(2,1)S(1)}, u32[]{:S(2)}, u32[]{:S(2)}) async-start(bf16[16,64,128]{2,1,0:T(8,128)(2,1)} %broadcast_in_dim.44), calls=%async_computation | async-start | bytes 524288 | tf_op jit(solution)/shard_map/all_to_all | solution.py:20
  17.8 2.8 %all-gather = bf16[128,1024]{1,0:T(8,128)(2,1)S(1)} all-gather(bf16[64,1024]{1,0:T(8,128)(2,1)} %param.11), channel_id=2, replica_groups=mesh['row'=16,'z'=16,'core'=2] {'core'}, dimensions={0}, use_global_device_ids=true | all-gather | bytes 393216 | tf_op jit(solution)/shard_map/all_gather | solution.py:45
  21.1 9.8 %all-to-all-done = bf16[16,64,128]{2,1,0:T(8,128)(2,1)S(1)} async-done(((bf16[16,64,128]{2,1,0:T(8,128)(2,1)}), bf16[16,64,128]{2,1,0:T(8,128)(2,1)S(1)}, u32[]{:S(2)}, u32[]{:S(2)}) %all-to-all-start) | async-done | bytes 262176 | tf_op jit(solution)/shard_map/all_to_all | solution.py:20
  31.1 8.1 %while.48 = (s32[]{:T(128)}, f32[4,2048]{1,0:T(4,128)S(1)}, f32[4,2048]{1,0:T(4,128)S(1)}, f32[4,512]{1,0:T(4,128)S(1)}, f32[16,128]{1,0:T(8,128)S(1)}, /*index=...) while((s32[]{:T(128)}, f32[4,2048]{1,0:T(4,128)S(1)}, ...), condition=%wide.region_5.6_spmd, body=%wide.region_2.5_spmd.sunk | while | flops 142602240 | bytes 8788077 | solution.py:36
  40.0 10.9 %all-to-all-start.1 = ((f32[16,1,2048]{2,1,0:T(1,128)}), f32[16,1,2048]{2,1,0:T(1,128)S(1)}, u32[]{:S(2)}, u32[]{:S(2)}) async-start(f32[16,1,2048]{2,1,0:T(1,128)} %broadcast_in_dim.48), calls=%async_computation.1 | async-start | bytes 262144 | tf_op jit(solution)/shard_map/all_to_all | solution.py:20
  51.4 11.6 %all-to-all-done.1 = f32[16,1,2048]{2,1,0:T(1,128)S(1)} async-done(((f32[16,1,2048]{2,1,0:T(1,128)}), f32[16,1,2048]{2,1,0:T(1,128)S(1)}, u32[]{:S(2)}, u32[]{:S(2)}) %all-to-all-start.1) | async-done | bytes 131104 | tf_op jit(solution)/shard_map/all_to_all | solution.py:20
  63.2 8.3 %while.49 = (s32[]{:T(128)}, f32[4,2048]{1,0:T(4,128)S(1)}, f32[4,2048]{1,0:T(4,128)S(1)}, f32[4,512]{1,0:T(4,128)S(1)}, f32[4,512]{1,0:T(4,128)S(1)}, /*index=5...) while((s32[]{:T(128)}, f32[4,2048]{1,0:T(4,128)S(1)}, ...), condition=%wide.region_13.14_spmd, body=%wide.region_10.13_spmd.sunk | while | flops 142602240 | bytes 8810613 | solution.py:36
  65.3 1.1 fusion.41
  67.4 1.1 fusion.41
  69.5 1.1 fusion.41
  72.5 10.8 %all-to-all-start.2 = ((f32[32,1,2048]{2,1,0:T(1,128)}), f32[32,1,2048]{2,1,0:T(1,128)S(1)}, u32[]{:S(2)}, u32[]{:S(2)}) async-start(f32[32,1,2048]{2,1,0:T(1,128)} %broadcast_in_dim.49), calls=%async_computation.2 | async-start | bytes 524288 | tf_op jit(solution)/shard_map/all_to_all | solution.py:20
  83.3 8.9 %all-to-all-done.2 = f32[32,1,2048]{2,1,0:T(1,128)S(1)} async-done(((f32[32,1,2048]{2,1,0:T(1,128)}), f32[32,1,2048]{2,1,0:T(1,128)S(1)}, u32[]{:S(2)}, u32[]{:S(2)}) %all-to-all-start.2) | async-done | bytes 262176 | tf_op jit(solution)/shard_map/all_to_all | solution.py:20
  92.5 8.3 %while.50 = (s32[]{:T(128)}, f32[4,2048]{1,0:T(4,128)S(1)}, f32[4,2048]{1,0:T(4,128)S(1)}, f32[4,512]{1,0:T(4,128)S(1)}, f32[4,512]{1,0:T(4,128)S(1)}, /*index=5...) while((s32[]{:T(128)}, f32[4,2048]{1,0:T(4,128)S(1)}, ...), condition=%wide.region_21.22_spmd, body=%wide.region_18.21_spmd.sunk | while | flops 142602240 | bytes 8794229 | solution.py:36
  96.7 1.1 fusion.43
  98.8 1.1 fusion.43
  101.6 3.5 %all-to-all-start.3 = ((f32[16,1,2048]{2,1,0:T(1,128)}), f32[16,1,2048]{2,1,0:T(1,128)S(1)}, u32[]{:S(2)}, u32[]{:S(2)}) async-start(f32[16,1,2048]{2,1,0:T(1,128)} %broadcast_in_dim.50), calls=%async_computation.3 | async-start | bytes 262144 | tf_op jit(solution)/shard_map/all_to_all | solution.py:20
  105.2 12.1 %all-to-all-done.3 = f32[16,1,2048]{2,1,0:T(1,128)S(1)} async-done(((f32[16,1,2048]{2,1,0:T(1,128)}), f32[16,1,2048]{2,1,0:T(1,128)S(1)}, u32[]{:S(2)}, u32[]{:S(2)}) %all-to-all-start.3) | async-done | bytes 131104 | tf_op jit(solution)/shard_map/all_to_all | solution.py:20
  117.4 8.3 %while.51 = (s32[]{:T(128)}, f32[4,2048]{1,0:T(4,128)S(1)}, f32[4,2048]{1,0:T(4,128)S(1)}, f32[4,512]{1,0:T(4,128)S(1)}, f32[4,512]{1,0:T(4,128)S(1)}, /*index=5...) while((s32[]{:T(128)}, f32[4,2048]{1,0:T(4,128)S(1)}, ...), condition=%wide.region_29.30_spmd, body=%wide.region_26.29_spmd.sunk | while | flops 142602240 | bytes 8810613 | solution.py:36
  117.5 1.1 fusion.45
  121.6 1.1 fusion.45
  126.7 6.5 %all-to-all-start.4 = ((f32[32,1,1024]{2,1,0:T(1,128)}), f32[32,1,1024]{2,1,0:T(1,128)S(1)}, u32[]{:S(2)}, u32[]{:S(2)}) async-start(f32[32,1,1024]{2,1,0:T(1,128)} %all_to_all.36), calls=%async_computation.4 | async-start | bytes 262144 | tf_op jit(solution)/shard_map/all_to_all | solution.py:65
  133.3 1.8 %all_gather.11 = f32[16,2,128]{2,0,1:T(8,128)S(1)} all-gather(f32[16,1,128]{2,0,1:T(8,128)S(1)} %bitcast.166), channel_id=1, replica_groups=mesh['row'=16,'z'=16,'core'=2] {'core'}, dimensions={1}, use_global_device_ids=true | all-gather | bytes 24576 | tf_op jit(solution)/shard_map/all_gather | solution.py:67
  135.7 5.2 %all-to-all-done.4 = f32[32,1,1024]{2,1,0:T(1,128)S(1)} async-done(((f32[32,1,1024]{2,1,0:T(1,128)}), f32[32,1,1024]{2,1,0:T(1,128)S(1)}, u32[]{:S(2)}, u32[]{:S(2)}) %all-to-all-start.4) | async-done | bytes 131104 | tf_op jit(solution)/shard_map/all_to_all | solution.py:65
  (135 shorter events, 30.8 us)
Async XLA Ops:
  2.1 28.9 %all-to-all-start = ((bf16[16,64,128]{2,1,0:T(8,128)(2,1)}), bf16[16,64,128]{2,1,0:T(8,128)(2,1)S(1)}, u32[]{:S(2)}, u32[]{:S(2)}) async-start(bf16[16,64,128]{2,1,0:T(8,128)(2,1)} %broadcast_in_dim.44), calls=%async_computation | async-start | bytes 524288 | tf_op jit(solution)/shard_map/all_to_all | solution.py:20
  40.0 22.9 %all-to-all-start.1 = ((f32[16,1,2048]{2,1,0:T(1,128)}), f32[16,1,2048]{2,1,0:T(1,128)S(1)}, u32[]{:S(2)}, u32[]{:S(2)}) async-start(f32[16,1,2048]{2,1,0:T(1,128)} %broadcast_in_dim.48), calls=%async_computation.1 | async-start | bytes 262144 | tf_op jit(solution)/shard_map/all_to_all | solution.py:20
  72.5 19.8 %all-to-all-start.2 = ((f32[32,1,2048]{2,1,0:T(1,128)}), f32[32,1,2048]{2,1,0:T(1,128)S(1)}, u32[]{:S(2)}, u32[]{:S(2)}) async-start(f32[32,1,2048]{2,1,0:T(1,128)} %broadcast_in_dim.49), calls=%async_computation.2 | async-start | bytes 524288 | tf_op jit(solution)/shard_map/all_to_all | solution.py:20
  101.6 15.6 %all-to-all-start.3 = ((f32[16,1,2048]{2,1,0:T(1,128)}), f32[16,1,2048]{2,1,0:T(1,128)S(1)}, u32[]{:S(2)}, u32[]{:S(2)}) async-start(f32[16,1,2048]{2,1,0:T(1,128)} %broadcast_in_dim.50), calls=%async_computation.3 | async-start | bytes 262144 | tf_op jit(solution)/shard_map/all_to_all | solution.py:20
  126.7 14.2 %all-to-all-start.4 = ((f32[32,1,1024]{2,1,0:T(1,128)}), f32[32,1,1024]{2,1,0:T(1,128)S(1)}, u32[]{:S(2)}, u32[]{:S(2)}) async-start(f32[32,1,1024]{2,1,0:T(1,128)} %all_to_all.36), calls=%async_computation.4 | async-start | bytes 262144 | tf_op jit(solution)/shard_map/all_to_all | solution.py:65

commit v2 on v1

v2 whole, which is shorter than its diff:
```python
import functools
import math

import jax
import jax.numpy as jnp
from jax import lax
from jax.experimental import pallas as pl
from jax.experimental.pallas import tpu as pltpu
from jax.sharding import Mesh, PartitionSpec as P

ITERS = 2
INV_EPS = 20.0
EPS = 0.05
LANES = 128
INNER_GAIN = 2.0 * INV_EPS * math.log2(math.e)
SQ_GAIN = -INV_EPS * math.log2(math.e)
FROM_LOG2 = EPS * math.log(2.0)
LOW, HIGH = -91.0, 100.0
F32, BF16 = jnp.float32, jnp.bfloat16


def split3(v):
    hi = v.astype(BF16)
    rest = v - hi.astype(F32)
    mid = rest.astype(BF16)
    return hi, mid, (rest - mid.astype(F32)).astype(BF16)


def bias_rows(v, own, width):
    row = lax.broadcasted_iota(jnp.int32, (width, LANES), 0)
    other = 3 - own
    out = jnp.where((row >= other) & (row < other + 3), 1.0, 0.0)
    for k, term in enumerate(split3(v)):
        out = jnp.where(row == own + k, term.astype(F32), out)
    return out


def prep_targets(y_ref, yt_ref):
    cores, width, own = y_ref.shape
    for c in range(cores):
        for k in range(0, own, LANES):
            y = y_ref[c, :, k : k + LANES].astype(F32)
            sq = jnp.sum(y * y, axis=0, keepdims=True)
            rows = pl.ds(c * own + k, LANES)
            yt_ref[rows, : 2 * width] = jnp.concatenate([y, y], axis=0).T.astype(BF16)
            tail = bias_rows(SQ_GAIN * sq, 0, width)
            yt_ref[rows, 2 * width :] = jnp.concatenate([y, tail], axis=0).T.astype(BF16)


def scores(yt_ref, xa_ref, rows, cols):
    return jnp.dot(yt_ref[rows, :], xa_ref[:, cols], preferred_element_type=F32)


def merge(parts):
    peak = jnp.max(parts, axis=0)
    return peak + jnp.log2(jnp.sum(jnp.exp2(parts - peak[None]), axis=0))


def spread_to_rows(v, out_ref):
    for k in range(v.shape[0]):
        out_ref[k * LANES : (k + 1) * LANES, :] = jnp.broadcast_to(v[k : k + 1], (LANES, LANES)).T


def slow_over_targets(yt_ref, xa_ref, pot_ref, out_ref):
    n_tgt = yt_ref.shape[0]
    step = 256

    def one(it, _):
        cols = pl.ds(pl.multiple_of(it * LANES, LANES), LANES)

        def tile(jt):
            rows = pl.ds(pl.multiple_of(jt * step, step), step)
            s = scores(yt_ref, xa_ref, rows, cols)
            return s if pot_ref is None else s + pot_ref[rows, :]

        def peak_step(jt, peak):
            return jnp.maximum(peak, jnp.max(tile(jt), axis=0, keepdims=True))

        peak = lax.fori_loop(0, n_tgt // step, peak_step, jnp.full((1, LANES), -jnp.inf, F32))

        def sum_step(jt, total):
            return total + jnp.sum(jnp.exp2(tile(jt) - peak), axis=0, keepdims=True)

        total = lax.fori_loop(0, n_tgt // step, sum_step, jnp.zeros((1, LANES), F32))
        out_ref[pl.ds(it, 1), :] = peak + jnp.log2(total)
        return 0

    lax.fori_loop(0, out_ref.shape[0], one, 0)


def slow_over_sources(yt_ref, xa_ref, pot_ref, out_ref):
    n_blocks = xa_ref.shape[1] // LANES

    def one(jt, _):
        rows = pl.ds(pl.multiple_of(jt * LANES, LANES), LANES)

        def tile(it):
            cols = pl.ds(pl.multiple_of(it * LANES, LANES), LANES)
            return scores(yt_ref, xa_ref, rows, cols) + pot_ref[pl.ds(it, 1), :]

        def peak_step(it, peak):
            return jnp.maximum(peak, tile(it))

        peak = lax.fori_loop(0, n_blocks, peak_step, jnp.full((LANES, LANES), -jnp.inf, F32))
        peak = jnp.max(peak, axis=1, keepdims=True)

        def sum_step(it, total):
            return total + jnp.exp2(tile(it) - peak)

        total = lax.fori_loop(0, n_blocks, sum_step, jnp.zeros((LANES, LANES), F32))
        value = peak + jnp.log2(jnp.sum(total, axis=1, keepdims=True))
        out_ref[pl.ds(jt, 1), :] = jnp.broadcast_to(value, (LANES, LANES)).T[:1]
        return 0

    lax.fori_loop(0, out_ref.shape[0], one, 0)


def send(value, part_ref):
    copies = part_ref.shape[0]
    part_ref[...] = jnp.broadcast_to(value[None], (copies,) + value.shape)


def first_over_targets(tile, yt_ref, x_ref, e_ref, xa_ref, part_ref, sum_ref):
    n_blocks, width, _ = x_ref.shape
    n_tgt = yt_ref.shape[0]
    for b in range(n_blocks):
        x = x_ref[b].astype(F32)
        sq = jnp.sum(x * x, axis=0, keepdims=True)
        tail = bias_rows(SQ_GAIN * sq, 3, width).astype(BF16)
        xa_ref[:, b * LANES : (b + 1) * LANES] = jnp.concatenate([*split3(INNER_GAIN * x), tail], axis=0)
    wide = 2 * LANES

    def one(it, _):
        cols = pl.ds(pl.multiple_of(it * wide, wide), wide)
        acc = jnp.zeros((8, wide), F32)
        for jt in range(0, n_tgt, tile):
            rows = pl.ds(jt, tile)
            e = jnp.exp2(scores(yt_ref, xa_ref, rows, cols))
            e_ref[rows, cols] = e
            acc = acc + jnp.sum(e.reshape(tile // 8, 8, wide), axis=0)
        total = jnp.sum(acc, axis=0, keepdims=True)
        sum_ref[pl.ds(2 * it, 1), :] = total[:, :LANES]
        sum_ref[pl.ds(2 * it + 1, 1), :] = total[:, LANES:]
        return 0

    lax.fori_loop(0, n_blocks // 2, one, 0)
    totals = sum_ref[...]
    fast = (jnp.min(totals) >= 2.0**LOW) & (jnp.max(totals) <= 2.0**HIGH)

    @pl.when(fast)
    def _():
        send(jnp.log2(totals), part_ref)

    @pl.when(jnp.logical_not(fast))
    def _():
        slow_over_targets(yt_ref, xa_ref, None, sum_ref)
        send(sum_ref[...], part_ref)


def checked(totals, pot):
    top = jnp.max(pot)
    floor = jnp.exp2(jnp.minimum(jnp.maximum(top, 0.0), HIGH) + LOW)
    return (top <= HIGH) & (jnp.min(totals) >= floor)


def over_sources(log_targets, rows_at_once, parts_ref, e_ref, yt_ref, xa_ref, part_ref, pot_ref, sum_ref, acc_ref, yt_buf, xa_buf):
    n_tgt, n_src = e_ref.shape
    n_blocks = n_src // LANES
    pot = log_targets - merge(parts_ref[...])
    pot_ref[...] = pot
    u = jnp.exp2(jnp.minimum(pot, HIGH))

    def one(jt, _):
        rows = pl.ds(pl.multiple_of(jt * rows_at_once, rows_at_once), rows_at_once)
        acc = e_ref[rows, :LANES] * u[:1]
        for b in range(1, n_blocks):
            acc = acc + e_ref[rows, b * LANES : (b + 1) * LANES] * u[b : b + 1]
        acc_ref[rows, :] = acc
        return 0

    lax.fori_loop(0, n_tgt // rows_at_once, one, 0)
    for k in range(n_tgt // LANES):
        block = acc_ref[k * LANES : (k + 1) * LANES, :].T
        sum_ref[k : k + 1, :] = jnp.sum(block, axis=0, keepdims=True)
    totals = sum_ref[...]
    fast = checked(totals, pot)

    def put(value):
        copies, n, _ = part_ref.shape
        for k in range(copies):
            at = (k * n) % value.shape[0]
            part_ref[k] = value[at : at + n]

    @pl.when(fast)
    def _():
        put(jnp.log2(totals))

    @pl.when(jnp.logical_not(fast))
    def _():
        pltpu.sync_copy(yt_ref, yt_buf)
        pltpu.sync_copy(xa_ref, xa_buf)
        slow_over_sources(yt_buf, xa_buf, pot_ref, sum_ref)
        put(sum_ref[...])


def over_targets(log_sources, rows_at_once, parts_ref, e_ref, yt_ref, xa_ref, part_ref, sum_ref, pot_ref, yt_buf, xa_buf):
    n_tgt, n_src = e_ref.shape
    n_blocks = n_src // LANES
    pot = log_sources - merge(parts_ref[...])
    spread_to_rows(jnp.exp2(jnp.minimum(pot, HIGH)), pot_ref)

    def one(jt, acc):
        acc = list(acc)
        for r in range(rows_at_once // 8):
            rows = pl.ds(pl.multiple_of(jt * rows_at_once + 8 * r, 8), 8)
            v = pot_ref[rows, :]
            for b in range(n_blocks):
                acc[b] = acc[b] + e_ref[rows, b * LANES : (b + 1) * LANES] * v
        return tuple(acc)

    acc = lax.fori_loop(0, n_tgt // rows_at_once, one, (jnp.zeros((8, LANES), F32),) * n_blocks)
    for b in range(n_blocks):
        sum_ref[b : b + 1, :] = jnp.sum(acc[b], axis=0, keepdims=True)
    totals = sum_ref[...]
    fast = checked(totals, pot)

    @pl.when(fast)
    def _():
        send(jnp.log2(totals), part_ref)

    @pl.when(jnp.logical_not(fast))
    def _():
        pltpu.sync_copy(yt_ref, yt_buf)
        pltpu.sync_copy(xa_ref, xa_buf)
        spread_to_rows(pot, pot_ref)
        slow_over_targets(yt_buf, xa_buf, pot_ref, sum_ref)
        send(sum_ref[...], part_ref)


VMEM = pl.BlockSpec(memory_space=pltpu.VMEM)
ANY = pl.BlockSpec(memory_space=pl.ANY)
LIMIT = 20 << 20


def params():
    return pltpu.CompilerParams(vmem_limit_bytes=LIMIT)


def call_prep(y):
    cores, width, own = y.shape
    return pl.pallas_call(
        prep_targets,
        out_shape=jax.ShapeDtypeStruct((cores * own, 4 * width), BF16),
        in_specs=[VMEM],
        out_specs=VMEM,
        compiler_params=params(),
        name="prep_targets",
    )(y)


def call_first(yt, x, copies, tile=512):
    n_blocks, width, lanes = x.shape
    n_tgt, n_src = yt.shape[0], n_blocks * lanes
    return pl.pallas_call(
        functools.partial(first_over_targets, tile),
        out_shape=(
            pltpu.VMEM((n_tgt, n_src), F32),
            jax.ShapeDtypeStruct((4 * width, n_src), BF16),
            jax.ShapeDtypeStruct((copies, n_blocks, lanes), F32),
        ),
        in_specs=[VMEM, VMEM],
        out_specs=(VMEM, VMEM, VMEM),
        scratch_shapes=[pltpu.VMEM((n_blocks, lanes), F32)],
        compiler_params=params(),
        name="first_over_targets",
    )(yt, x)


def call_over_sources(log_targets, parts, e, yt, xa, part_shape, rows_at_once=32):
    n_tgt, n_src = e.shape
    return pl.pallas_call(
        functools.partial(over_sources, log_targets, rows_at_once),
        out_shape=(
            jax.ShapeDtypeStruct(part_shape, F32),
            jax.ShapeDtypeStruct((n_src // LANES, LANES), F32),
        ),
        in_specs=[VMEM, VMEM, ANY, ANY],
        out_specs=(VMEM, VMEM),
        scratch_shapes=[
            pltpu.VMEM((n_tgt // LANES, LANES), F32),
            pltpu.VMEM((n_tgt, LANES), F32),
            pltpu.VMEM(yt.shape, BF16),
            pltpu.VMEM(xa.shape, BF16),
        ],
        compiler_params=params(),
        name="over_sources",
    )(parts, e, yt, xa)


def call_over_targets(log_sources, parts, e, yt, xa, copies, rows_at_once=32):
    n_tgt, n_src = e.shape
    return pl.pallas_call(
        functools.partial(over_targets, log_sources, rows_at_once),
        out_shape=jax.ShapeDtypeStruct((copies, n_src // LANES, LANES), F32),
        in_specs=[VMEM, VMEM, ANY, ANY],
        out_specs=VMEM,
        scratch_shapes=[
            pltpu.VMEM((n_src // LANES, LANES), F32),
            pltpu.VMEM((n_tgt, LANES), F32),
            pltpu.VMEM(yt.shape, BF16),
            pltpu.VMEM(xa.shape, BF16),
        ],
        compiler_params=params(),
        name="over_targets",
    )(parts, e, yt, xa)


def exchange(value, axis):
    return lax.all_to_all(value, axis, 0, 0, tiled=False)


def per_device(n_row, n_z, n_core, src_feat, tgt_feat):
    width, src_own = src_feat.shape
    tgt_own = tgt_feat.shape[1]
    log_sources = math.log2(src_own * n_row * n_z * n_core)
    log_targets = math.log2(tgt_own * n_z * n_core)
    n_tgt = n_core * tgt_own
    group = n_row * n_core
    x = exchange(jnp.broadcast_to(src_feat[None], (n_z, width, src_own)), "z")
    yt = call_prep(lax.all_gather(tgt_feat, "core"))
    e, xa, part = call_first(yt, x, n_z)
    for step in range(ITERS):
        parts = exchange(part, "z")
        if step < ITERS - 1:
            part, _ = call_over_sources(log_targets, parts, e, yt, xa, (group, n_tgt // LANES, LANES))
            parts = exchange(part, ("row", "core"))
            part = call_over_targets(log_sources, parts, e, yt, xa, n_z)
        else:
            part, src = call_over_sources(log_targets, parts, e, yt, xa, (group, tgt_own // LANES, LANES))
            parts = exchange(part, ("row", "core"))
    tgt_pot = FROM_LOG2 * (log_sources - merge(parts)).reshape(tgt_own)
    src = lax.all_gather(src, "core", axis=1)
    return FROM_LOG2 * src.reshape(n_core * n_z * src_own), tgt_pot


def solution(mesh):
    n_row, n_col = mesh.shape["row"], mesh.shape["col"]
    n_core = 2
    n_z = n_col // n_core
    fine = Mesh(mesh.devices.reshape(n_row, n_z, n_core), ("row", "z", "core"))
    return jax.shard_map(
        functools.partial(per_device, n_row, n_z, n_core),
        mesh=fine,
        in_specs=(P(None, ("row", "z", "core")), P(None, ("z", "core"))),
        out_specs=(P("row"), P(("z", "core"))),
        check_vma=False,
    )
```

time: 142 us -> 396 us (2.79)
  Pallas kernels: 0 us -> 291 us
  blocking collectives: 4.61 us -> 64.9 us
  waiting for transfers between devices: 47.6 us -> 17 us
  starting transfers between devices: 47.6 us -> 19.7 us
  matrix products: 17.7 us -> 0 us
  other arithmetic: 12 us -> 0.7 us
  local copies, waits for them, and re-layouts: 10.4 us -> 2.07 us
    pallas_call x0 -> x5, Pallas kernels: none -> 291 us  [the longest x2 180 us: call_over_sources(): pl.pallas_call(functools.partial(over_sources, log_targets, rows_at_once)...]
    all_to_all x0 -> x3, blocking collectives: none -> 57.7 us  [exchange(): return lax.all_to_all(value, axis, 0, 0, tiled=False)]
    all_to_all x5 -> x2, waiting for transfers between devices: 47.6 us -> 17 us  [exchange(): return lax.all_to_all(value, axis, 0, 0, tiled=False)]
    all_to_all x5 -> x2, starting transfers between devices: 47.6 us -> 19.7 us  [exchange(): return lax.all_to_all(value, axis, 0, 0, tiled=False)]
    dot_general x16 -> x0, matrix products: 17.7 us -> none  [one(): lax.dot_general(feats, kept, (((0,), (0,)), ((), ())), preferred_element_...]
    reduce_sum x26 -> x1, other arithmetic: 10.9 us -> 0.05 us  [merge(): return peak + jnp.log2(jnp.sum(jnp.exp2(parts - peak[None]), axis=0))]
    dynamic_update_slice x32 -> x0, local copies, waits for them, and re-layouts: 4.08 us -> none  [partial_lse(): peaks, totals = lax.map(one, (over, over_sq, over_pot))]
  transfers between devices with their start and end apart: 5 -> 2, of which waited for: 5 -> 2; matrix products, arithmetic and copies ran while one was open for 1% -> 0% of each run, Pallas kernels for 0% -> 0%
where the time goes in v2:
time: 396 us
  Pallas kernels  291 us (73%)
  blocking collectives  64.9 us (16%)
  starting transfers between devices  19.7 us (5%)
  waiting for transfers between devices  17 us (4%)
    pallas_call x2, Pallas kernels, call_over_sources(): pl.pallas_call(functools.partial(over_sources, log_targets, rows_at_once)...  180 us
    all_to_all x3, blocking collectives, exchange(): return lax.all_to_all(value, axis, 0, 0, tiled=False)  57.7 us
    pallas_call x1, Pallas kernels, call_first(): pl.pallas_call(functools.partial(first_over_targets, tile), out_shape=(pl...  55.7 us
    pallas_call x1, Pallas kernels, call_over_targets(): pl.pallas_call(functools.partial(over_targets, log_sources, rows_at_once)...  54.3 us
    all_to_all x2, starting transfers between devices, exchange(): return lax.all_to_all(value, axis, 0, 0, tiled=False)  19.7 us
    all_to_all x2, waiting for transfers between devices, exchange(): return lax.all_to_all(value, axis, 0, 0, tiled=False)  17 us
  transfers between devices with their start and end apart: 2, of which 2 were waited for; matrix products, arithmetic and copies ran while one was open for 0% of the time, Pallas kernels for 0%

profile of v2, /device:TPU:1, one launch (start us, length us, event | category | flops | bytes accessed | tf_op | source)
XLA Modules:
  0.0 395.6 jit_solution(11519071384073753963)
XLA Ops:
  0.6 1.5 broadcast_in_dim.2
  2.1 15.7 %all-to-all-start = ((bf16[16,64,128]{2,1,0:T(8,128)(2,1)}), bf16[16,64,128]{2,1,0:T(8,128)(2,1)S(1)}, u32[]{:S(2)}, u32[]{:S(2)}) async-start(bf16[16,64,128]{2,1,0:T(8,128)(2,1)} %broadcast_in_dim.2), calls=%async_computation | async-start | bytes 524288 | tf_op jit(solution)/shard_map/all_to_all | solution.py:319
  17.8 2.8 all-gather
  20.6 0.4 prep_targets.1.yt_ref
  21.0 10.0 %all-to-all-done.x_ref = bf16[16,64,128]{2,1,0:T(8,128)(2,1)S(1)} async-done(((bf16[16,64,128]{2,1,0:T(8,128)(2,1)}), bf16[16,64,128]{2,1,0:T(8,128)(2,1)S(1)}, u32[]{:S(2)}, u32[]{:S(2)}) %all-to-all-start) | async-done | bytes 262176 | tf_op jit(solution)/shard_map/all_to_all | solution.py:319
  31.0 55.7 %first_over_targets.1 = (f32[2048,2048]{1,0:T(8,128)S(1)}, bf16[256,2048]{1,0:T(8,128)(2,1)S(1)}, f32[16,16,128]{2,1,0:T(8,128)S(1)}) custom-call(bf16[2048,256]{1,0:T(8,128)(2,1)S(1)} %prep_targets.1.yt_ref, bf16[16,64,128]{2,1,0:T(8,128)(2,1)S(1)} %all-to-all-done.x_ref), custom_call_target="tpu_custom_call" | custom-call | tf_op jit(solution)/shard_map/first_over_targets/pallas_call | solution.py:264
  86.7 22.8 %all_to_all.25.parts_ref = f32[16,16,128]{2,1,0:T(8,128)S(1)} all-to-all(f32[16,16,128]{2,1,0:T(8,128)S(1)} %get-tuple-element.8), channel_id=1, replica_groups=mesh['row'=16,'z'=16,'core'=2] {'z'}, dimensions={0} | all-to-all | bytes 262144 | tf_op jit(solution)/shard_map/all_to_all | solution.py:319
  109.5 90.1 %over_sources.2 = (f32[32,16,128]{2,1,0:T(8,128)S(1)}, f32[16,128]{1,0:T(8,128)}) custom-call(f32[16,16,128]{2,1,0:T(8,128)S(1)} %all_to_all.25.parts_ref, f32[2048,2048]{1,0:T(8,128)S(1)} %get-tuple-element.9.e_ref, bf16[2048,256]{1,0:T(8,128)(2,1)S(1)} %prep_targets.1.yt_ref, bf16[256,2048]{1,0:T(8,128)(2,1)S(1)} %get-tuple-element.10.xa_ref), custom_call_target="tpu_custom_call" | custom-call | tf_op jit(solution)/shard_map/over_sources/pallas_call | solution.py:281
  199.6 19.5 %all_to_all.26.parts_ref = f32[32,16,128]{2,1,0:T(8,128)S(1)} all-to-all(f32[32,16,128]{2,1,0:T(8,128)S(1)} %get-tuple-element.11), channel_id=1, replica_groups=mesh['row'=16,'z'=16,'core'=2] {'row','core'}, dimensions={0} | all-to-all | bytes 524288 | tf_op jit(solution)/shard_map/all_to_all | solution.py:319
  219.1 54.3 %over_targets.1 = f32[16,16,128]{2,1,0:T(8,128)S(1)} custom-call(f32[32,16,128]{2,1,0:T(8,128)S(1)} %all_to_all.26.parts_ref, f32[2048,2048]{1,0:T(8,128)S(1)} %get-tuple-element.9.e_ref, bf16[2048,256]{1,0:T(8,128)(2,1)S(1)} %prep_targets.1.yt_ref, bf16[256,2048]{1,0:T(8,128)(2,1)S(1)} %get-tuple-element.10.xa_ref), custom_call_target="tpu_custom_call" | custom-call | tf_op jit(solution)/shard_map/over_targets/pallas_call | solution.py:302
  273.4 15.4 %all_to_all.27.parts_ref = f32[16,16,128]{2,1,0:T(8,128)S(1)} all-to-all(f32[16,16,128]{2,1,0:T(8,128)S(1)} %over_targets.1), channel_id=1, replica_groups=mesh['row'=16,'z'=16,'core'=2] {'z'}, dimensions={0} | all-to-all | bytes 262144 | tf_op jit(solution)/shard_map/all_to_all | solution.py:319
  288.8 90.1 %over_sources.3 = (f32[32,8,128]{2,1,0:T(8,128)}, f32[16,128]{1,0:T(8,128)S(1)}) custom-call(f32[16,16,128]{2,1,0:T(8,128)S(1)} %all_to_all.27.parts_ref, f32[2048,2048]{1,0:T(8,128)S(1)} %get-tuple-element.9.e_ref, bf16[2048,256]{1,0:T(8,128)(2,1)S(1)} %prep_targets.1.yt_ref, bf16[256,2048]{1,0:T(8,128)(2,1)S(1)} %get-tuple-element.10.xa_ref), custom_call_target="tpu_custom_call" | custom-call | tf_op jit(solution)/shard_map/over_sources/pallas_call | solution.py:281
  379.0 4.4 %all-gather.1 = f32[16,256]{1,0:T(8,128)S(1)} all-gather(f32[16,128]{1,0:T(8,128)S(1)} %get-tuple-element.12), channel_id=3, replica_groups=mesh['row'=16,'z'=16,'core'=2] {'core'}, dimensions={1}, use_global_device_ids=true | all-gather | bytes 24576 | tf_op jit(solution)/shard_map/all_gather | solution.py:342
  383.4 3.9 all-to-all-start.4
  387.3 0.6 copy.4
  388.0 7.0 %all-to-all-done.4 = f32[32,8,128]{2,1,0:T(8,128)S(1)} async-done(((f32[32,8,128]{2,1,0:T(8,128)}), f32[32,8,128]{2,1,0:T(8,128)S(1)}, u32[]{:S(2)}, u32[]{:S(2)}) %all-to-all-start.4) | async-done | bytes 131104 | tf_op jit(solution)/shard_map/all_to_all | solution.py:319
  395.0 0.6 multiply_bitcast_fusion.1
  (3 shorter events, 0.1 us)
Async XLA Ops:
  2.1 28.9 %all-to-all-start = ((bf16[16,64,128]{2,1,0:T(8,128)(2,1)}), bf16[16,64,128]{2,1,0:T(8,128)(2,1)S(1)}, u32[]{:S(2)}, u32[]{:S(2)}) async-start(bf16[16,64,128]{2,1,0:T(8,128)(2,1)} %broadcast_in_dim.2), calls=%async_computation | async-start | bytes 524288 | tf_op jit(solution)/shard_map/all_to_all | solution.py:319
  383.4 11.6 %all-to-all-start.4 = ((f32[32,8,128]{2,1,0:T(8,128)}), f32[32,8,128]{2,1,0:T(8,128)S(1)}, u32[]{:S(2)}, u32[]{:S(2)}) async-start(f32[32,8,128]{2,1,0:T(8,128)} %get-tuple-element.13), calls=%async_computation.4 | async-start | bytes 262144 | tf_op jit(solution)/shard_map/all_to_all | solution.py:319

commit v3 on v2

--- a/solution.py
+++ b/solution.py
@@ -123,33 +123,23 @@
 def first_over_targets(tile, yt_ref, x_ref, e_ref, xa_ref, part_ref, sum_ref):
     n_blocks, width, _ = x_ref.shape
     n_tgt = yt_ref.shape[0]
+    n_src = n_blocks * LANES
     for b in range(n_blocks):
         x = x_ref[b].astype(F32)
         sq = jnp.sum(x * x, axis=0, keepdims=True)
         tail = bias_rows(SQ_GAIN * sq, 3, width).astype(BF16)
         xa_ref[:, b * LANES : (b + 1) * LANES] = jnp.concatenate([*split3(INNER_GAIN * x), tail], axis=0)
-    wide = 2 * LANES
-
-    def one(it, _):
-        cols = pl.ds(pl.multiple_of(it * wide, wide), wide)
-        acc = jnp.zeros((8, wide), F32)
-        for jt in range(0, n_tgt, tile):
-            rows = pl.ds(jt, tile)
-            e = jnp.exp2(scores(yt_ref, xa_ref, rows, cols))
-            e_ref[rows, cols] = e
-            acc = acc + jnp.sum(e.reshape(tile // 8, 8, wide), axis=0)
-        total = jnp.sum(acc, axis=0, keepdims=True)
-        sum_ref[pl.ds(2 * it, 1), :] = total[:, :LANES]
-        sum_ref[pl.ds(2 * it + 1, 1), :] = total[:, LANES:]
-        return 0
-
-    lax.fori_loop(0, n_blocks // 2, one, 0)
+    acc = jnp.zeros((8, n_src), F32)
+    for jt in range(0, n_tgt, tile):
+        e = jnp.exp2(scores(yt_ref, xa_ref, pl.ds(jt, tile), slice(None)))
+        e_ref[jt : jt + tile, :] = e
+        acc = acc + jnp.sum(e.reshape(tile // 8, 8, n_src), axis=0)
+    total = jnp.sum(acc, axis=0, keepdims=True)
+    for b in range(n_blocks):
+        sum_ref[b : b + 1, :] = total[:, b * LANES : (b + 1) * LANES]
     totals = sum_ref[...]
+    send(jnp.log2(totals), part_ref)
     fast = (jnp.min(totals) >= 2.0**LOW) & (jnp.max(totals) <= 2.0**HIGH)
-
-    @pl.when(fast)
-    def _():
-        send(jnp.log2(totals), part_ref)
 
     @pl.when(jnp.logical_not(fast))
     def _():
@@ -163,27 +153,28 @@
     return (top <= HIGH) & (jnp.min(totals) >= floor)
 
 
-def over_sources(log_targets, rows_at_once, parts_ref, e_ref, yt_ref, xa_ref, part_ref, pot_ref, sum_ref, acc_ref, yt_buf, xa_buf):
+def over_sources(log_targets, at_once, parts_ref, e_ref, yt_ref, xa_ref, part_ref, sum_ref, pot_ref, acc_ref, yt_buf, xa_buf):
     n_tgt, n_src = e_ref.shape
     n_blocks = n_src // LANES
     pot = log_targets - merge(parts_ref[...])
     pot_ref[...] = pot
     u = jnp.exp2(jnp.minimum(pot, HIGH))
+    u = [jnp.broadcast_to(u[b : b + 1], (8, LANES)) for b in range(n_blocks)]
 
     def one(jt, _):
-        rows = pl.ds(pl.multiple_of(jt * rows_at_once, rows_at_once), rows_at_once)
-        acc = e_ref[rows, :LANES] * u[:1]
-        for b in range(1, n_blocks):
-            acc = acc + e_ref[rows, b * LANES : (b + 1) * LANES] * u[b : b + 1]
-        acc_ref[rows, :] = acc
+        for r in range(0, at_once, 8):
+            rows = pl.ds(pl.multiple_of(jt * at_once + r, 8), 8)
+            acc = e_ref[rows, :LANES] * u[0]
+            for b in range(1, n_blocks):
+                acc = acc + e_ref[rows, b * LANES : (b + 1) * LANES] * u[b]
+            acc_ref[rows, :] = acc
         return 0
 
-    lax.fori_loop(0, n_tgt // rows_at_once, one, 0)
+    lax.fori_loop(0, n_tgt // at_once, one, 0)
     for k in range(n_tgt // LANES):
         block = acc_ref[k * LANES : (k + 1) * LANES, :].T
         sum_ref[k : k + 1, :] = jnp.sum(block, axis=0, keepdims=True)
     totals = sum_ref[...]
-    fast = checked(totals, pot)
 
     def put(value):
         copies, n, _ = part_ref.shape
@@ -191,11 +182,9 @@
             at = (k * n) % value.shape[0]
             part_ref[k] = value[at : at + n]
 
-    @pl.when(fast)
-    def _():
-        put(jnp.log2(totals))
-
-    @pl.when(jnp.logical_not(fast))
+    put(jnp.log2(totals))
+
+    @pl.when(jnp.logical_not(checked(totals, pot)))
     def _():
         pltpu.sync_copy(yt_ref, yt_buf)
         pltpu.sync_copy(xa_ref, xa_buf)
@@ -203,7 +192,7 @@
         put(sum_ref[...])
 
 
-def over_targets(log_sources, rows_at_once, parts_ref, e_ref, yt_ref, xa_ref, part_ref, sum_ref, pot_ref, yt_buf, xa_buf):
+def over_targets(log_sources, at_once, parts_ref, e_ref, yt_ref, xa_ref, part_ref, sum_ref, pot_ref, yt_buf, xa_buf):
     n_tgt, n_src = e_ref.shape
     n_blocks = n_src // LANES
     pot = log_sources - merge(parts_ref[...])
@@ -211,24 +200,20 @@
 
     def one(jt, acc):
         acc = list(acc)
-        for r in range(rows_at_once // 8):
-            rows = pl.ds(pl.multiple_of(jt * rows_at_once + 8 * r, 8), 8)
+        for r in range(0, at_once, 8):
+            rows = pl.ds(pl.multiple_of(jt * at_once + r, 8), 8)
             v = pot_ref[rows, :]
             for b in range(n_blocks):
                 acc[b] = acc[b] + e_ref[rows, b * LANES : (b + 1) * LANES] * v
         return tuple(acc)
 
-    acc = lax.fori_loop(0, n_tgt // rows_at_once, one, (jnp.zeros((8, LANES), F32),) * n_blocks)
+    acc = lax.fori_loop(0, n_tgt // at_once, one, (jnp.zeros((8, LANES), F32),) * n_blocks)
     for b in range(n_blocks):
         sum_ref[b : b + 1, :] = jnp.sum(acc[b], axis=0, keepdims=True)
     totals = sum_ref[...]
-    fast = checked(totals, pot)
-
-    @pl.when(fast)
-    def _():
-        send(jnp.log2(totals), part_ref)
-
-    @pl.when(jnp.logical_not(fast))
+    send(jnp.log2(totals), part_ref)
+
+    @pl.when(jnp.logical_not(checked(totals, pot)))
     def _():
         pltpu.sync_copy(yt_ref, yt_buf)
         pltpu.sync_copy(xa_ref, xa_buf)
@@ -237,6 +222,14 @@
         send(sum_ref[...], part_ref)
 
 
+def make_copies(x_ref, out_ref):
+    send(x_ref[...], out_ref)
+
+
+def finish_targets(log_sources, parts_ref, out_ref):
+    out_ref[...] = FROM_LOG2 * (log_sources - merge(parts_ref[...]))
+
+
 VMEM = pl.BlockSpec(memory_space=pltpu.VMEM)
 ANY = pl.BlockSpec(memory_space=pl.ANY)
 LIMIT = 20 << 20
@@ -258,7 +251,29 @@
     )(y)
 
 
-def call_first(yt, x, copies, tile=512):
+def call_copies(x, copies):
+    return pl.pallas_call(
+        make_copies,
+        out_shape=jax.ShapeDtypeStruct((copies,) + x.shape, x.dtype),
+        in_specs=[VMEM],
+        out_specs=VMEM,
+        compiler_params=params(),
+        name="make_copies",
+    )(x)
+
+
+def call_finish(log_sources, parts):
+    return pl.pallas_call(
+        functools.partial(finish_targets, log_sources),
+        out_shape=jax.ShapeDtypeStruct(parts.shape[1:], F32),
+        in_specs=[VMEM],
+        out_specs=VMEM,
+        compiler_params=params(),
+        name="finish_targets",
+    )(parts)
+
+
+def call_first(yt, x, copies, tile=128):
     n_blocks, width, lanes = x.shape
     n_tgt, n_src = yt.shape[0], n_blocks * lanes
     return pl.pallas_call(
@@ -276,18 +291,16 @@
     )(yt, x)
 
 
-def call_over_sources(log_targets, parts, e, yt, xa, part_shape, rows_at_once=32):
+def call_over_sources(log_targets, parts, e, yt, xa, part_shape, at_once=128):
     n_tgt, n_src = e.shape
     return pl.pallas_call(
-        functools.partial(over_sources, log_targets, rows_at_once),
-        out_shape=(
-            jax.ShapeDtypeStruct(part_shape, F32),
-            jax.ShapeDtypeStruct((n_src // LANES, LANES), F32),
-        ),
+        functools.partial(over_sources, log_targets, at_once),
+        out_shape=jax.ShapeDtypeStruct(part_shape, F32),
         in_specs=[VMEM, VMEM, ANY, ANY],
-        out_specs=(VMEM, VMEM),
+        out_specs=VMEM,
         scratch_shapes=[
             pltpu.VMEM((n_tgt // LANES, LANES), F32),
+            pltpu.VMEM((n_src // LANES, LANES), F32),
             pltpu.VMEM((n_tgt, LANES), F32),
             pltpu.VMEM(yt.shape, BF16),
             pltpu.VMEM(xa.shape, BF16),
@@ -297,10 +310,10 @@
     )(parts, e, yt, xa)
 
 
-def call_over_targets(log_sources, parts, e, yt, xa, copies, rows_at_once=32):
+def call_over_targets(log_sources, parts, e, yt, xa, copies, at_once=128):
     n_tgt, n_src = e.shape
     return pl.pallas_call(
-        functools.partial(over_targets, log_sources, rows_at_once),
+        functools.partial(over_targets, log_sources, at_once),
         out_shape=jax.ShapeDtypeStruct((copies, n_src // LANES, LANES), F32),
         in_specs=[VMEM, VMEM, ANY, ANY],
         out_specs=VMEM,
@@ -326,21 +339,20 @@
     log_targets = math.log2(tgt_own * n_z * n_core)
     n_tgt = n_core * tgt_own
     group = n_row * n_core
-    x = exchange(jnp.broadcast_to(src_feat[None], (n_z, width, src_own)), "z")
+    x = exchange(call_copies(src_feat, n_z), "z")
     yt = call_prep(lax.all_gather(tgt_feat, "core"))
     e, xa, part = call_first(yt, x, n_z)
     for step in range(ITERS):
         parts = exchange(part, "z")
         if step < ITERS - 1:
-            part, _ = call_over_sources(log_targets, parts, e, yt, xa, (group, n_tgt // LANES, LANES))
-            parts = exchange(part, ("row", "core"))
-            part = call_over_targets(log_sources, parts, e, yt, xa, n_z)
+            part = call_over_sources(log_targets, parts, e, yt, xa, (group, n_tgt // LANES, LANES))
+            part = call_over_targets(log_sources, exchange(part, ("row", "core")), e, yt, xa, n_z)
         else:
-            part, src = call_over_sources(log_targets, parts, e, yt, xa, (group, tgt_own // LANES, LANES))
-            parts = exchange(part, ("row", "core"))
-    tgt_pot = FROM_LOG2 * (log_sources - merge(parts)).reshape(tgt_own)
-    src = lax.all_gather(src, "core", axis=1)
-    return FROM_LOG2 * src.reshape(n_core * n_z * src_own), tgt_pot
+            part = call_over_sources(log_targets, parts, e, yt, xa, (group, tgt_own // LANES, LANES))
+            src_pot = FROM_LOG2 * (log_targets - merge(parts))
+            src_pot = lax.all_gather(src_pot, "core", axis=1)
+            tgt_pot = call_finish(log_sources, exchange(part, ("row", "core")))
+    return src_pot.reshape(n_core * n_z * src_own), tgt_pot.reshape(tgt_own)
 
 
 def solution(mesh):

time: 396 us -> 391 us (0.987)
    pallas_call x3 -> x5, Pallas kernels: 235 us -> 234 us  [the longest x2 178 us: call_over_sources(): pl.pallas_call(functools.partial(over_sources, log_targets, at_once), out...]
where the time goes in v3:
time: 391 us
  Pallas kernels  289 us (74%)
  blocking collectives  62.3 us (16%)
  starting transfers between devices  22.3 us (6%)
  waiting for transfers between devices  15.1 us (4%)
    pallas_call x2, Pallas kernels, call_over_sources(): pl.pallas_call(functools.partial(over_sources, log_targets, at_once), out...  178 us
    all_to_all x3, blocking collectives, exchange(): return lax.all_to_all(value, axis, 0, 0, tiled=False)  57.7 us
    pallas_call x1, Pallas kernels, call_first(): pl.pallas_call(functools.partial(first_over_targets, tile), out_shape=(pl...  54.5 us
    pallas_call x1, Pallas kernels, call_over_targets(): pl.pallas_call(functools.partial(over_targets, log_sources, at_once), out...  54 us
    all_to_all x2, starting transfers between devices, exchange(): return lax.all_to_all(value, axis, 0, 0, tiled=False)  22.3 us
    all_to_all x2, waiting for transfers between devices, exchange(): return lax.all_to_all(value, axis, 0, 0, tiled=False)  15.1 us
  transfers between devices with their start and end apart: 2, of which 2 were waited for; matrix products, arithmetic and copies ran while one was open for 0% of the time, Pallas kernels for 0%

profile of v3, /device:TPU:1, one launch (start us, length us, event | category | flops | bytes accessed | tf_op | source)
XLA Modules:
  0.0 390.6 jit_solution(18446609920282074886)
XLA Ops:
  0.6 0.0 copy-start
  0.6 0.7 copy-done
  1.3 0.7 make_copies.1
  2.1 15.7 %all-to-all-start = ((bf16[16,64,128]{2,1,0:T(8,128)(2,1)}), bf16[16,64,128]{2,1,0:T(8,128)(2,1)S(1)}, u32[]{:S(2)}, u32[]{:S(2)}) async-start(bf16[16,64,128]{2,1,0:T(8,128)(2,1)} %make_copies.1), calls=%async_computation | async-start | bytes 524288 | tf_op jit(solution)/shard_map/all_to_all | solution.py:332
  17.8 2.8 all-gather
  20.6 0.4 prep_targets.1.yt_ref
  21.0 10.0 %all-to-all-done.x_ref = bf16[16,64,128]{2,1,0:T(8,128)(2,1)S(1)} async-done(((bf16[16,64,128]{2,1,0:T(8,128)(2,1)}), bf16[16,64,128]{2,1,0:T(8,128)(2,1)S(1)}, u32[]{:S(2)}, u32[]{:S(2)}) %all-to-all-start) | async-done | bytes 262176 | tf_op jit(solution)/shard_map/all_to_all | solution.py:332
  31.0 54.5 %first_over_targets.1 = (f32[2048,2048]{1,0:T(8,128)S(1)}, bf16[256,2048]{1,0:T(8,128)(2,1)S(1)}, f32[16,16,128]{2,1,0:T(8,128)S(1)}) custom-call(bf16[2048,256]{1,0:T(8,128)(2,1)S(1)} %prep_targets.1.yt_ref, bf16[16,64,128]{2,1,0:T(8,128)(2,1)S(1)} %all-to-all-done.x_ref), custom_call_target="tpu_custom_call" | custom-call | tf_op jit(solution)/shard_map/first_over_targets/pallas_call | solution.py:279
  85.5 22.7 %all_to_all.25.parts_ref = f32[16,16,128]{2,1,0:T(8,128)S(1)} all-to-all(f32[16,16,128]{2,1,0:T(8,128)S(1)} %get-tuple-element.5), channel_id=1, replica_groups=mesh['row'=16,'z'=16,'core'=2] {'z'}, dimensions={0} | all-to-all | bytes 262144 | tf_op jit(solution)/shard_map/all_to_all | solution.py:332
  108.2 88.9 %over_sources.2 = f32[32,16,128]{2,1,0:T(8,128)S(1)} custom-call(f32[16,16,128]{2,1,0:T(8,128)S(1)} %all_to_all.25.parts_ref, f32[2048,2048]{1,0:T(8,128)S(1)} %get-tuple-element.6.e_ref, bf16[2048,256]{1,0:T(8,128)(2,1)S(1)} %prep_targets.1.yt_ref, bf16[256,2048]{1,0:T(8,128)(2,1)S(1)} %get-tuple-element.7.xa_ref), custom_call_target="tpu_custom_call" | custom-call | tf_op jit(solution)/shard_map/over_sources/pallas_call | solution.py:296
  197.1 19.5 %all_to_all.26.parts_ref = f32[32,16,128]{2,1,0:T(8,128)S(1)} all-to-all(f32[32,16,128]{2,1,0:T(8,128)S(1)} %over_sources.2), channel_id=1, replica_groups=mesh['row'=16,'z'=16,'core'=2] {'row','core'}, dimensions={0} | all-to-all | bytes 524288 | tf_op jit(solution)/shard_map/all_to_all | solution.py:332
  216.7 54.0 %over_targets.1 = f32[16,16,128]{2,1,0:T(8,128)S(1)} custom-call(f32[32,16,128]{2,1,0:T(8,128)S(1)} %all_to_all.26.parts_ref, f32[2048,2048]{1,0:T(8,128)S(1)} %get-tuple-element.6.e_ref, bf16[2048,256]{1,0:T(8,128)(2,1)S(1)} %prep_targets.1.yt_ref, bf16[256,2048]{1,0:T(8,128)(2,1)S(1)} %get-tuple-element.7.xa_ref), custom_call_target="tpu_custom_call" | custom-call | tf_op jit(solution)/shard_map/over_targets/pallas_call | solution.py:315
  270.7 15.4 %all_to_all.27.parts_ref = f32[16,16,128]{2,1,0:T(8,128)S(1)} all-to-all(f32[16,16,128]{2,1,0:T(8,128)S(1)} %over_targets.1), channel_id=1, replica_groups=mesh['row'=16,'z'=16,'core'=2] {'z'}, dimensions={0} | all-to-all | bytes 262144 | tf_op jit(solution)/shard_map/all_to_all | solution.py:332
  286.2 89.6 %over_sources.3 = f32[32,8,128]{2,1,0:T(8,128)} custom-call(f32[16,16,128]{2,1,0:T(8,128)S(1)} %all_to_all.27.parts_ref, f32[2048,2048]{1,0:T(8,128)S(1)} %get-tuple-element.6.e_ref, bf16[2048,256]{1,0:T(8,128)(2,1)S(1)} %prep_targets.1.yt_ref, bf16[256,2048]{1,0:T(8,128)(2,1)S(1)} %get-tuple-element.7.xa_ref), custom_call_target="tpu_custom_call" | custom-call | tf_op jit(solution)/shard_map/over_sources/pallas_call | solution.py:296
  375.7 6.6 %all-to-all-start.4 = ((f32[32,8,128]{2,1,0:T(8,128)}), f32[32,8,128]{2,1,0:T(8,128)S(1)}, u32[]{:S(2)}, u32[]{:S(2)}) async-start(f32[32,8,128]{2,1,0:T(8,128)} %over_sources.3), calls=%async_computation.4 | async-start | bytes 262144 | tf_op jit(solution)/shard_map/all_to_all | solution.py:332
  382.4 1.8 all-gather.1
  384.2 0.6 copy.4
  384.8 5.1 %all-to-all-done.4.parts_ref = f32[32,8,128]{2,1,0:T(8,128)S(1)} async-done(((f32[32,8,128]{2,1,0:T(8,128)}), f32[32,8,128]{2,1,0:T(8,128)S(1)}, u32[]{:S(2)}, u32[]{:S(2)}) %all-to-all-start.4) | async-done | bytes 131104 | tf_op jit(solution)/shard_map/all_to_all | solution.py:332
  389.9 0.7 finish_targets.1
  (3 shorter events, 0.1 us)
Async XLA Ops:
  0.6 0.7 copy-start
  2.1 28.9 %all-to-all-start = ((bf16[16,64,128]{2,1,0:T(8,128)(2,1)}), bf16[16,64,128]{2,1,0:T(8,128)(2,1)S(1)}, u32[]{:S(2)}, u32[]{:S(2)}) async-start(bf16[16,64,128]{2,1,0:T(8,128)(2,1)} %make_copies.1), calls=%async_computation | async-start | bytes 524288 | tf_op jit(solution)/shard_map/all_to_all | solution.py:332
  375.7 14.2 %all-to-all-start.4 = ((f32[32,8,128]{2,1,0:T(8,128)}), f32[32,8,128]{2,1,0:T(8,128)S(1)}, u32[]{:S(2)}, u32[]{:S(2)}) async-start(f32[32,8,128]{2,1,0:T(8,128)} %over_sources.3), calls=%async_computation.4 | async-start | bytes 262144 | tf_op jit(solution)/shard_map/all_to_all | solution.py:332

commit v4 on v3

--- a/solution.py
+++ b/solution.py
@@ -8,7 +8,6 @@
 from jax.experimental.pallas import tpu as pltpu
 from jax.sharding import Mesh, PartitionSpec as P
 
-ITERS = 2
 INV_EPS = 20.0
 EPS = 0.05
 LANES = 128
@@ -153,10 +152,17 @@
     return (top <= HIGH) & (jnp.min(totals) >= floor)
 
 
-def over_sources(log_targets, at_once, parts_ref, e_ref, yt_ref, xa_ref, part_ref, sum_ref, pot_ref, acc_ref, yt_buf, xa_buf):
+def changed(before, change):
+    return before + change.astype(F32)
+
+
+def over_sources(log_targets, at_once, n_parts, *refs):
+    parts_refs, refs = refs[:n_parts], refs[n_parts:]
+    e_ref, yt_ref, xa_ref, part_ref, sum_ref, pot_ref, acc_ref, yt_buf, xa_buf = refs
     n_tgt, n_src = e_ref.shape
     n_blocks = n_src // LANES
-    pot = log_targets - merge(parts_ref[...])
+    parts = [ref[...] for ref in parts_refs]
+    pot = log_targets - merge(parts[0] if n_parts == 1 else changed(*parts))
     pot_ref[...] = pot
     u = jnp.exp2(jnp.minimum(pot, HIGH))
     u = [jnp.broadcast_to(u[b : b + 1], (8, LANES)) for b in range(n_blocks)]
@@ -192,7 +198,7 @@
         put(sum_ref[...])
 
 
-def over_targets(log_sources, at_once, parts_ref, e_ref, yt_ref, xa_ref, part_ref, sum_ref, pot_ref, yt_buf, xa_buf):
+def over_targets(log_sources, at_once, parts_ref, before_ref, e_ref, yt_ref, xa_ref, part_ref, sum_ref, pot_ref, yt_buf, xa_buf):
     n_tgt, n_src = e_ref.shape
     n_blocks = n_src // LANES
     pot = log_sources - merge(parts_ref[...])
@@ -211,7 +217,8 @@
     for b in range(n_blocks):
         sum_ref[b : b + 1, :] = jnp.sum(acc[b], axis=0, keepdims=True)
     totals = sum_ref[...]
-    send(jnp.log2(totals), part_ref)
+    before = before_ref[0]
+    send((jnp.log2(totals) - before).astype(BF16), part_ref)
 
     @pl.when(jnp.logical_not(checked(totals, pot)))
     def _():
@@ -219,11 +226,15 @@
         pltpu.sync_copy(xa_ref, xa_buf)
         spread_to_rows(pot, pot_ref)
         slow_over_targets(yt_buf, xa_buf, pot_ref, sum_ref)
-        send(sum_ref[...], part_ref)
-
-
-def make_copies(x_ref, out_ref):
-    send(x_ref[...], out_ref)
+        send((sum_ref[...] - before).astype(BF16), part_ref)
+
+
+def make_copies(x_ref, out_ref, sems):
+    copies = [pltpu.make_async_copy(x_ref, out_ref.at[k], sems.at[k]) for k in range(out_ref.shape[0])]
+    for copy in copies:
+        copy.start()
+    for copy in copies:
+        copy.wait()
 
 
 def finish_targets(log_sources, parts_ref, out_ref):
@@ -254,12 +265,13 @@
 def call_copies(x, copies):
     return pl.pallas_call(
         make_copies,
-        out_shape=jax.ShapeDtypeStruct((copies,) + x.shape, x.dtype),
-        in_specs=[VMEM],
-        out_specs=VMEM,
+        out_shape=pltpu.HBM((copies,) + x.shape, x.dtype),
+        in_specs=[ANY],
+        out_specs=ANY,
+        scratch_shapes=[pltpu.SemaphoreType.DMA((copies,))],
         compiler_params=params(),
         name="make_copies",
-    )(x)
+    )(pltpu.with_memory_space_constraint(x, pltpu.HBM))
 
 
 def call_finish(log_sources, parts):
@@ -291,12 +303,12 @@
     )(yt, x)
 
 
-def call_over_sources(log_targets, parts, e, yt, xa, part_shape, at_once=128):
+def call_over_sources(log_targets, e, yt, xa, part_shape, *parts, at_once=128):
     n_tgt, n_src = e.shape
     return pl.pallas_call(
-        functools.partial(over_sources, log_targets, at_once),
+        functools.partial(over_sources, log_targets, at_once, len(parts)),
         out_shape=jax.ShapeDtypeStruct(part_shape, F32),
-        in_specs=[VMEM, VMEM, ANY, ANY],
+        in_specs=[VMEM] * len(parts) + [VMEM, ANY, ANY],
         out_specs=VMEM,
         scratch_shapes=[
             pltpu.VMEM((n_tgt // LANES, LANES), F32),
@@ -307,15 +319,15 @@
         ],
         compiler_params=params(),
         name="over_sources",
-    )(parts, e, yt, xa)
-
-
-def call_over_targets(log_sources, parts, e, yt, xa, copies, at_once=128):
+    )(*parts, e, yt, xa)
+
+
+def call_over_targets(log_sources, parts, before, e, yt, xa, copies, at_once=128):
     n_tgt, n_src = e.shape
     return pl.pallas_call(
         functools.partial(over_targets, log_sources, at_once),
-        out_shape=jax.ShapeDtypeStruct((copies, n_src // LANES, LANES), F32),
-        in_specs=[VMEM, VMEM, ANY, ANY],
+        out_shape=jax.ShapeDtypeStruct((copies, n_src // LANES, LANES), BF16),
+        in_specs=[VMEM, VMEM, VMEM, ANY, ANY],
         out_specs=VMEM,
         scratch_shapes=[
             pltpu.VMEM((n_src // LANES, LANES), F32),
@@ -325,7 +337,7 @@
         ],
         compiler_params=params(),
         name="over_targets",
-    )(parts, e, yt, xa)
+    )(parts, before, e, yt, xa)
 
 
 def exchange(value, axis):
@@ -342,16 +354,14 @@
     x = exchange(call_copies(src_feat, n_z), "z")
     yt = call_prep(lax.all_gather(tgt_feat, "core"))
     e, xa, part = call_first(yt, x, n_z)
-    for step in range(ITERS):
-        parts = exchange(part, "z")
-        if step < ITERS - 1:
-            part = call_over_sources(log_targets, parts, e, yt, xa, (group, n_tgt // LANES, LANES))
-            part = call_over_targets(log_sources, exchange(part, ("row", "core")), e, yt, xa, n_z)
-        else:
-            part = call_over_sources(log_targets, parts, e, yt, xa, (group, tgt_own // LANES, LANES))
-            src_pot = FROM_LOG2 * (log_targets - merge(parts))
-            src_pot = lax.all_gather(src_pot, "core", axis=1)
-            tgt_pot = call_finish(log_sources, exchange(part, ("row", "core")))
+    first = exchange(part, "z")
+    col_part = call_over_sources(log_targets, e, yt, xa, (group, n_tgt // LANES, LANES), first)
+    col_parts = exchange(col_part, ("row", "core"))
+    change = exchange(call_over_targets(log_sources, col_parts, part, e, yt, xa, n_z), "z")
+    col_part = call_over_sources(log_targets, e, yt, xa, (group, tgt_own // LANES, LANES), first, change)
+    src_pot = FROM_LOG2 * (log_targets - merge(changed(first, change)))
+    src_pot = lax.all_gather(src_pot, "core", axis=1)
+    tgt_pot = call_finish(log_sources, exchange(col_part, ("row", "core")))
     return src_pot.reshape(n_core * n_z * src_own), tgt_pot.reshape(tgt_own)
 
 

time: 391 us -> 397 us (1.015)
  Pallas kernels: 289 us -> 297 us
    pallas_call x3, Pallas kernels: 179 us -> 188 us  [the longest x2 178 us: call_over_sources(): pl.pallas_call(functools.partial(over_sources, log_targets, at_once, len(...]
where the time goes in v4:
time: 397 us
  Pallas kernels  297 us (75%)
  blocking collectives  61.8 us (16%)
  starting transfers between devices  21.3 us (5%)
  waiting for transfers between devices  15.2 us (4%)
    pallas_call x2, Pallas kernels, call_over_sources(): pl.pallas_call(functools.partial(over_sources, log_targets, at_once, len(...  178 us
    all_to_all x3, blocking collectives, exchange(): return lax.all_to_all(value, axis, 0, 0, tiled=False)  57.1 us
    pallas_call x1, Pallas kernels, call_first(): pl.pallas_call(functools.partial(first_over_targets, tile), out_shape=(pl...  54.5 us
    pallas_call x1, Pallas kernels, call_over_targets(): pl.pallas_call(functools.partial(over_targets, log_sources, at_once), out...  54 us
    all_to_all x2, starting transfers between devices, exchange(): return lax.all_to_all(value, axis, 0, 0, tiled=False)  21.3 us
    all_to_all x2, waiting for transfers between devices, exchange(): return lax.all_to_all(value, axis, 0, 0, tiled=False)  15.2 us
    pallas_call x1, Pallas kernels, call_copies(): pl.pallas_call(make_copies, out_shape=pltpu.HBM((copies,) + x.shape, x.dt...  9.18 us
  transfers between devices with their start and end apart: 2, of which 2 were waited for; matrix products, arithmetic and copies ran while one was open for 0% of the time, Pallas kernels for 0%

profile of v4, /device:TPU:1, one launch (start us, length us, event | category | flops | bytes accessed | tf_op | source)
XLA Modules:
  0.0 396.7 jit_solution(5152867292917358662)
XLA Ops:
  0.6 9.2 %make_copies.1 = bf16[16,64,128]{2,1,0:T(8,128)(2,1)} custom-call(bf16[64,128]{1,0:T(8,128)(2,1)} %x_ref.1), custom_call_target="tpu_custom_call" | custom-call | tf_op jit(solution)/shard_map/make_copies/pallas_call | solution.py:266
  9.8 15.8 %all-to-all-start = ((bf16[16,64,128]{2,1,0:T(8,128)(2,1)}), bf16[16,64,128]{2,1,0:T(8,128)(2,1)S(1)}, u32[]{:S(2)}, u32[]{:S(2)}) async-start(bf16[16,64,128]{2,1,0:T(8,128)(2,1)} %make_copies.1), calls=%async_computation | async-start | bytes 524288 | tf_op jit(solution)/shard_map/all_to_all | solution.py:344
  25.6 2.8 all-gather
  28.4 0.4 prep_targets.1.yt_ref.refs_2_.refs_3_
  28.8 10.0 %all-to-all-done.x_ref = bf16[16,64,128]{2,1,0:T(8,128)(2,1)S(1)} async-done(((bf16[16,64,128]{2,1,0:T(8,128)(2,1)}), bf16[16,64,128]{2,1,0:T(8,128)(2,1)S(1)}, u32[]{:S(2)}, u32[]{:S(2)}) %all-to-all-start) | async-done | bytes 262176 | tf_op jit(solution)/shard_map/all_to_all | solution.py:344
  38.7 54.5 %first_over_targets.1 = (f32[2048,2048]{1,0:T(8,128)S(1)}, bf16[256,2048]{1,0:T(8,128)(2,1)S(1)}, f32[16,16,128]{2,1,0:T(8,128)S(1)}) custom-call(bf16[2048,256]{1,0:T(8,128)(2,1)S(1)} %prep_targets.1.yt_ref.refs_2_.refs_3_, bf16[16,64,128]{2,1,0:T(8,128)(2,1)S(1)} %all-to-all-done.x_ref), custom_call_target="tpu_custom_call" | custom-call | tf_op jit(solution)/shard_map/first_over_targets/pallas_call | solution.py:291
  93.2 22.7 %all_to_all.25.refs_0_ = f32[16,16,128]{2,1,0:T(8,128)S(1)} all-to-all(f32[16,16,128]{2,1,0:T(8,128)S(1)} %get-tuple-element.5.before_ref), channel_id=1, replica_groups=mesh['row'=16,'z'=16,'core'=2] {'z'}, dimensions={0} | all-to-all | bytes 262144 | tf_op jit(solution)/shard_map/all_to_all | solution.py:344
  115.9 88.9 %over_sources.2 = f32[32,16,128]{2,1,0:T(8,128)S(1)} custom-call(f32[16,16,128]{2,1,0:T(8,128)S(1)} %all_to_all.25.refs_0_, f32[2048,2048]{1,0:T(8,128)S(1)} %get-tuple-element.6.refs_1_.e_ref.refs_2_, bf16[2048,256]{1,0:T(8,128)(2,1)S(1)} %prep_targets.1.yt_ref.refs_2_.refs_3_, bf16[256,2048]{1,0:T(8,128)(2,1)S(1)} %get-tuple-element.7.refs_3_.xa_ref.refs_4_), custom_call_target="tpu_custom_call" | custom-call | tf_op jit(solution)/shard_map/over_sources/pallas_call | solution.py:308
  204.9 19.5 %all_to_all.26.parts_ref = f32[32,16,128]{2,1,0:T(8,128)S(1)} all-to-all(f32[32,16,128]{2,1,0:T(8,128)S(1)} %over_sources.2), channel_id=1, replica_groups=mesh['row'=16,'z'=16,'core'=2] {'row','core'}, dimensions={0} | all-to-all | bytes 524288 | tf_op jit(solution)/shard_map/all_to_all | solution.py:344
  224.4 54.0 %over_targets.1 = bf16[16,16,128]{2,1,0:T(8,128)(2,1)S(1)} custom-call(f32[32,16,128]{2,1,0:T(8,128)S(1)} %all_to_all.26.parts_ref, f32[16,16,128]{2,1,0:T(8,128)S(1)} %get-tuple-element.5.before_ref, f32[2048,2048]{1,0:T(8,128)S(1)} %get-tuple-element.6.refs_1_.e_ref.refs_2_, bf16[2048,256]{1,0:T(8,128)(2,1)S(1)} %prep_targets.1.yt_ref.refs_2_.refs_3_, ...), custom_call_target="tpu_custom_call" | custom-call | tf_op jit(solution)/shard_map/over_targets/pallas_call | solution.py:327
  278.4 14.9 %all_to_all.27.refs_1_ = bf16[16,16,128]{2,1,0:T(8,128)(2,1)S(1)} all-to-all(bf16[16,16,128]{2,1,0:T(8,128)(2,1)S(1)} %over_targets.1), channel_id=1, replica_groups=mesh['row'=16,'z'=16,'core'=2] {'z'}, dimensions={0} | all-to-all | bytes 131072 | tf_op jit(solution)/shard_map/all_to_all | solution.py:344
  293.2 89.6 %over_sources.3 = f32[32,8,128]{2,1,0:T(8,128)} custom-call(f32[16,16,128]{2,1,0:T(8,128)S(1)} %all_to_all.25.refs_0_, bf16[16,16,128]{2,1,0:T(8,128)(2,1)S(1)} %all_to_all.27.refs_1_, f32[2048,2048]{1,0:T(8,128)S(1)} %get-tuple-element.6.refs_1_.e_ref.refs_2_, bf16[2048,256]{1,0:T(8,128)(2,1)S(1)} %prep_targets.1.yt_ref.refs_2_.refs_3_, ...), custom_call_target="tpu_custom_call" | custom-call | tf_op jit(solution)/shard_map/over_sources/pallas_call | solution.py:308
  382.8 5.6 %all-to-all-start.4 = ((f32[32,8,128]{2,1,0:T(8,128)}), f32[32,8,128]{2,1,0:T(8,128)S(1)}, u32[]{:S(2)}, u32[]{:S(2)}) async-start(f32[32,8,128]{2,1,0:T(8,128)} %over_sources.3), calls=%async_computation.4 | async-start | bytes 262144 | tf_op jit(solution)/shard_map/all_to_all | solution.py:344
  388.4 1.8 all-gather.1
  390.3 0.6 copy.4
  390.9 5.2 %all-to-all-done.4.parts_ref = f32[32,8,128]{2,1,0:T(8,128)S(1)} async-done(((f32[32,8,128]{2,1,0:T(8,128)}), f32[32,8,128]{2,1,0:T(8,128)S(1)}, u32[]{:S(2)}, u32[]{:S(2)}) %all-to-all-start.4) | async-done | bytes 131104 | tf_op jit(solution)/shard_map/all_to_all | solution.py:344
  396.1 0.7 finish_targets.1
  (3 shorter events, 0.1 us)
Async XLA Ops:
  9.8 28.9 %all-to-all-start = ((bf16[16,64,128]{2,1,0:T(8,128)(2,1)}), bf16[16,64,128]{2,1,0:T(8,128)(2,1)S(1)}, u32[]{:S(2)}, u32[]{:S(2)}) async-start(bf16[16,64,128]{2,1,0:T(8,128)(2,1)} %make_copies.1), calls=%async_computation | async-start | bytes 524288 | tf_op jit(solution)/shard_map/all_to_all | solution.py:344
  382.8 13.3 %all-to-all-start.4 = ((f32[32,8,128]{2,1,0:T(8,128)}), f32[32,8,128]{2,1,0:T(8,128)S(1)}, u32[]{:S(2)}, u32[]{:S(2)}) async-start(f32[32,8,128]{2,1,0:T(8,128)} %over_sources.3), calls=%async_computation.4 | async-start | bytes 262144 | tf_op jit(solution)/shard_map/all_to_all | solution.py:344

commit v5 on v4

--- a/solution.py
+++ b/solution.py
@@ -16,6 +16,7 @@
 FROM_LOG2 = EPS * math.log(2.0)
 LOW, HIGH = -91.0, 100.0
 F32, BF16 = jnp.float32, jnp.bfloat16
+POWER, SHIFT, SMALL = 11.0, -22.0, 2.0**-9
 
 
 def split3(v):
@@ -53,6 +54,21 @@
 def merge(parts):
     peak = jnp.max(parts, axis=0)
     return peak + jnp.log2(jnp.sum(jnp.exp2(parts - peak[None]), axis=0))
+
+
+def encode(d):
+    size = jnp.abs(d)
+    t = jnp.exp2(POWER * jnp.log2(jnp.maximum(size, SMALL)) + SHIFT)
+    t = jnp.where(size < SMALL, 0.0, t)
+    return jnp.where(d < 0.0, -t, t).astype(BF16)
+
+
+def decode(code):
+    t = code.astype(F32)
+    size = jnp.abs(t)
+    d = jnp.exp2((jnp.log2(jnp.maximum(size, 2.0**-126)) - SHIFT) * (1.0 / POWER))
+    d = jnp.where(size > 0.0, d, 0.0)
+    return jnp.where(t < 0.0, -d, d)
 
 
 def spread_to_rows(v, out_ref):
@@ -152,8 +168,8 @@
     return (top <= HIGH) & (jnp.min(totals) >= floor)
 
 
-def changed(before, change):
-    return before + change.astype(F32)
+def row_sums(first, *codes):
+    return first + sum(decode(code) for code in codes)
 
 
 def over_sources(log_targets, at_once, n_parts, *refs):
@@ -161,8 +177,7 @@
     e_ref, yt_ref, xa_ref, part_ref, sum_ref, pot_ref, acc_ref, yt_buf, xa_buf = refs
     n_tgt, n_src = e_ref.shape
     n_blocks = n_src // LANES
-    parts = [ref[...] for ref in parts_refs]
-    pot = log_targets - merge(parts[0] if n_parts == 1 else changed(*parts))
+    pot = log_targets - merge(row_sums(*[ref[...] for ref in parts_refs]))
     pot_ref[...] = pot
     u = jnp.exp2(jnp.minimum(pot, HIGH))
     u = [jnp.broadcast_to(u[b : b + 1], (8, LANES)) for b in range(n_blocks)]
@@ -184,6 +199,8 @@
 
     def put(value):
         copies, n, _ = part_ref.shape
+        if part_ref.dtype == BF16:
+            value = encode(value - math.log2(n_src))
         for k in range(copies):
             at = (k * n) % value.shape[0]
             part_ref[k] = value[at : at + n]
@@ -201,7 +218,7 @@
 def over_targets(log_sources, at_once, parts_ref, before_ref, e_ref, yt_ref, xa_ref, part_ref, sum_ref, pot_ref, yt_buf, xa_buf):
     n_tgt, n_src = e_ref.shape
     n_blocks = n_src // LANES
-    pot = log_sources - merge(parts_ref[...])
+    pot = log_sources - merge(math.log2(n_src) + decode(parts_ref[...]))
     spread_to_rows(jnp.exp2(jnp.minimum(pot, HIGH)), pot_ref)
 
     def one(jt, acc):
@@ -218,7 +235,7 @@
         sum_ref[b : b + 1, :] = jnp.sum(acc[b], axis=0, keepdims=True)
     totals = sum_ref[...]
     before = before_ref[0]
-    send((jnp.log2(totals) - before).astype(BF16), part_ref)
+    send(encode(jnp.log2(totals) - before), part_ref)
 
     @pl.when(jnp.logical_not(checked(totals, pot)))
     def _():
@@ -226,15 +243,11 @@
         pltpu.sync_copy(xa_ref, xa_buf)
         spread_to_rows(pot, pot_ref)
         slow_over_targets(yt_buf, xa_buf, pot_ref, sum_ref)
-        send((sum_ref[...] - before).astype(BF16), part_ref)
-
-
-def make_copies(x_ref, out_ref, sems):
-    copies = [pltpu.make_async_copy(x_ref, out_ref.at[k], sems.at[k]) for k in range(out_ref.shape[0])]
-    for copy in copies:
-        copy.start()
-    for copy in copies:
-        copy.wait()
+        send(encode(sum_ref[...] - before), part_ref)
+
+
+def make_copies(x_ref, out_ref):
+    send(x_ref[...], out_ref)
 
 
 def finish_targets(log_sources, parts_ref, out_ref):
@@ -265,13 +278,12 @@
 def call_copies(x, copies):
     return pl.pallas_call(
         make_copies,
-        out_shape=pltpu.HBM((copies,) + x.shape, x.dtype),
-        in_specs=[ANY],
-        out_specs=ANY,
-        scratch_shapes=[pltpu.SemaphoreType.DMA((copies,))],
+        out_shape=jax.ShapeDtypeStruct((copies,) + x.shape, x.dtype),
+        in_specs=[VMEM],
+        out_specs=VMEM,
         compiler_params=params(),
         name="make_copies",
-    )(pltpu.with_memory_space_constraint(x, pltpu.HBM))
+    )(x)
 
 
 def call_finish(log_sources, parts):
@@ -303,11 +315,11 @@
     )(yt, x)
 
 
-def call_over_sources(log_targets, e, yt, xa, part_shape, *parts, at_once=128):
+def call_over_sources(log_targets, e, yt, xa, part_shape, part_type, *parts, at_once=128):
     n_tgt, n_src = e.shape
     return pl.pallas_call(
         functools.partial(over_sources, log_targets, at_once, len(parts)),
-        out_shape=jax.ShapeDtypeStruct(part_shape, F32),
+        out_shape=jax.ShapeDtypeStruct(part_shape, part_type),
         in_specs=[VMEM] * len(parts) + [VMEM, ANY, ANY],
         out_specs=VMEM,
         scratch_shapes=[
@@ -355,11 +367,11 @@
     yt = call_prep(lax.all_gather(tgt_feat, "core"))
     e, xa, part = call_first(yt, x, n_z)
     first = exchange(part, "z")
-    col_part = call_over_sources(log_targets, e, yt, xa, (group, n_tgt // LANES, LANES), first)
+    col_part = call_over_sources(log_targets, e, yt, xa, (group, n_tgt // LANES, LANES), BF16, first)
     col_parts = exchange(col_part, ("row", "core"))
     change = exchange(call_over_targets(log_sources, col_parts, part, e, yt, xa, n_z), "z")
-    col_part = call_over_sources(log_targets, e, yt, xa, (group, tgt_own // LANES, LANES), first, change)
-    src_pot = FROM_LOG2 * (log_targets - merge(changed(first, change)))
+    col_part = call_over_sources(log_targets, e, yt, xa, (group, tgt_own // LANES, LANES), F32, first, change)
+    src_pot = FROM_LOG2 * (log_targets - merge(row_sums(first, change)))
     src_pot = lax.all_gather(src_pot, "core", axis=1)
     tgt_pot = call_finish(log_sources, exchange(col_part, ("row", "core")))
     return src_pot.reshape(n_core * n_z * src_own), tgt_pot.reshape(tgt_own)

time: 397 us -> 388 us (0.977)
  Pallas kernels: 297 us -> 289 us
    pallas_call x1, Pallas kernels: 9.18 us -> 0.74 us  [call_copies(): pl.pallas_call(make_copies, out_shape=jax.ShapeDtypeStruct((copies,) + x....]
where the time goes in v5:
time: 388 us
  Pallas kernels  289 us (74%)
  blocking collectives  60.5 us (16%)
  starting transfers between devices  21.4 us (6%)
  waiting for transfers between devices  15 us (4%)
    pallas_call x2, Pallas kernels, call_over_sources(): pl.pallas_call(functools.partial(over_sources, log_targets, at_once, len(...  179 us
    all_to_all x3, blocking collectives, exchange(): return lax.all_to_all(value, axis, 0, 0, tiled=False)  55.9 us
    pallas_call x1, Pallas kernels, call_first(): pl.pallas_call(functools.partial(first_over_targets, tile), out_shape=(pl...  54.5 us
    pallas_call x1, Pallas kernels, call_over_targets(): pl.pallas_call(functools.partial(over_targets, log_sources, at_once), out...  54.1 us
    all_to_all x2, starting transfers between devices, exchange(): return lax.all_to_all(value, axis, 0, 0, tiled=False)  21.4 us
    all_to_all x2, waiting for transfers between devices, exchange(): return lax.all_to_all(value, axis, 0, 0, tiled=False)  15 us
  transfers between devices with their start and end apart: 2, of which 2 were waited for; matrix products, arithmetic and copies ran while one was open for 0% of the time, Pallas kernels for 0%

profile of v5, /device:TPU:1, one launch (start us, length us, event | category | flops | bytes accessed | tf_op | source)
XLA Modules:
  0.0 388.0 jit_solution(13216536031063186140)
XLA Ops:
  0.6 0.0 copy-start
  0.6 0.7 copy-done
  1.3 0.7 make_copies.1
  2.1 15.7 %all-to-all-start = ((bf16[16,64,128]{2,1,0:T(8,128)(2,1)}), bf16[16,64,128]{2,1,0:T(8,128)(2,1)S(1)}, u32[]{:S(2)}, u32[]{:S(2)}) async-start(bf16[16,64,128]{2,1,0:T(8,128)(2,1)} %make_copies.1), calls=%async_computation | async-start | bytes 524288 | tf_op jit(solution)/shard_map/all_to_all | solution.py:356
  17.8 2.8 all-gather
  20.6 0.4 prep_targets.1.yt_ref.refs_2_.refs_3_
  21.0 10.0 %all-to-all-done.x_ref = bf16[16,64,128]{2,1,0:T(8,128)(2,1)S(1)} async-done(((bf16[16,64,128]{2,1,0:T(8,128)(2,1)}), bf16[16,64,128]{2,1,0:T(8,128)(2,1)S(1)}, u32[]{:S(2)}, u32[]{:S(2)}) %all-to-all-start) | async-done | bytes 262176 | tf_op jit(solution)/shard_map/all_to_all | solution.py:356
  31.0 54.5 %first_over_targets.1 = (f32[2048,2048]{1,0:T(8,128)S(1)}, bf16[256,2048]{1,0:T(8,128)(2,1)S(1)}, f32[16,16,128]{2,1,0:T(8,128)S(1)}) custom-call(bf16[2048,256]{1,0:T(8,128)(2,1)S(1)} %prep_targets.1.yt_ref.refs_2_.refs_3_, bf16[16,64,128]{2,1,0:T(8,128)(2,1)S(1)} %all-to-all-done.x_ref), custom_call_target="tpu_custom_call" | custom-call | tf_op jit(solution)/shard_map/first_over_targets/pallas_call | solution.py:303
  85.5 22.7 %all_to_all.25.refs_0_ = f32[16,16,128]{2,1,0:T(8,128)S(1)} all-to-all(f32[16,16,128]{2,1,0:T(8,128)S(1)} %get-tuple-element.5.before_ref), channel_id=1, replica_groups=mesh['row'=16,'z'=16,'core'=2] {'z'}, dimensions={0} | all-to-all | bytes 262144 | tf_op jit(solution)/shard_map/all_to_all | solution.py:356
  108.2 88.9 %over_sources.2 = bf16[32,16,128]{2,1,0:T(8,128)(2,1)S(1)} custom-call(f32[16,16,128]{2,1,0:T(8,128)S(1)} %all_to_all.25.refs_0_, f32[2048,2048]{1,0:T(8,128)S(1)} %get-tuple-element.6.refs_1_.e_ref.refs_2_, bf16[2048,256]{1,0:T(8,128)(2,1)S(1)} %prep_targets.1.yt_ref.refs_2_.refs_3_, bf16[256,2048]{1,0:T(8,128)(2,1)S(1)} %get-tuple-element.7.refs_3_.xa_ref.refs_4_), custom_call_target="tpu_custom_call" | custom-call | tf_op jit(solution)/shard_map/over_sources/pallas_call | solution.py:320
  197.1 18.3 %all_to_all.26.parts_ref = bf16[32,16,128]{2,1,0:T(8,128)(2,1)S(1)} all-to-all(bf16[32,16,128]{2,1,0:T(8,128)(2,1)S(1)} %over_sources.2), channel_id=1, replica_groups=mesh['row'=16,'z'=16,'core'=2] {'row','core'}, dimensions={0} | all-to-all | bytes 262144 | tf_op jit(solution)/shard_map/all_to_all | solution.py:356
  215.4 54.1 %over_targets.1 = bf16[16,16,128]{2,1,0:T(8,128)(2,1)S(1)} custom-call(bf16[32,16,128]{2,1,0:T(8,128)(2,1)S(1)} %all_to_all.26.parts_ref, f32[16,16,128]{2,1,0:T(8,128)S(1)} %get-tuple-element.5.before_ref, f32[2048,2048]{1,0:T(8,128)S(1)} %get-tuple-element.6.refs_1_.e_ref.refs_2_, bf16[2048,256]{1,0:T(8,128)(2,1)S(1)} %prep_targets.1.yt_ref.refs_2_.refs_3_, ...), custom_call_target="tpu_custom_call" | custom-call | tf_op jit(solution)/shard_map/over_targets/pallas_call | solution.py:339
  269.5 14.9 %all_to_all.27.refs_1_ = bf16[16,16,128]{2,1,0:T(8,128)(2,1)S(1)} all-to-all(bf16[16,16,128]{2,1,0:T(8,128)(2,1)S(1)} %over_targets.1), channel_id=1, replica_groups=mesh['row'=16,'z'=16,'core'=2] {'z'}, dimensions={0} | all-to-all | bytes 131072 | tf_op jit(solution)/shard_map/all_to_all | solution.py:356
  284.3 89.6 %over_sources.3 = f32[32,8,128]{2,1,0:T(8,128)} custom-call(f32[16,16,128]{2,1,0:T(8,128)S(1)} %all_to_all.25.refs_0_, bf16[16,16,128]{2,1,0:T(8,128)(2,1)S(1)} %all_to_all.27.refs_1_, f32[2048,2048]{1,0:T(8,128)S(1)} %get-tuple-element.6.refs_1_.e_ref.refs_2_, bf16[2048,256]{1,0:T(8,128)(2,1)S(1)} %prep_targets.1.yt_ref.refs_2_.refs_3_, ...), custom_call_target="tpu_custom_call" | custom-call | tf_op jit(solution)/shard_map/over_sources/pallas_call | solution.py:320
  374.0 5.6 %all-to-all-start.4 = ((f32[32,8,128]{2,1,0:T(8,128)}), f32[32,8,128]{2,1,0:T(8,128)S(1)}, u32[]{:S(2)}, u32[]{:S(2)}) async-start(f32[32,8,128]{2,1,0:T(8,128)} %over_sources.3), calls=%async_computation.4 | async-start | bytes 262144 | tf_op jit(solution)/shard_map/all_to_all | solution.py:356
  379.6 0.1 fusion.9
  379.7 0.1 exponential_reduce_fusion
  379.8 1.8 all-gather.1
  381.7 0.6 copy.4
  382.3 5.1 %all-to-all-done.4.parts_ref = f32[32,8,128]{2,1,0:T(8,128)S(1)} async-done(((f32[32,8,128]{2,1,0:T(8,128)}), f32[32,8,128]{2,1,0:T(8,128)S(1)}, u32[]{:S(2)}, u32[]{:S(2)}) %all-to-all-start.4) | async-done | bytes 131104 | tf_op jit(solution)/shard_map/all_to_all | solution.py:356
  387.3 0.7 finish_targets.1
  (1 shorter events, 0.0 us)
Async XLA Ops:
  0.6 0.7 copy-start
  2.1 28.9 %all-to-all-start = ((bf16[16,64,128]{2,1,0:T(8,128)(2,1)}), bf16[16,64,128]{2,1,0:T(8,128)(2,1)S(1)}, u32[]{:S(2)}, u32[]{:S(2)}) async-start(bf16[16,64,128]{2,1,0:T(8,128)(2,1)} %make_copies.1), calls=%async_computation | async-start | bytes 524288 | tf_op jit(solution)/shard_map/all_to_all | solution.py:356
  374.0 13.4 %all-to-all-start.4 = ((f32[32,8,128]{2,1,0:T(8,128)}), f32[32,8,128]{2,1,0:T(8,128)S(1)}, u32[]{:S(2)}, u32[]{:S(2)}) async-start(f32[32,8,128]{2,1,0:T(8,128)} %over_sources.3), calls=%async_computation.4 | async-start | bytes 262144 | tf_op jit(solution)/shard_map/all_to_all | solution.py:356

commit v6 on v5

--- a/solution.py
+++ b/solution.py
@@ -16,7 +16,7 @@
 FROM_LOG2 = EPS * math.log(2.0)
 LOW, HIGH = -91.0, 100.0
 F32, BF16 = jnp.float32, jnp.bfloat16
-POWER, SHIFT, SMALL = 11.0, -22.0, 2.0**-9
+ABOVE, BELOW, SHIFT, SMALL = 14.0, 4.0, -57.0, 2.0**-17
 
 
 def split3(v):
@@ -58,7 +58,8 @@
 
 def encode(d):
     size = jnp.abs(d)
-    t = jnp.exp2(POWER * jnp.log2(jnp.maximum(size, SMALL)) + SHIFT)
+    log = jnp.log2(jnp.maximum(size, SMALL))
+    t = jnp.exp2(log * jnp.where(log > 0.0, ABOVE, BELOW) + SHIFT)
     t = jnp.where(size < SMALL, 0.0, t)
     return jnp.where(d < 0.0, -t, t).astype(BF16)
 
@@ -66,9 +67,29 @@
 def decode(code):
     t = code.astype(F32)
     size = jnp.abs(t)
-    d = jnp.exp2((jnp.log2(jnp.maximum(size, 2.0**-126)) - SHIFT) * (1.0 / POWER))
+    log = jnp.log2(jnp.maximum(size, 2.0**-126)) - SHIFT
+    d = jnp.exp2(log * jnp.where(log > 0.0, 1.0 / ABOVE, 1.0 / BELOW))
     d = jnp.where(size > 0.0, d, 0.0)
     return jnp.where(t < 0.0, -d, d)
+
+
+def base_of(d, around):
+    a, b, c = (d[..., :1, k : k + 1] + around for k in range(3))
+    base = jnp.maximum(jnp.minimum(a, b), jnp.minimum(jnp.maximum(a, b), c))
+    at = [lax.broadcasted_iota(jnp.int32, d.shape, d.ndim - k) for k in (2, 1)]
+    return base, (at[0] == 0) & (at[1] < 3)
+
+
+def encode_from_base(value, around):
+    head = encode(value - around)
+    base, first = base_of(decode(head), around)
+    return jnp.where(first, head.astype(F32), encode(value - base).astype(F32)).astype(BF16)
+
+
+def decode_from_base(code, around):
+    d = decode(code)
+    base, first = base_of(d, around)
+    return jnp.where(first, around, base) + d
 
 
 def spread_to_rows(v, out_ref):
@@ -153,13 +174,13 @@
     for b in range(n_blocks):
         sum_ref[b : b + 1, :] = total[:, b * LANES : (b + 1) * LANES]
     totals = sum_ref[...]
-    send(jnp.log2(totals), part_ref)
+    send(encode_from_base(jnp.log2(totals), math.log2(n_tgt)), part_ref)
     fast = (jnp.min(totals) >= 2.0**LOW) & (jnp.max(totals) <= 2.0**HIGH)
 
     @pl.when(jnp.logical_not(fast))
     def _():
         slow_over_targets(yt_ref, xa_ref, None, sum_ref)
-        send(sum_ref[...], part_ref)
+        send(encode_from_base(sum_ref[...], math.log2(n_tgt)), part_ref)
 
 
 def checked(totals, pot):
@@ -168,8 +189,8 @@
     return (top <= HIGH) & (jnp.min(totals) >= floor)
 
 
-def row_sums(first, *codes):
-    return first + sum(decode(code) for code in codes)
+def row_sums(n_tgt, first, *changes):
+    return decode_from_base(first, math.log2(n_tgt)) + sum(decode(change) for change in changes)
 
 
 def over_sources(log_targets, at_once, n_parts, *refs):
@@ -177,7 +198,7 @@
     e_ref, yt_ref, xa_ref, part_ref, sum_ref, pot_ref, acc_ref, yt_buf, xa_buf = refs
     n_tgt, n_src = e_ref.shape
     n_blocks = n_src // LANES
-    pot = log_targets - merge(row_sums(*[ref[...] for ref in parts_refs]))
+    pot = log_targets - merge(row_sums(n_tgt, *[ref[...] for ref in parts_refs]))
     pot_ref[...] = pot
     u = jnp.exp2(jnp.minimum(pot, HIGH))
     u = [jnp.broadcast_to(u[b : b + 1], (8, LANES)) for b in range(n_blocks)]
@@ -234,7 +255,7 @@
     for b in range(n_blocks):
         sum_ref[b : b + 1, :] = jnp.sum(acc[b], axis=0, keepdims=True)
     totals = sum_ref[...]
-    before = before_ref[0]
+    before = row_sums(n_tgt, before_ref[0])
     send(encode(jnp.log2(totals) - before), part_ref)
 
     @pl.when(jnp.logical_not(checked(totals, pot)))
@@ -305,7 +326,7 @@
         out_shape=(
             pltpu.VMEM((n_tgt, n_src), F32),
             jax.ShapeDtypeStruct((4 * width, n_src), BF16),
-            jax.ShapeDtypeStruct((copies, n_blocks, lanes), F32),
+            jax.ShapeDtypeStruct((copies, n_blocks, lanes), BF16),
         ),
         in_specs=[VMEM, VMEM],
         out_specs=(VMEM, VMEM, VMEM),
@@ -371,7 +392,7 @@
     col_parts = exchange(col_part, ("row", "core"))
     change = exchange(call_over_targets(log_sources, col_parts, part, e, yt, xa, n_z), "z")
     col_part = call_over_sources(log_targets, e, yt, xa, (group, tgt_own // LANES, LANES), F32, first, change)
-    src_pot = FROM_LOG2 * (log_targets - merge(row_sums(first, change)))
+    src_pot = FROM_LOG2 * (log_targets - merge(row_sums(n_tgt, first, change)))
     src_pot = lax.all_gather(src_pot, "core", axis=1)
     tgt_pot = call_finish(log_sources, exchange(col_part, ("row", "core")))
     return src_pot.reshape(n_core * n_z * src_own), tgt_pot.reshape(tgt_own)

time: 388 us -> 406 us (1.046)
  blocking collectives: 60.5 us -> 27 us
  waiting for transfers between devices: 15 us -> 33.9 us
  local copies, waits for them, and re-layouts: 1.32 us -> 18.6 us
  starting transfers between devices: 21.4 us -> 34.1 us
    all_to_all x3 -> x1, blocking collectives: 55.9 us -> 22.3 us  [exchange(): return lax.all_to_all(value, axis, 0, 0, tiled=False)]
    all_to_all x2 -> x4, waiting for transfers between devices: 15 us -> 33.9 us  [exchange(): return lax.all_to_all(value, axis, 0, 0, tiled=False)]
    unnamed x3 -> x9, local copies, waits for them, and re-layouts: 1.32 us -> 18.6 us
    all_to_all x2 -> x4, starting transfers between devices: 21.4 us -> 34.1 us  [exchange(): return lax.all_to_all(value, axis, 0, 0, tiled=False)]
  transfers between devices with their start and end apart: 2 -> 4, of which waited for: 2 -> 4; matrix products, arithmetic and copies ran while one was open for 0% -> 0% of each run, Pallas kernels for 0% -> 0%
where the time goes in v6:
time: 406 us; the launch traced here: 405 us
  Pallas kernels  291 us (72%)
  starting transfers between devices  34.1 us (8%)
  waiting for transfers between devices  33.9 us (8%)
  blocking collectives  27 us (7%)
  local copies, waits for them, and re-layouts  18.6 us (5%)
    pallas_call x2, Pallas kernels, call_over_sources(): pl.pallas_call(functools.partial(over_sources, log_targets, at_once, len(...  179 us
    pallas_call x1, Pallas kernels, call_over_targets(): pl.pallas_call(functools.partial(over_targets, log_sources, at_once), out...  54.7 us
    pallas_call x1, Pallas kernels, call_first(): pl.pallas_call(functools.partial(first_over_targets, tile), out_shape=(pl...  54.7 us
    all_to_all x4, starting transfers between devices, exchange(): return lax.all_to_all(value, axis, 0, 0, tiled=False)  34.1 us
    all_to_all x4, waiting for transfers between devices, exchange(): return lax.all_to_all(value, axis, 0, 0, tiled=False)  33.9 us
    all_to_all x1, blocking collectives, exchange(): return lax.all_to_all(value, axis, 0, 0, tiled=False)  22.3 us
    unnamed x9, local copies, waits for them, and re-layouts  18.6 us
  transfers between devices with their start and end apart: 4, of which 4 were waited for; matrix products, arithmetic and copies ran while one was open for 0% of the time, Pallas kernels for 0%

profile of v6, /device:TPU:1, one launch (start us, length us, event | category | flops | bytes accessed | tf_op | source)
XLA Modules:
  0.0 405.5 jit_solution(11546162761779620535)
XLA Ops:
  0.6 0.7 copy-done.3
  1.3 0.8 make_copies.1
  2.1 15.7 %all-to-all-start = ((bf16[16,64,128]{2,1,0:T(8,128)(2,1)}), bf16[16,64,128]{2,1,0:T(8,128)(2,1)S(1)}, u32[]{:S(2)}, u32[]{:S(2)}) async-start(bf16[16,64,128]{2,1,0:T(8,128)(2,1)} %make_copies.1), calls=%async_computation | async-start | bytes 524288 | tf_op jit(solution)/shard_map/all_to_all | solution.py:377
  17.9 2.8 all-gather
  20.6 0.4 prep_targets.1.yt_ref.refs_2_.refs_3_
  21.0 10.0 %all-to-all-done.x_ref = bf16[16,64,128]{2,1,0:T(8,128)(2,1)S(1)} async-done(((bf16[16,64,128]{2,1,0:T(8,128)(2,1)}), bf16[16,64,128]{2,1,0:T(8,128)(2,1)S(1)}, u32[]{:S(2)}, u32[]{:S(2)}) %all-to-all-start) | async-done | bytes 262176 | tf_op jit(solution)/shard_map/all_to_all | solution.py:377
  31.0 54.7 %first_over_targets.1 = (f32[2048,2048]{1,0:T(8,128)S(1)}, bf16[256,2048]{1,0:T(8,128)(2,1)S(1)}, bf16[16,16,128]{2,1,0:T(8,128)(2,1)S(1)}) custom-call(bf16[2048,256]{1,0:T(8,128)(2,1)S(1)} %prep_targets.1.yt_ref.refs_2_.refs_3_, bf16[16,64,128]{2,1,0:T(8,128)(2,1)S(1)} %all-to-all-done.x_ref), custom_call_target="tpu_custom_call" | custom-call | tf_op jit(solution)/shard_map/first_over_targets/pallas_call | solution.py:324
  85.7 22.3 %all_to_all.25.refs_0_ = bf16[16,16,128]{2,1,0:T(8,128)(2,1)S(1)} all-to-all(bf16[16,16,128]{2,1,0:T(8,128)(2,1)S(1)} %get-tuple-element.5.before_ref), channel_id=1, replica_groups=mesh['row'=16,'z'=16,'core'=2] {'z'}, dimensions={0} | all-to-all | bytes 131072 | tf_op jit(solution)/shard_map/all_to_all | solution.py:377
  108.0 89.7 %over_sources.2 = bf16[32,16,128]{2,1,0:T(8,128)(2,1)} custom-call(bf16[16,16,128]{2,1,0:T(8,128)(2,1)S(1)} %all_to_all.25.refs_0_, f32[2048,2048]{1,0:T(8,128)S(1)} %get-tuple-element.6.refs_1_.e_ref.refs_2_, bf16[2048,256]{1,0:T(8,128)(2,1)S(1)} %prep_targets.1.yt_ref.refs_2_.refs_3_, bf16[256,2048]{1,0:T(8,128)(2,1)S(1)} %get-tuple-element.7.refs_3_.xa_ref.refs_4_), custom_call_target="tpu_custom_call" | custom-call | tf_op jit(solution)/shard_map/over_sources/pallas_call | solution.py:341
  197.7 5.7 %copy-done = f32[2048,2048]{1,0:T(8,128)} copy-done((f32[2048,2048]{1,0:T(8,128)}, f32[2048,2048]{1,0:T(8,128)S(1)}, u32[]{:S(2)}) %copy-start) | copy-done | bytes 16777240
  203.5 9.3 %all-to-all-start.2 = ((bf16[32,16,128]{2,1,0:T(8,128)(2,1)}), bf16[32,16,128]{2,1,0:T(8,128)(2,1)S(1)}, u32[]{:S(2)}, u32[]{:S(2)}) async-start(bf16[32,16,128]{2,1,0:T(8,128)(2,1)} %over_sources.2), calls=%async_computation.2 | async-start | bytes 262144 | tf_op jit(solution)/shard_map/all_to_all | solution.py:377
  212.8 7.6 %all-to-all-done.2.parts_ref = bf16[32,16,128]{2,1,0:T(8,128)(2,1)S(1)} async-done(((bf16[32,16,128]{2,1,0:T(8,128)(2,1)}), bf16[32,16,128]{2,1,0:T(8,128)(2,1)S(1)}, u32[]{:S(2)}, u32[]{:S(2)}) %all-to-all-start.2) | async-done | bytes 131104 | tf_op jit(solution)/shard_map/all_to_all | solution.py:377
  220.4 5.8 %copy-done.1 = f32[2048,2048]{1,0:T(8,128)S(1)} copy-done((f32[2048,2048]{1,0:T(8,128)S(1)}, f32[2048,2048]{1,0:T(8,128)}, u32[]{:S(2)}) %copy-start.1) | copy-done | bytes 16777240
  226.1 54.7 %over_targets.1 = bf16[16,16,128]{2,1,0:T(8,128)(2,1)} custom-call(bf16[32,16,128]{2,1,0:T(8,128)(2,1)S(1)} %all-to-all-done.2.parts_ref, bf16[16,16,128]{2,1,0:T(8,128)(2,1)S(1)} %get-tuple-element.5.before_ref, f32[2048,2048]{1,0:T(8,128)S(1)} %copy-done.1, bf16[2048,256]{1,0:T(8,128)(2,1)S(1)} %prep_targets.1.yt_ref.refs_2_.refs_3_, ...), custom_call_target="tpu_custom_call" | custom-call | tf_op jit(solution)/shard_map/over_targets/pallas_call | solution.py:360
  280.9 3.5 all-to-all-start.3
  284.5 0.3 fusion.13
  284.8 11.2 %all-to-all-done.3.refs_1_ = bf16[16,16,128]{2,1,0:T(8,128)(2,1)S(1)} async-done(((bf16[16,16,128]{2,1,0:T(8,128)(2,1)}), bf16[16,16,128]{2,1,0:T(8,128)(2,1)S(1)}, u32[]{:S(2)}, u32[]{:S(2)}) %all-to-all-start.3) | async-done | bytes 65568 | tf_op jit(solution)/shard_map/all_to_all | solution.py:377
  296.0 5.8 %copy-done.2 = f32[2048,2048]{1,0:T(8,128)S(1)} copy-done((f32[2048,2048]{1,0:T(8,128)S(1)}, f32[2048,2048]{1,0:T(8,128)}, u32[]{:S(2)}) %copy-start.2) | copy-done | bytes 16777240
  301.8 89.7 %over_sources.3 = f32[32,8,128]{2,1,0:T(8,128)} custom-call(bf16[16,16,128]{2,1,0:T(8,128)(2,1)S(1)} %all_to_all.25.refs_0_, bf16[16,16,128]{2,1,0:T(8,128)(2,1)S(1)} %all-to-all-done.3.refs_1_, f32[2048,2048]{1,0:T(8,128)S(1)} %copy-done.2, bf16[2048,256]{1,0:T(8,128)(2,1)S(1)} %prep_targets.1.yt_ref.refs_2_.refs_3_, ...), custom_call_target="tpu_custom_call" | custom-call | tf_op jit(solution)/shard_map/over_sources/pallas_call | solution.py:341
  391.6 5.5 %all-to-all-start.4 = ((f32[32,8,128]{2,1,0:T(8,128)}), f32[32,8,128]{2,1,0:T(8,128)S(1)}, u32[]{:S(2)}, u32[]{:S(2)}) async-start(f32[32,8,128]{2,1,0:T(8,128)} %over_sources.3), calls=%async_computation.4 | async-start | bytes 262144 | tf_op jit(solution)/shard_map/all_to_all | solution.py:377
  397.4 1.8 all-gather.1
  399.2 0.6 copy.7
  399.8 5.0 %all-to-all-done.4.parts_ref = f32[32,8,128]{2,1,0:T(8,128)S(1)} async-done(((f32[32,8,128]{2,1,0:T(8,128)}), f32[32,8,128]{2,1,0:T(8,128)S(1)}, u32[]{:S(2)}, u32[]{:S(2)}) %all-to-all-start.4) | async-done | bytes 131104 | tf_op jit(solution)/shard_map/all_to_all | solution.py:377
  404.8 0.7 finish_targets.1
  (10 shorter events, 0.3 us)
Async XLA Ops:
  0.6 0.7 copy-start.3
  2.1 28.9 %all-to-all-start = ((bf16[16,64,128]{2,1,0:T(8,128)(2,1)}), bf16[16,64,128]{2,1,0:T(8,128)(2,1)S(1)}, u32[]{:S(2)}, u32[]{:S(2)}) async-start(bf16[16,64,128]{2,1,0:T(8,128)(2,1)} %make_copies.1), calls=%async_computation | async-start | bytes 524288 | tf_op jit(solution)/shard_map/all_to_all | solution.py:377
  197.7 5.7 %copy-start = (f32[2048,2048]{1,0:T(8,128)}, f32[2048,2048]{1,0:T(8,128)S(1)}, u32[]{:S(2)}) copy-start(f32[2048,2048]{1,0:T(8,128)S(1)} %get-tuple-element.6.refs_1_.e_ref.refs_2_) | copy-start | bytes 50331652
  203.5 16.9 %all-to-all-start.2 = ((bf16[32,16,128]{2,1,0:T(8,128)(2,1)}), bf16[32,16,128]{2,1,0:T(8,128)(2,1)S(1)}, u32[]{:S(2)}, u32[]{:S(2)}) async-start(bf16[32,16,128]{2,1,0:T(8,128)(2,1)} %over_sources.2), calls=%async_computation.2 | async-start | bytes 262144 | tf_op jit(solution)/shard_map/all_to_all | solution.py:377
  220.4 5.8 %copy-start.1 = (f32[2048,2048]{1,0:T(8,128)S(1)}, f32[2048,2048]{1,0:T(8,128)}, u32[]{:S(2)}) copy-start(f32[2048,2048]{1,0:T(8,128)} %copy-done) | copy-start | bytes 50331652
  280.9 15.1 %all-to-all-start.3 = ((bf16[16,16,128]{2,1,0:T(8,128)(2,1)}), bf16[16,16,128]{2,1,0:T(8,128)(2,1)S(1)}, u32[]{:S(2)}, u32[]{:S(2)}) async-start(bf16[16,16,128]{2,1,0:T(8,128)(2,1)} %over_targets.1), calls=%async_computation.3 | async-start | bytes 131072 | tf_op jit(solution)/shard_map/all_to_all | solution.py:377
  296.0 5.8 %copy-start.2 = (f32[2048,2048]{1,0:T(8,128)S(1)}, f32[2048,2048]{1,0:T(8,128)}, u32[]{:S(2)}) copy-start(f32[2048,2048]{1,0:T(8,128)} %copy-done) | copy-start | bytes 50331652
  391.6 13.3 %all-to-all-start.4 = ((f32[32,8,128]{2,1,0:T(8,128)}), f32[32,8,128]{2,1,0:T(8,128)S(1)}, u32[]{:S(2)}, u32[]{:S(2)}) async-start(f32[32,8,128]{2,1,0:T(8,128)} %over_sources.3), calls=%async_computation.4 | async-start | bytes 262144 | tf_op jit(solution)/shard_map/all_to_all | solution.py:377

commit v7 on v6

--- a/solution.py
+++ b/solution.py
@@ -271,6 +271,10 @@
     send(x_ref[...], out_ref)
 
 
+def finish_sources(log_targets, n_tgt, first_ref, change_ref, out_ref):
+    out_ref[...] = FROM_LOG2 * (log_targets - merge(row_sums(n_tgt, first_ref[...], change_ref[...])))
+
+
 def finish_targets(log_sources, parts_ref, out_ref):
     out_ref[...] = FROM_LOG2 * (log_sources - merge(parts_ref[...]))
 
@@ -305,6 +309,17 @@
         compiler_params=params(),
         name="make_copies",
     )(x)
+
+
+def call_finish_sources(log_targets, n_tgt, first, change):
+    return pl.pallas_call(
+        functools.partial(finish_sources, log_targets, n_tgt),
+        out_shape=jax.ShapeDtypeStruct(first.shape[1:], F32),
+        in_specs=[VMEM, VMEM],
+        out_specs=VMEM,
+        compiler_params=params(),
+        name="finish_sources",
+    )(first, change)
 
 
 def call_finish(log_sources, parts):
@@ -392,7 +407,7 @@
     col_parts = exchange(col_part, ("row", "core"))
     change = exchange(call_over_targets(log_sources, col_parts, part, e, yt, xa, n_z), "z")
     col_part = call_over_sources(log_targets, e, yt, xa, (group, tgt_own // LANES, LANES), F32, first, change)
-    src_pot = FROM_LOG2 * (log_targets - merge(row_sums(n_tgt, first, change)))
+    src_pot = call_finish_sources(log_targets, n_tgt, first, change)
     src_pot = lax.all_gather(src_pot, "core", axis=1)
     tgt_pot = call_finish(log_sources, exchange(col_part, ("row", "core")))
     return src_pot.reshape(n_core * n_z * src_own), tgt_pot.reshape(tgt_own)

time: 406 us -> 386 us (0.951)
  blocking collectives: 27 us -> 58 us
  waiting for transfers between devices: 33.9 us -> 15 us
  local copies, waits for them, and re-layouts: 18.6 us -> 1.32 us
  starting transfers between devices: 34.1 us -> 21.1 us
    all_to_all x1 -> x3, blocking collectives: 22.3 us -> 53.3 us  [exchange(): return lax.all_to_all(value, axis, 0, 0, tiled=False)]
    all_to_all x4 -> x2, waiting for transfers between devices: 33.9 us -> 15 us  [exchange(): return lax.all_to_all(value, axis, 0, 0, tiled=False)]
    unnamed x9 -> x3, local copies, waits for them, and re-layouts: 18.6 us -> 1.32 us
    all_to_all x4 -> x2, starting transfers between devices: 34.1 us -> 21.1 us  [exchange(): return lax.all_to_all(value, axis, 0, 0, tiled=False)]
  transfers between devices with their start and end apart: 4 -> 2, of which waited for: 4 -> 2; matrix products, arithmetic and copies ran while one was open for 0% -> 0% of each run, Pallas kernels for 0% -> 0%
where the time goes in v7:
time: 386 us
  Pallas kernels  290 us (75%)
  blocking collectives  58 us (15%)
  starting transfers between devices  21.1 us (5%)
  waiting for transfers between devices  15 us (4%)
    pallas_call x2, Pallas kernels, call_over_sources(): pl.pallas_call(functools.partial(over_sources, log_targets, at_once, len(...  179 us
    pallas_call x1, Pallas kernels, call_first(): pl.pallas_call(functools.partial(first_over_targets, tile), out_shape=(pl...  54.7 us
    pallas_call x1, Pallas kernels, call_over_targets(): pl.pallas_call(functools.partial(over_targets, log_sources, at_once), out...  54.1 us
    all_to_all x3, blocking collectives, exchange(): return lax.all_to_all(value, axis, 0, 0, tiled=False)  53.3 us
    all_to_all x2, starting transfers between devices, exchange(): return lax.all_to_all(value, axis, 0, 0, tiled=False)  21.1 us
    all_to_all x2, waiting for transfers between devices, exchange(): return lax.all_to_all(value, axis, 0, 0, tiled=False)  15 us
  transfers between devices with their start and end apart: 2, of which 2 were waited for; matrix products, arithmetic and copies ran while one was open for 0% of the time, Pallas kernels for 0%

profile of v7, /device:TPU:1, one launch (start us, length us, event | category | flops | bytes accessed | tf_op | source)
XLA Modules:
  0.0 385.8 jit_solution(1569788765535921739)
XLA Ops:
  0.6 0.0 copy-start
  0.6 0.7 copy-done
  1.3 0.8 make_copies.1
  2.1 15.7 %all-to-all-start = ((bf16[16,64,128]{2,1,0:T(8,128)(2,1)}), bf16[16,64,128]{2,1,0:T(8,128)(2,1)S(1)}, u32[]{:S(2)}, u32[]{:S(2)}) async-start(bf16[16,64,128]{2,1,0:T(8,128)(2,1)} %make_copies.1), calls=%async_computation | async-start | bytes 524288 | tf_op jit(solution)/shard_map/all_to_all | solution.py:392
  17.9 2.8 all-gather
  20.6 0.4 prep_targets.1.yt_ref.refs_2_.refs_3_
  21.0 10.0 %all-to-all-done.x_ref = bf16[16,64,128]{2,1,0:T(8,128)(2,1)S(1)} async-done(((bf16[16,64,128]{2,1,0:T(8,128)(2,1)}), bf16[16,64,128]{2,1,0:T(8,128)(2,1)S(1)}, u32[]{:S(2)}, u32[]{:S(2)}) %all-to-all-start) | async-done | bytes 262176 | tf_op jit(solution)/shard_map/all_to_all | solution.py:392
  31.0 54.7 %first_over_targets.1 = (f32[2048,2048]{1,0:T(8,128)S(1)}, bf16[256,2048]{1,0:T(8,128)(2,1)S(1)}, bf16[16,16,128]{2,1,0:T(8,128)(2,1)S(1)}) custom-call(bf16[2048,256]{1,0:T(8,128)(2,1)S(1)} %prep_targets.1.yt_ref.refs_2_.refs_3_, bf16[16,64,128]{2,1,0:T(8,128)(2,1)S(1)} %all-to-all-done.x_ref), custom_call_target="tpu_custom_call" | custom-call | tf_op jit(solution)/shard_map/first_over_targets/pallas_call | solution.py:339
  85.7 22.3 %all_to_all.25.refs_0_.first_ref = bf16[16,16,128]{2,1,0:T(8,128)(2,1)S(1)} all-to-all(bf16[16,16,128]{2,1,0:T(8,128)(2,1)S(1)} %get-tuple-element.5.before_ref), channel_id=1, replica_groups=mesh['row'=16,'z'=16,'core'=2] {'z'}, dimensions={0} | all-to-all | bytes 131072 | tf_op jit(solution)/shard_map/all_to_all | solution.py:392
  108.0 89.1 %over_sources.2 = bf16[32,16,128]{2,1,0:T(8,128)(2,1)S(1)} custom-call(bf16[16,16,128]{2,1,0:T(8,128)(2,1)S(1)} %all_to_all.25.refs_0_.first_ref, f32[2048,2048]{1,0:T(8,128)S(1)} %get-tuple-element.6.refs_1_.e_ref.refs_2_, bf16[2048,256]{1,0:T(8,128)(2,1)S(1)} %prep_targets.1.yt_ref.refs_2_.refs_3_, ...), custom_call_target="tpu_custom_call" | custom-call | tf_op jit(solution)/shard_map/over_sources/pallas_call | solution.py:356
  197.1 16.7 %all_to_all.26.parts_ref = bf16[32,16,128]{2,1,0:T(8,128)(2,1)S(1)} all-to-all(bf16[32,16,128]{2,1,0:T(8,128)(2,1)S(1)} %over_sources.2), channel_id=1, replica_groups=mesh['row'=16,'z'=16,'core'=2] {'row','core'}, dimensions={0} | all-to-all | bytes 262144 | tf_op jit(solution)/shard_map/all_to_all | solution.py:392
  213.8 54.1 %over_targets.1 = bf16[16,16,128]{2,1,0:T(8,128)(2,1)S(1)} custom-call(bf16[32,16,128]{2,1,0:T(8,128)(2,1)S(1)} %all_to_all.26.parts_ref, bf16[16,16,128]{2,1,0:T(8,128)(2,1)S(1)} %get-tuple-element.5.before_ref, f32[2048,2048]{1,0:T(8,128)S(1)} %get-tuple-element.6.refs_1_.e_ref.refs_2_, bf16[2048,256]{1,0:T(8,128)(2,1)S(1)} %prep_targets.1.yt_ref.refs_2_.refs_3_, ...), custom_call_target="tpu_custom_call" | custom-call | tf_op jit(solution)/shard_map/over_targets/pallas_call | solution.py:375
  267.9 14.3 %all_to_all.27.change_ref.refs_1_ = bf16[16,16,128]{2,1,0:T(8,128)(2,1)S(1)} all-to-all(bf16[16,16,128]{2,1,0:T(8,128)(2,1)S(1)} %over_targets.1), channel_id=1, replica_groups=mesh['row'=16,'z'=16,'core'=2] {'z'}, dimensions={0} | all-to-all | bytes 131072 | tf_op jit(solution)/shard_map/all_to_all | solution.py:392
  282.2 89.7 %over_sources.3 = f32[32,8,128]{2,1,0:T(8,128)} custom-call(bf16[16,16,128]{2,1,0:T(8,128)(2,1)S(1)} %all_to_all.25.refs_0_.first_ref, bf16[16,16,128]{2,1,0:T(8,128)(2,1)S(1)} %all_to_all.27.change_ref.refs_1_, f32[2048,2048]{1,0:T(8,128)S(1)} %get-tuple-element.6.refs_1_.e_ref.refs_2_, bf16[2048,256]{1,0:T(8,128)(2,1)S(1)} %prep_targets.1.yt_ref.refs_2_.refs_3_, ...), custom_call_target="tpu_custom_call" | custom-call | tf_op jit(solution)/shard_map/over_sources/pallas_call | solution.py:356
  372.0 5.4 %all-to-all-start.4 = ((f32[32,8,128]{2,1,0:T(8,128)}), f32[32,8,128]{2,1,0:T(8,128)S(1)}, u32[]{:S(2)}, u32[]{:S(2)}) async-start(f32[32,8,128]{2,1,0:T(8,128)} %over_sources.3), calls=%async_computation.4 | async-start | bytes 262144 | tf_op jit(solution)/shard_map/all_to_all | solution.py:392
  377.4 0.2 finish_sources.1
  377.6 1.8 all-gather.1
  379.5 0.6 copy.4
  380.1 5.0 %all-to-all-done.4.parts_ref = f32[32,8,128]{2,1,0:T(8,128)S(1)} async-done(((f32[32,8,128]{2,1,0:T(8,128)}), f32[32,8,128]{2,1,0:T(8,128)S(1)}, u32[]{:S(2)}, u32[]{:S(2)}) %all-to-all-start.4) | async-done | bytes 131104 | tf_op jit(solution)/shard_map/all_to_all | solution.py:392
  385.1 0.7 finish_targets.1
Async XLA Ops:
  0.6 0.7 copy-start
  2.1 28.9 %all-to-all-start = ((bf16[16,64,128]{2,1,0:T(8,128)(2,1)}), bf16[16,64,128]{2,1,0:T(8,128)(2,1)S(1)}, u32[]{:S(2)}, u32[]{:S(2)}) async-start(bf16[16,64,128]{2,1,0:T(8,128)(2,1)} %make_copies.1), calls=%async_computation | async-start | bytes 524288 | tf_op jit(solution)/shard_map/all_to_all | solution.py:392
  372.0 13.1 %all-to-all-start.4 = ((f32[32,8,128]{2,1,0:T(8,128)}), f32[32,8,128]{2,1,0:T(8,128)S(1)}, u32[]{:S(2)}, u32[]{:S(2)}) async-start(f32[32,8,128]{2,1,0:T(8,128)} %over_sources.3), calls=%async_computation.4 | async-start | bytes 262144 | tf_op jit(solution)/shard_map/all_to_all | solution.py:392

commit v8 on v7

--- a/solution.py
+++ b/solution.py
@@ -193,29 +193,23 @@
     return decode_from_base(first, math.log2(n_tgt)) + sum(decode(change) for change in changes)
 
 
-def over_sources(log_targets, at_once, n_parts, *refs):
+def over_sources(log_targets, n_parts, *refs):
     parts_refs, refs = refs[:n_parts], refs[n_parts:]
-    e_ref, yt_ref, xa_ref, part_ref, sum_ref, pot_ref, acc_ref, yt_buf, xa_buf = refs
+    e_ref, yt_ref, xa_ref, part_ref, sum_ref, pot_ref, yt_buf, xa_buf = refs
     n_tgt, n_src = e_ref.shape
     n_blocks = n_src // LANES
     pot = log_targets - merge(row_sums(n_tgt, *[ref[...] for ref in parts_refs]))
     pot_ref[...] = pot
     u = jnp.exp2(jnp.minimum(pot, HIGH))
     u = [jnp.broadcast_to(u[b : b + 1], (8, LANES)) for b in range(n_blocks)]
-
-    def one(jt, _):
-        for r in range(0, at_once, 8):
-            rows = pl.ds(pl.multiple_of(jt * at_once + r, 8), 8)
-            acc = e_ref[rows, :LANES] * u[0]
+    for k in range(n_tgt // LANES):
+        block = []
+        for r in range(k * LANES, (k + 1) * LANES, 8):
+            acc = e_ref[r : r + 8, :LANES] * u[0]
             for b in range(1, n_blocks):
-                acc = acc + e_ref[rows, b * LANES : (b + 1) * LANES] * u[b]
-            acc_ref[rows, :] = acc
-        return 0
-
-    lax.fori_loop(0, n_tgt // at_once, one, 0)
-    for k in range(n_tgt // LANES):
-        block = acc_ref[k * LANES : (k + 1) * LANES, :].T
-        sum_ref[k : k + 1, :] = jnp.sum(block, axis=0, keepdims=True)
+                acc = acc + e_ref[r : r + 8, b * LANES : (b + 1) * LANES] * u[b]
+            block.append(acc)
+        sum_ref[k : k + 1, :] = jnp.sum(jnp.concatenate(block, axis=0).T, axis=0, keepdims=True)
     totals = sum_ref[...]
 
     def put(value):
@@ -236,22 +230,18 @@
         put(sum_ref[...])
 
 
-def over_targets(log_sources, at_once, parts_ref, before_ref, e_ref, yt_ref, xa_ref, part_ref, sum_ref, pot_ref, yt_buf, xa_buf):
+def over_targets(log_sources, parts_ref, before_ref, e_ref, yt_ref, xa_ref, part_ref, sum_ref, pot_ref, yt_buf, xa_buf):
     n_tgt, n_src = e_ref.shape
     n_blocks = n_src // LANES
     pot = log_sources - merge(math.log2(n_src) + decode(parts_ref[...]))
-    spread_to_rows(jnp.exp2(jnp.minimum(pot, HIGH)), pot_ref)
-
-    def one(jt, acc):
-        acc = list(acc)
-        for r in range(0, at_once, 8):
-            rows = pl.ds(pl.multiple_of(jt * at_once + r, 8), 8)
-            v = pot_ref[rows, :]
+    u = jnp.exp2(jnp.minimum(pot, HIGH))
+    acc = [jnp.zeros((8, LANES), F32)] * n_blocks
+    for k in range(n_tgt // LANES):
+        v = jnp.broadcast_to(u[k : k + 1], (LANES, LANES)).T
+        for r in range(0, LANES, 8):
+            at = k * LANES + r
             for b in range(n_blocks):
-                acc[b] = acc[b] + e_ref[rows, b * LANES : (b + 1) * LANES] * v
-        return tuple(acc)
-
-    acc = lax.fori_loop(0, n_tgt // at_once, one, (jnp.zeros((8, LANES), F32),) * n_blocks)
+                acc[b] = acc[b] + e_ref[at : at + 8, b * LANES : (b + 1) * LANES] * v[r : r + 8]
     for b in range(n_blocks):
         sum_ref[b : b + 1, :] = jnp.sum(acc[b], axis=0, keepdims=True)
     totals = sum_ref[...]
@@ -267,8 +257,13 @@
         send(encode(sum_ref[...] - before), part_ref)
 
 
-def make_copies(x_ref, out_ref):
-    send(x_ref[...], out_ref)
+def make_copies(x_ref, out_ref, buf, sems):
+    pltpu.sync_copy(x_ref, buf)
+    copies = [pltpu.make_async_copy(buf, out_ref.at[k], sems.at[k]) for k in range(out_ref.shape[0])]
+    for copy in copies:
+        copy.start()
+    for copy in copies:
+        copy.wait()
 
 
 def finish_sources(log_targets, n_tgt, first_ref, change_ref, out_ref):
@@ -303,12 +298,13 @@
 def call_copies(x, copies):
     return pl.pallas_call(
         make_copies,
-        out_shape=jax.ShapeDtypeStruct((copies,) + x.shape, x.dtype),
-        in_specs=[VMEM],
-        out_specs=VMEM,
+        out_shape=pltpu.HBM((copies,) + x.shape, x.dtype),
+        in_specs=[ANY],
+        out_specs=ANY,
+        scratch_shapes=[pltpu.VMEM(x.shape, x.dtype), pltpu.SemaphoreType.DMA((copies,))],
         compiler_params=params(),
         name="make_copies",
-    )(x)
+    )(pltpu.with_memory_space_constraint(x, pltpu.HBM))
 
 
 def call_finish_sources(log_targets, n_tgt, first, change):
@@ -351,17 +347,16 @@
     )(yt, x)
 
 
-def call_over_sources(log_targets, e, yt, xa, part_shape, part_type, *parts, at_once=128):
+def call_over_sources(log_targets, e, yt, xa, part_shape, part_type, *parts):
     n_tgt, n_src = e.shape
     return pl.pallas_call(
-        functools.partial(over_sources, log_targets, at_once, len(parts)),
+        functools.partial(over_sources, log_targets, len(parts)),
         out_shape=jax.ShapeDtypeStruct(part_shape, part_type),
         in_specs=[VMEM] * len(parts) + [VMEM, ANY, ANY],
         out_specs=VMEM,
         scratch_shapes=[
             pltpu.VMEM((n_tgt // LANES, LANES), F32),
             pltpu.VMEM((n_src // LANES, LANES), F32),
-            pltpu.VMEM((n_tgt, LANES), F32),
             pltpu.VMEM(yt.shape, BF16),
             pltpu.VMEM(xa.shape, BF16),
         ],
@@ -370,10 +365,10 @@
     )(*parts, e, yt, xa)
 
 
-def call_over_targets(log_sources, parts, before, e, yt, xa, copies, at_once=128):
+def call_over_targets(log_sources, parts, before, e, yt, xa, copies):
     n_tgt, n_src = e.shape
     return pl.pallas_call(
-        functools.partial(over_targets, log_sources, at_once),
+        functools.partial(over_targets, log_sources),
         out_shape=jax.ShapeDtypeStruct((copies, n_src // LANES, LANES), BF16),
         in_specs=[VMEM, VMEM, VMEM, ANY, ANY],
         out_specs=VMEM,

time: 386 us -> 385 us (level)
  no operation moved by 1% of the time
where the time goes in v8:
time: 385 us
  Pallas kernels  289 us (75%)
  blocking collectives  58 us (15%)
  starting transfers between devices  21.1 us (5%)
  waiting for transfers between devices  15 us (4%)
    pallas_call x2, Pallas kernels, call_over_sources(): pl.pallas_call(functools.partial(over_sources, log_targets, len(parts)),...  178 us
    pallas_call x1, Pallas kernels, call_first(): pl.pallas_call(functools.partial(first_over_targets, tile), out_shape=(pl...  54.7 us
    pallas_call x1, Pallas kernels, call_over_targets(): pl.pallas_call(functools.partial(over_targets, log_sources), out_shape=ja...  53.9 us
    all_to_all x3, blocking collectives, exchange(): return lax.all_to_all(value, axis, 0, 0, tiled=False)  53.3 us
    all_to_all x2, starting transfers between devices, exchange(): return lax.all_to_all(value, axis, 0, 0, tiled=False)  21.1 us
    all_to_all x2, waiting for transfers between devices, exchange(): return lax.all_to_all(value, axis, 0, 0, tiled=False)  15 us
  transfers between devices with their start and end apart: 2, of which 2 were waited for; matrix products, arithmetic and copies ran while one was open for 0% of the time, Pallas kernels for 0%

profile of v8, /device:TPU:1, one launch (start us, length us, event | category | flops | bytes accessed | tf_op | source)
XLA Modules:
  0.0 384.9 jit_solution(16919848610600284097)
XLA Ops:
  0.6 1.6 make_copies.1
  2.2 15.8 %all-to-all-start = ((bf16[16,64,128]{2,1,0:T(8,128)(2,1)}), bf16[16,64,128]{2,1,0:T(8,128)(2,1)S(1)}, u32[]{:S(2)}, u32[]{:S(2)}) async-start(bf16[16,64,128]{2,1,0:T(8,128)(2,1)} %make_copies.1), calls=%async_computation | async-start | bytes 524288 | tf_op jit(solution)/shard_map/all_to_all | solution.py:387
  18.0 2.8 all-gather
  20.8 0.4 prep_targets.1.yt_ref.refs_2_.refs_3_
  21.1 10.0 %all-to-all-done.x_ref = bf16[16,64,128]{2,1,0:T(8,128)(2,1)S(1)} async-done(((bf16[16,64,128]{2,1,0:T(8,128)(2,1)}), bf16[16,64,128]{2,1,0:T(8,128)(2,1)S(1)}, u32[]{:S(2)}, u32[]{:S(2)}) %all-to-all-start) | async-done | bytes 262176 | tf_op jit(solution)/shard_map/all_to_all | solution.py:387
  31.1 54.7 %first_over_targets.1 = (f32[2048,2048]{1,0:T(8,128)S(1)}, bf16[256,2048]{1,0:T(8,128)(2,1)S(1)}, bf16[16,16,128]{2,1,0:T(8,128)(2,1)S(1)}) custom-call(bf16[2048,256]{1,0:T(8,128)(2,1)S(1)} %prep_targets.1.yt_ref.refs_2_.refs_3_, bf16[16,64,128]{2,1,0:T(8,128)(2,1)S(1)} %all-to-all-done.x_ref), custom_call_target="tpu_custom_call" | custom-call | tf_op jit(solution)/shard_map/first_over_targets/pallas_call | solution.py:335
  85.8 22.3 %all_to_all.25.refs_0_.first_ref = bf16[16,16,128]{2,1,0:T(8,128)(2,1)S(1)} all-to-all(bf16[16,16,128]{2,1,0:T(8,128)(2,1)S(1)} %get-tuple-element.5.before_ref), channel_id=1, replica_groups=mesh['row'=16,'z'=16,'core'=2] {'z'}, dimensions={0} | all-to-all | bytes 131072 | tf_op jit(solution)/shard_map/all_to_all | solution.py:387
  108.1 88.7 %over_sources.2 = bf16[32,16,128]{2,1,0:T(8,128)(2,1)S(1)} custom-call(bf16[16,16,128]{2,1,0:T(8,128)(2,1)S(1)} %all_to_all.25.refs_0_.first_ref, f32[2048,2048]{1,0:T(8,128)S(1)} %get-tuple-element.6.refs_1_.e_ref.refs_2_, bf16[2048,256]{1,0:T(8,128)(2,1)S(1)} %prep_targets.1.yt_ref.refs_2_.refs_3_, ...), custom_call_target="tpu_custom_call" | custom-call | tf_op jit(solution)/shard_map/over_sources/pallas_call | solution.py:352
  196.8 16.7 %all_to_all.26.parts_ref = bf16[32,16,128]{2,1,0:T(8,128)(2,1)S(1)} all-to-all(bf16[32,16,128]{2,1,0:T(8,128)(2,1)S(1)} %over_sources.2), channel_id=1, replica_groups=mesh['row'=16,'z'=16,'core'=2] {'row','core'}, dimensions={0} | all-to-all | bytes 262144 | tf_op jit(solution)/shard_map/all_to_all | solution.py:387
  213.5 53.9 %over_targets.1 = bf16[16,16,128]{2,1,0:T(8,128)(2,1)S(1)} custom-call(bf16[32,16,128]{2,1,0:T(8,128)(2,1)S(1)} %all_to_all.26.parts_ref, bf16[16,16,128]{2,1,0:T(8,128)(2,1)S(1)} %get-tuple-element.5.before_ref, f32[2048,2048]{1,0:T(8,128)S(1)} %get-tuple-element.6.refs_1_.e_ref.refs_2_, bf16[2048,256]{1,0:T(8,128)(2,1)S(1)} %prep_targets.1.yt_ref.refs_2_.refs_3_, ...), custom_call_target="tpu_custom_call" | custom-call | tf_op jit(solution)/shard_map/over_targets/pallas_call | solution.py:370
  267.4 14.3 %all_to_all.27.change_ref.refs_1_ = bf16[16,16,128]{2,1,0:T(8,128)(2,1)S(1)} all-to-all(bf16[16,16,128]{2,1,0:T(8,128)(2,1)S(1)} %over_targets.1), channel_id=1, replica_groups=mesh['row'=16,'z'=16,'core'=2] {'z'}, dimensions={0} | all-to-all | bytes 131072 | tf_op jit(solution)/shard_map/all_to_all | solution.py:387
  281.7 89.4 %over_sources.3 = f32[32,8,128]{2,1,0:T(8,128)} custom-call(bf16[16,16,128]{2,1,0:T(8,128)(2,1)S(1)} %all_to_all.25.refs_0_.first_ref, bf16[16,16,128]{2,1,0:T(8,128)(2,1)S(1)} %all_to_all.27.change_ref.refs_1_, f32[2048,2048]{1,0:T(8,128)S(1)} %get-tuple-element.6.refs_1_.e_ref.refs_2_, bf16[2048,256]{1,0:T(8,128)(2,1)S(1)} %prep_targets.1.yt_ref.refs_2_.refs_3_, ...), custom_call_target="tpu_custom_call" | custom-call | tf_op jit(solution)/shard_map/over_sources/pallas_call | solution.py:352
  371.1 5.4 %all-to-all-start.4 = ((f32[32,8,128]{2,1,0:T(8,128)}), f32[32,8,128]{2,1,0:T(8,128)S(1)}, u32[]{:S(2)}, u32[]{:S(2)}) async-start(f32[32,8,128]{2,1,0:T(8,128)} %over_sources.3), calls=%async_computation.4 | async-start | bytes 262144 | tf_op jit(solution)/shard_map/all_to_all | solution.py:387
  376.5 0.2 finish_sources.1
  376.7 1.8 all-gather.1
  378.6 0.6 copy.4
  379.2 5.0 %all-to-all-done.4.parts_ref = f32[32,8,128]{2,1,0:T(8,128)S(1)} async-done(((f32[32,8,128]{2,1,0:T(8,128)}), f32[32,8,128]{2,1,0:T(8,128)S(1)}, u32[]{:S(2)}, u32[]{:S(2)}) %all-to-all-start.4) | async-done | bytes 131104 | tf_op jit(solution)/shard_map/all_to_all | solution.py:387
  384.2 0.7 finish_targets.1
Async XLA Ops:
  2.2 28.9 %all-to-all-start = ((bf16[16,64,128]{2,1,0:T(8,128)(2,1)}), bf16[16,64,128]{2,1,0:T(8,128)(2,1)S(1)}, u32[]{:S(2)}, u32[]{:S(2)}) async-start(bf16[16,64,128]{2,1,0:T(8,128)(2,1)} %make_copies.1), calls=%async_computation | async-start | bytes 524288 | tf_op jit(solution)/shard_map/all_to_all | solution.py:387
  371.1 13.1 %all-to-all-start.4 = ((f32[32,8,128]{2,1,0:T(8,128)}), f32[32,8,128]{2,1,0:T(8,128)S(1)}, u32[]{:S(2)}, u32[]{:S(2)}) async-start(f32[32,8,128]{2,1,0:T(8,128)} %over_sources.3), calls=%async_computation.4 | async-start | bytes 262144 | tf_op jit(solution)/shard_map/all_to_all | solution.py:387

commit v9 on v8

--- a/solution.py
+++ b/solution.py
@@ -16,7 +16,9 @@
 FROM_LOG2 = EPS * math.log(2.0)
 LOW, HIGH = -91.0, 100.0
 F32, BF16 = jnp.float32, jnp.bfloat16
-ABOVE, BELOW, SHIFT, SMALL = 14.0, 4.0, -57.0, 2.0**-17
+LOW_SLOPE, MID_SLOPE, HIGH_SLOPE = 4.0, 18.0, 9.0
+KNEE, SHIFT, SMALL = 9.0, -72.0, 2.0**-13
+KNEE_HEIGHT = MID_SLOPE * KNEE
 
 
 def split3(v):
@@ -59,37 +61,19 @@
 def encode(d):
     size = jnp.abs(d)
     log = jnp.log2(jnp.maximum(size, SMALL))
-    t = jnp.exp2(log * jnp.where(log > 0.0, ABOVE, BELOW) + SHIFT)
-    t = jnp.where(size < SMALL, 0.0, t)
+    height = jnp.where(log > KNEE, KNEE_HEIGHT + HIGH_SLOPE * (log - KNEE), jnp.where(log > 0.0, MID_SLOPE, LOW_SLOPE) * log)
+    t = jnp.where(size < SMALL, 0.0, jnp.exp2(height + SHIFT))
     return jnp.where(d < 0.0, -t, t).astype(BF16)
 
 
 def decode(code):
     t = code.astype(F32)
     size = jnp.abs(t)
-    log = jnp.log2(jnp.maximum(size, 2.0**-126)) - SHIFT
-    d = jnp.exp2(log * jnp.where(log > 0.0, 1.0 / ABOVE, 1.0 / BELOW))
-    d = jnp.where(size > 0.0, d, 0.0)
+    height = jnp.log2(jnp.maximum(size, 2.0**-126)) - SHIFT
+    low = jnp.where(height > 0.0, 1.0 / MID_SLOPE, 1.0 / LOW_SLOPE) * height
+    log = jnp.where(height > KNEE_HEIGHT, KNEE + (height - KNEE_HEIGHT) * (1.0 / HIGH_SLOPE), low)
+    d = jnp.where(size > 0.0, jnp.exp2(log), 0.0)
     return jnp.where(t < 0.0, -d, d)
-
-
-def base_of(d, around):
-    a, b, c = (d[..., :1, k : k + 1] + around for k in range(3))
-    base = jnp.maximum(jnp.minimum(a, b), jnp.minimum(jnp.maximum(a, b), c))
-    at = [lax.broadcasted_iota(jnp.int32, d.shape, d.ndim - k) for k in (2, 1)]
-    return base, (at[0] == 0) & (at[1] < 3)
-
-
-def encode_from_base(value, around):
-    head = encode(value - around)
-    base, first = base_of(decode(head), around)
-    return jnp.where(first, head.astype(F32), encode(value - base).astype(F32)).astype(BF16)
-
-
-def decode_from_base(code, around):
-    d = decode(code)
-    base, first = base_of(d, around)
-    return jnp.where(first, around, base) + d
 
 
 def spread_to_rows(v, out_ref):
@@ -174,13 +158,13 @@
     for b in range(n_blocks):
         sum_ref[b : b + 1, :] = total[:, b * LANES : (b + 1) * LANES]
     totals = sum_ref[...]
-    send(encode_from_base(jnp.log2(totals), math.log2(n_tgt)), part_ref)
+    send(jnp.log2(totals), part_ref)
     fast = (jnp.min(totals) >= 2.0**LOW) & (jnp.max(totals) <= 2.0**HIGH)
 
     @pl.when(jnp.logical_not(fast))
     def _():
         slow_over_targets(yt_ref, xa_ref, None, sum_ref)
-        send(encode_from_base(sum_ref[...], math.log2(n_tgt)), part_ref)
+        send(sum_ref[...], part_ref)
 
 
 def checked(totals, pot):
@@ -189,8 +173,8 @@
     return (top <= HIGH) & (jnp.min(totals) >= floor)
 
 
-def row_sums(n_tgt, first, *changes):
-    return decode_from_base(first, math.log2(n_tgt)) + sum(decode(change) for change in changes)
+def row_sums(first, *changes):
+    return first + sum(decode(change) for change in changes)
 
 
 def over_sources(log_targets, n_parts, *refs):
@@ -198,7 +182,7 @@
     e_ref, yt_ref, xa_ref, part_ref, sum_ref, pot_ref, yt_buf, xa_buf = refs
     n_tgt, n_src = e_ref.shape
     n_blocks = n_src // LANES
-    pot = log_targets - merge(row_sums(n_tgt, *[ref[...] for ref in parts_refs]))
+    pot = log_targets - merge(row_sums(*[ref[...] for ref in parts_refs]))
     pot_ref[...] = pot
     u = jnp.exp2(jnp.minimum(pot, HIGH))
     u = [jnp.broadcast_to(u[b : b + 1], (8, LANES)) for b in range(n_blocks)]
@@ -245,7 +229,7 @@
     for b in range(n_blocks):
         sum_ref[b : b + 1, :] = jnp.sum(acc[b], axis=0, keepdims=True)
     totals = sum_ref[...]
-    before = row_sums(n_tgt, before_ref[0])
+    before = before_ref[0]
     send(encode(jnp.log2(totals) - before), part_ref)
 
     @pl.when(jnp.logical_not(checked(totals, pot)))
@@ -266,8 +250,8 @@
         copy.wait()
 
 
-def finish_sources(log_targets, n_tgt, first_ref, change_ref, out_ref):
-    out_ref[...] = FROM_LOG2 * (log_targets - merge(row_sums(n_tgt, first_ref[...], change_ref[...])))
+def finish_sources(log_targets, first_ref, change_ref, out_ref):
+    out_ref[...] = FROM_LOG2 * (log_targets - merge(row_sums(first_ref[...], change_ref[...])))
 
 
 def finish_targets(log_sources, parts_ref, out_ref):
@@ -307,9 +291,9 @@
     )(pltpu.with_memory_space_constraint(x, pltpu.HBM))
 
 
-def call_finish_sources(log_targets, n_tgt, first, change):
-    return pl.pallas_call(
-        functools.partial(finish_sources, log_targets, n_tgt),
+def call_finish_sources(log_targets, first, change):
+    return pl.pallas_call(
+        functools.partial(finish_sources, log_targets),
         out_shape=jax.ShapeDtypeStruct(first.shape[1:], F32),
         in_specs=[VMEM, VMEM],
         out_specs=VMEM,
@@ -337,7 +321,7 @@
         out_shape=(
             pltpu.VMEM((n_tgt, n_src), F32),
             jax.ShapeDtypeStruct((4 * width, n_src), BF16),
-            jax.ShapeDtypeStruct((copies, n_blocks, lanes), BF16),
+            jax.ShapeDtypeStruct((copies, n_blocks, lanes), F32),
         ),
         in_specs=[VMEM, VMEM],
         out_specs=(VMEM, VMEM, VMEM),
@@ -402,7 +386,7 @@
     col_parts = exchange(col_part, ("row", "core"))
     change = exchange(call_over_targets(log_sources, col_parts, part, e, yt, xa, n_z), "z")
     col_part = call_over_sources(log_targets, e, yt, xa, (group, tgt_own // LANES, LANES), F32, first, change)
-    src_pot = call_finish_sources(log_targets, n_tgt, first, change)
+    src_pot = call_finish_sources(log_targets, first, change)
     src_pot = lax.all_gather(src_pot, "core", axis=1)
     tgt_pot = call_finish(log_sources, exchange(col_part, ("row", "core")))
     return src_pot.reshape(n_core * n_z * src_own), tgt_pot.reshape(tgt_own)

time: 385 us -> 388 us (level)
  no operation moved by 1% of the time
where the time goes in v9:
time: 388 us; the launch traced here: 387 us
  Pallas kernels  289 us (74%)
  blocking collectives  60.5 us (16%)
  starting transfers between devices  21.4 us (6%)
  waiting for transfers between devices  15.1 us (4%)
    pallas_call x2, Pallas kernels, call_over_sources(): pl.pallas_call(functools.partial(over_sources, log_targets, len(parts)),...  178 us
    all_to_all x3, blocking collectives, exchange(): return lax.all_to_all(value, axis, 0, 0, tiled=False)  55.8 us
    pallas_call x1, Pallas kernels, call_first(): pl.pallas_call(functools.partial(first_over_targets, tile), out_shape=(pl...  54.5 us
    pallas_call x1, Pallas kernels, call_over_targets(): pl.pallas_call(functools.partial(over_targets, log_sources), out_shape=ja...  53.9 us
    all_to_all x2, starting transfers between devices, exchange(): return lax.all_to_all(value, axis, 0, 0, tiled=False)  21.4 us
    all_to_all x2, waiting for transfers between devices, exchange(): return lax.all_to_all(value, axis, 0, 0, tiled=False)  15.1 us
  transfers between devices with their start and end apart: 2, of which 2 were waited for; matrix products, arithmetic and copies ran while one was open for 0% of the time, Pallas kernels for 0%

profile of v9, /device:TPU:1, one launch (start us, length us, event | category | flops | bytes accessed | tf_op | source)
XLA Modules:
  0.0 387.2 jit_solution(12175086731389948691)
XLA Ops:
  0.6 1.6 make_copies.1
  2.2 15.8 %all-to-all-start = ((bf16[16,64,128]{2,1,0:T(8,128)(2,1)}), bf16[16,64,128]{2,1,0:T(8,128)(2,1)S(1)}, u32[]{:S(2)}, u32[]{:S(2)}) async-start(bf16[16,64,128]{2,1,0:T(8,128)(2,1)} %make_copies.1), calls=%async_computation | async-start | bytes 524288 | tf_op jit(solution)/shard_map/all_to_all | solution.py:371
  18.0 2.8 all-gather
  20.8 0.4 prep_targets.1.yt_ref.refs_2_.refs_3_
  21.1 10.0 %all-to-all-done.x_ref = bf16[16,64,128]{2,1,0:T(8,128)(2,1)S(1)} async-done(((bf16[16,64,128]{2,1,0:T(8,128)(2,1)}), bf16[16,64,128]{2,1,0:T(8,128)(2,1)S(1)}, u32[]{:S(2)}, u32[]{:S(2)}) %all-to-all-start) | async-done | bytes 262176 | tf_op jit(solution)/shard_map/all_to_all | solution.py:371
  31.1 54.5 %first_over_targets.1 = (f32[2048,2048]{1,0:T(8,128)S(1)}, bf16[256,2048]{1,0:T(8,128)(2,1)S(1)}, f32[16,16,128]{2,1,0:T(8,128)S(1)}) custom-call(bf16[2048,256]{1,0:T(8,128)(2,1)S(1)} %prep_targets.1.yt_ref.refs_2_.refs_3_, bf16[16,64,128]{2,1,0:T(8,128)(2,1)S(1)} %all-to-all-done.x_ref), custom_call_target="tpu_custom_call" | custom-call | tf_op jit(solution)/shard_map/first_over_targets/pallas_call | solution.py:319
  85.6 22.7 %all_to_all.25.refs_0_.first_ref = f32[16,16,128]{2,1,0:T(8,128)S(1)} all-to-all(f32[16,16,128]{2,1,0:T(8,128)S(1)} %get-tuple-element.5.before_ref), channel_id=1, replica_groups=mesh['row'=16,'z'=16,'core'=2] {'z'}, dimensions={0} | all-to-all | bytes 262144 | tf_op jit(solution)/shard_map/all_to_all | solution.py:371
  108.3 88.5 %over_sources.2 = bf16[32,16,128]{2,1,0:T(8,128)(2,1)S(1)} custom-call(f32[16,16,128]{2,1,0:T(8,128)S(1)} %all_to_all.25.refs_0_.first_ref, f32[2048,2048]{1,0:T(8,128)S(1)} %get-tuple-element.6.refs_1_.e_ref.refs_2_, bf16[2048,256]{1,0:T(8,128)(2,1)S(1)} %prep_targets.1.yt_ref.refs_2_.refs_3_, bf16[256,2048]{1,0:T(8,128)(2,1)S(1)} %get-tuple-element.7.refs_3_.xa_ref.refs_4_), custom_call_target="tpu_custom_call" | custom-call | tf_op jit(solution)/shard_map/over_sources/pallas_call | solution.py:336
  196.9 18.3 %all_to_all.26.parts_ref = bf16[32,16,128]{2,1,0:T(8,128)(2,1)S(1)} all-to-all(bf16[32,16,128]{2,1,0:T(8,128)(2,1)S(1)} %over_sources.2), channel_id=1, replica_groups=mesh['row'=16,'z'=16,'core'=2] {'row','core'}, dimensions={0} | all-to-all | bytes 262144 | tf_op jit(solution)/shard_map/all_to_all | solution.py:371
  215.1 53.9 %over_targets.1 = bf16[16,16,128]{2,1,0:T(8,128)(2,1)S(1)} custom-call(bf16[32,16,128]{2,1,0:T(8,128)(2,1)S(1)} %all_to_all.26.parts_ref, f32[16,16,128]{2,1,0:T(8,128)S(1)} %get-tuple-element.5.before_ref, f32[2048,2048]{1,0:T(8,128)S(1)} %get-tuple-element.6.refs_1_.e_ref.refs_2_, bf16[2048,256]{1,0:T(8,128)(2,1)S(1)} %prep_targets.1.yt_ref.refs_2_.refs_3_, ...), custom_call_target="tpu_custom_call" | custom-call | tf_op jit(solution)/shard_map/over_targets/pallas_call | solution.py:354
  269.0 14.9 %all_to_all.27.change_ref.refs_1_ = bf16[16,16,128]{2,1,0:T(8,128)(2,1)S(1)} all-to-all(bf16[16,16,128]{2,1,0:T(8,128)(2,1)S(1)} %over_targets.1), channel_id=1, replica_groups=mesh['row'=16,'z'=16,'core'=2] {'z'}, dimensions={0} | all-to-all | bytes 131072 | tf_op jit(solution)/shard_map/all_to_all | solution.py:371
  283.9 89.3 %over_sources.3 = f32[32,8,128]{2,1,0:T(8,128)} custom-call(f32[16,16,128]{2,1,0:T(8,128)S(1)} %all_to_all.25.refs_0_.first_ref, bf16[16,16,128]{2,1,0:T(8,128)(2,1)S(1)} %all_to_all.27.change_ref.refs_1_, f32[2048,2048]{1,0:T(8,128)S(1)} %get-tuple-element.6.refs_1_.e_ref.refs_2_, bf16[2048,256]{1,0:T(8,128)(2,1)S(1)} %prep_targets.1.yt_ref.refs_2_.refs_3_, ...), custom_call_target="tpu_custom_call" | custom-call | tf_op jit(solution)/shard_map/over_sources/pallas_call | solution.py:336
  373.2 5.6 %all-to-all-start.4 = ((f32[32,8,128]{2,1,0:T(8,128)}), f32[32,8,128]{2,1,0:T(8,128)S(1)}, u32[]{:S(2)}, u32[]{:S(2)}) async-start(f32[32,8,128]{2,1,0:T(8,128)} %over_sources.3), calls=%async_computation.4 | async-start | bytes 262144 | tf_op jit(solution)/shard_map/all_to_all | solution.py:371
  378.8 0.1 finish_sources.1
  379.0 1.8 all-gather.1
  380.8 0.6 copy.4
  381.4 5.1 %all-to-all-done.4.parts_ref = f32[32,8,128]{2,1,0:T(8,128)S(1)} async-done(((f32[32,8,128]{2,1,0:T(8,128)}), f32[32,8,128]{2,1,0:T(8,128)S(1)}, u32[]{:S(2)}, u32[]{:S(2)}) %all-to-all-start.4) | async-done | bytes 131104 | tf_op jit(solution)/shard_map/all_to_all | solution.py:371
  386.6 0.7 finish_targets.1
Async XLA Ops:
  2.2 28.9 %all-to-all-start = ((bf16[16,64,128]{2,1,0:T(8,128)(2,1)}), bf16[16,64,128]{2,1,0:T(8,128)(2,1)S(1)}, u32[]{:S(2)}, u32[]{:S(2)}) async-start(bf16[16,64,128]{2,1,0:T(8,128)(2,1)} %make_copies.1), calls=%async_computation | async-start | bytes 524288 | tf_op jit(solution)/shard_map/all_to_all | solution.py:371
  373.2 13.4 %all-to-all-start.4 = ((f32[32,8,128]{2,1,0:T(8,128)}), f32[32,8,128]{2,1,0:T(8,128)S(1)}, u32[]{:S(2)}, u32[]{:S(2)}) async-start(f32[32,8,128]{2,1,0:T(8,128)} %over_sources.3), calls=%async_computation.4 | async-start | bytes 262144 | tf_op jit(solution)/shard_map/all_to_all | solution.py:371

commit v10 on v9

--- a/solution.py
+++ b/solution.py
@@ -74,6 +74,31 @@
     log = jnp.where(height > KNEE_HEIGHT, KNEE + (height - KNEE_HEIGHT) * (1.0 / HIGH_SLOPE), low)
     d = jnp.where(size > 0.0, jnp.exp2(log), 0.0)
     return jnp.where(t < 0.0, -d, d)
+
+
+def finest(d):
+    size = jnp.abs(d)
+    slope = jnp.where(size < 1.02, 1.0 / LOW_SLOPE, jnp.where(size > 0.98 * 2.0**KNEE, 1.0 / HIGH_SLOPE, 1.0 / MID_SLOPE))
+    return jnp.maximum(size * slope * (1.1 * 2.0**-8), 1.05 * SMALL)
+
+
+def pack(d):
+    n = d.shape[0]
+    code = encode(d)
+    near = decode(code)
+    lost = jnp.clip((d - near) / finest(near), -1.0, 1.0)
+    level = jnp.floor((lost + 1.0) * 63.5 + 0.5)
+    pair = jnp.exp2(level[: n // 2] - 64.0) * (1.0 + level[n // 2 :] * (1.0 / 128.0))
+    return jnp.concatenate([code.astype(F32), pair], axis=0).astype(BF16)
+
+
+def unpack(packed):
+    values = packed.astype(F32)
+    n = values.shape[-2] * 2 // 3
+    near, pair = decode(values[..., :n, :]), values[..., n:, :]
+    exponent = jnp.floor(jnp.log2(pair * (1.0 + 2.0**-9)))
+    level = jnp.concatenate([exponent + 64.0, (pair * jnp.exp2(-exponent) - 1.0) * 128.0], axis=-2)
+    return near + (level * (1.0 / 63.5) - 1.0) * finest(near)
 
 
 def spread_to_rows(v, out_ref):
@@ -158,13 +183,13 @@
     for b in range(n_blocks):
         sum_ref[b : b + 1, :] = total[:, b * LANES : (b + 1) * LANES]
     totals = sum_ref[...]
-    send(jnp.log2(totals), part_ref)
+    send(pack(jnp.log2(totals) - math.log2(n_tgt)), part_ref)
     fast = (jnp.min(totals) >= 2.0**LOW) & (jnp.max(totals) <= 2.0**HIGH)
 
     @pl.when(jnp.logical_not(fast))
     def _():
         slow_over_targets(yt_ref, xa_ref, None, sum_ref)
-        send(sum_ref[...], part_ref)
+        send(pack(sum_ref[...] - math.log2(n_tgt)), part_ref)
 
 
 def checked(totals, pot):
@@ -173,8 +198,8 @@
     return (top <= HIGH) & (jnp.min(totals) >= floor)
 
 
-def row_sums(first, *changes):
-    return first + sum(decode(change) for change in changes)
+def row_sums(n_tgt, first, *changes):
+    return math.log2(n_tgt) + unpack(first) + sum(decode(change) for change in changes)
 
 
 def over_sources(log_targets, n_parts, *refs):
@@ -182,7 +207,7 @@
     e_ref, yt_ref, xa_ref, part_ref, sum_ref, pot_ref, yt_buf, xa_buf = refs
     n_tgt, n_src = e_ref.shape
     n_blocks = n_src // LANES
-    pot = log_targets - merge(row_sums(*[ref[...] for ref in parts_refs]))
+    pot = log_targets - merge(row_sums(n_tgt, *[ref[...] for ref in parts_refs]))
     pot_ref[...] = pot
     u = jnp.exp2(jnp.minimum(pot, HIGH))
     u = [jnp.broadcast_to(u[b : b + 1], (8, LANES)) for b in range(n_blocks)]
@@ -229,7 +254,7 @@
     for b in range(n_blocks):
         sum_ref[b : b + 1, :] = jnp.sum(acc[b], axis=0, keepdims=True)
     totals = sum_ref[...]
-    before = before_ref[0]
+    before = row_sums(n_tgt, before_ref[0])
     send(encode(jnp.log2(totals) - before), part_ref)
 
     @pl.when(jnp.logical_not(checked(totals, pot)))
@@ -250,8 +275,8 @@
         copy.wait()
 
 
-def finish_sources(log_targets, first_ref, change_ref, out_ref):
-    out_ref[...] = FROM_LOG2 * (log_targets - merge(row_sums(first_ref[...], change_ref[...])))
+def finish_sources(log_targets, n_tgt, first_ref, change_ref, out_ref):
+    out_ref[...] = FROM_LOG2 * (log_targets - merge(row_sums(n_tgt, first_ref[...], change_ref[...])))
 
 
 def finish_targets(log_sources, parts_ref, out_ref):
@@ -291,10 +316,10 @@
     )(pltpu.with_memory_space_constraint(x, pltpu.HBM))
 
 
-def call_finish_sources(log_targets, first, change):
-    return pl.pallas_call(
-        functools.partial(finish_sources, log_targets),
-        out_shape=jax.ShapeDtypeStruct(first.shape[1:], F32),
+def call_finish_sources(log_targets, n_tgt, first, change):
+    return pl.pallas_call(
+        functools.partial(finish_sources, log_targets, n_tgt),
+        out_shape=jax.ShapeDtypeStruct(change.shape[1:], F32),
         in_specs=[VMEM, VMEM],
         out_specs=VMEM,
         compiler_params=params(),
@@ -321,7 +346,7 @@
         out_shape=(
             pltpu.VMEM((n_tgt, n_src), F32),
             jax.ShapeDtypeStruct((4 * width, n_src), BF16),
-            jax.ShapeDtypeStruct((copies, n_blocks, lanes), F32),
+            jax.ShapeDtypeStruct((copies, n_blocks + n_blocks // 2, lanes), BF16),
         ),
         in_specs=[VMEM, VMEM],
         out_specs=(VMEM, VMEM, VMEM),
@@ -386,7 +411,7 @@
     col_parts = exchange(col_part, ("row", "core"))
     change = exchange(call_over_targets(log_sources, col_parts, part, e, yt, xa, n_z), "z")
     col_part = call_over_sources(log_targets, e, yt, xa, (group, tgt_own // LANES, LANES), F32, first, change)
-    src_pot = call_finish_sources(log_targets, first, change)
+    src_pot = call_finish_sources(log_targets, n_tgt, first, change)
     src_pot = lax.all_gather(src_pot, "core", axis=1)
     tgt_pot = call_finish(log_sources, exchange(col_part, ("row", "core")))
     return src_pot.reshape(n_core * n_z * src_own), tgt_pot.reshape(tgt_own)

time: 388 us -> 387 us (level)
  no operation moved by 1% of the time
where the time goes in v10:
time: 387 us; the launch traced here: 386 us
  Pallas kernels  290 us (75%)
  blocking collectives  59.1 us (15%)
  starting transfers between devices  21.4 us (6%)
  waiting for transfers between devices  14.9 us (4%)
    pallas_call x2, Pallas kernels, call_over_sources(): pl.pallas_call(functools.partial(over_sources, log_targets, len(parts)),...  178 us
    pallas_call x1, Pallas kernels, call_first(): pl.pallas_call(functools.partial(first_over_targets, tile), out_shape=(pl...  54.6 us
    all_to_all x3, blocking collectives, exchange(): return lax.all_to_all(value, axis, 0, 0, tiled=False)  54.4 us
    pallas_call x1, Pallas kernels, call_over_targets(): pl.pallas_call(functools.partial(over_targets, log_sources), out_shape=ja...  53.9 us
    all_to_all x2, starting transfers between devices, exchange(): return lax.all_to_all(value, axis, 0, 0, tiled=False)  21.4 us
    all_to_all x2, waiting for transfers between devices, exchange(): return lax.all_to_all(value, axis, 0, 0, tiled=False)  14.9 us
  transfers between devices with their start and end apart: 2, of which 2 were waited for; matrix products, arithmetic and copies ran while one was open for 0% of the time, Pallas kernels for 0%

profile of v10, /device:TPU:1, one launch (start us, length us, event | category | flops | bytes accessed | tf_op | source)
XLA Modules:
  0.0 386.3 jit_solution(4461069922832684533)
XLA Ops:
  0.6 1.6 make_copies.1
  2.2 15.8 %all-to-all-start = ((bf16[16,64,128]{2,1,0:T(8,128)(2,1)}), bf16[16,64,128]{2,1,0:T(8,128)(2,1)S(1)}, u32[]{:S(2)}, u32[]{:S(2)}) async-start(bf16[16,64,128]{2,1,0:T(8,128)(2,1)} %make_copies.1), calls=%async_computation | async-start | bytes 524288 | tf_op jit(solution)/shard_map/all_to_all | solution.py:396
  18.0 2.8 all-gather
  20.8 0.4 prep_targets.1.yt_ref.refs_2_.refs_3_
  21.1 10.0 %all-to-all-done.x_ref = bf16[16,64,128]{2,1,0:T(8,128)(2,1)S(1)} async-done(((bf16[16,64,128]{2,1,0:T(8,128)(2,1)}), bf16[16,64,128]{2,1,0:T(8,128)(2,1)S(1)}, u32[]{:S(2)}, u32[]{:S(2)}) %all-to-all-start) | async-done | bytes 262176 | tf_op jit(solution)/shard_map/all_to_all | solution.py:396
  31.1 54.6 %first_over_targets.1 = (f32[2048,2048]{1,0:T(8,128)S(1)}, bf16[256,2048]{1,0:T(8,128)(2,1)S(1)}, bf16[16,24,128]{2,1,0:T(8,128)(2,1)S(1)}) custom-call(bf16[2048,256]{1,0:T(8,128)(2,1)S(1)} %prep_targets.1.yt_ref.refs_2_.refs_3_, bf16[16,64,128]{2,1,0:T(8,128)(2,1)S(1)} %all-to-all-done.x_ref), custom_call_target="tpu_custom_call" | custom-call | tf_op jit(solution)/shard_map/first_over_targets/pallas_call | solution.py:344
  85.7 22.6 %all_to_all.25.refs_0_.first_ref = bf16[16,24,128]{2,1,0:T(8,128)(2,1)S(1)} all-to-all(bf16[16,24,128]{2,1,0:T(8,128)(2,1)S(1)} %get-tuple-element.5.before_ref), channel_id=1, replica_groups=mesh['row'=16,'z'=16,'core'=2] {'z'}, dimensions={0} | all-to-all | bytes 196608 | tf_op jit(solution)/shard_map/all_to_all | solution.py:396
  108.2 88.8 %over_sources.2 = bf16[32,16,128]{2,1,0:T(8,128)(2,1)S(1)} custom-call(bf16[16,24,128]{2,1,0:T(8,128)(2,1)S(1)} %all_to_all.25.refs_0_.first_ref, f32[2048,2048]{1,0:T(8,128)S(1)} %get-tuple-element.6.refs_1_.e_ref.refs_2_, bf16[2048,256]{1,0:T(8,128)(2,1)S(1)} %prep_targets.1.yt_ref.refs_2_.refs_3_, ...), custom_call_target="tpu_custom_call" | custom-call | tf_op jit(solution)/shard_map/over_sources/pallas_call | solution.py:361
  197.0 17.2 %all_to_all.26.parts_ref = bf16[32,16,128]{2,1,0:T(8,128)(2,1)S(1)} all-to-all(bf16[32,16,128]{2,1,0:T(8,128)(2,1)S(1)} %over_sources.2), channel_id=1, replica_groups=mesh['row'=16,'z'=16,'core'=2] {'row','core'}, dimensions={0} | all-to-all | bytes 262144 | tf_op jit(solution)/shard_map/all_to_all | solution.py:396
  214.2 53.9 %over_targets.1 = bf16[16,16,128]{2,1,0:T(8,128)(2,1)S(1)} custom-call(bf16[32,16,128]{2,1,0:T(8,128)(2,1)S(1)} %all_to_all.26.parts_ref, bf16[16,24,128]{2,1,0:T(8,128)(2,1)S(1)} %get-tuple-element.5.before_ref, f32[2048,2048]{1,0:T(8,128)S(1)} %get-tuple-element.6.refs_1_.e_ref.refs_2_, bf16[2048,256]{1,0:T(8,128)(2,1)S(1)} %prep_targets.1.yt_ref.refs_2_.refs_3_, ...), custom_call_target="tpu_custom_call" | custom-call | tf_op jit(solution)/shard_map/over_targets/pallas_call | solution.py:379
  268.1 14.7 %all_to_all.27.change_ref.refs_1_ = bf16[16,16,128]{2,1,0:T(8,128)(2,1)S(1)} all-to-all(bf16[16,16,128]{2,1,0:T(8,128)(2,1)S(1)} %over_targets.1), channel_id=1, replica_groups=mesh['row'=16,'z'=16,'core'=2] {'z'}, dimensions={0} | all-to-all | bytes 131072 | tf_op jit(solution)/shard_map/all_to_all | solution.py:396
  282.8 89.5 %over_sources.3 = f32[32,8,128]{2,1,0:T(8,128)} custom-call(bf16[16,24,128]{2,1,0:T(8,128)(2,1)S(1)} %all_to_all.25.refs_0_.first_ref, bf16[16,16,128]{2,1,0:T(8,128)(2,1)S(1)} %all_to_all.27.change_ref.refs_1_, f32[2048,2048]{1,0:T(8,128)S(1)} %get-tuple-element.6.refs_1_.e_ref.refs_2_, bf16[2048,256]{1,0:T(8,128)(2,1)S(1)} %prep_targets.1.yt_ref.refs_2_.refs_3_, ...), custom_call_target="tpu_custom_call" | custom-call | tf_op jit(solution)/shard_map/over_sources/pallas_call | solution.py:361
  372.3 5.6 %all-to-all-start.4 = ((f32[32,8,128]{2,1,0:T(8,128)}), f32[32,8,128]{2,1,0:T(8,128)S(1)}, u32[]{:S(2)}, u32[]{:S(2)}) async-start(f32[32,8,128]{2,1,0:T(8,128)} %over_sources.3), calls=%async_computation.4 | async-start | bytes 262144 | tf_op jit(solution)/shard_map/all_to_all | solution.py:396
  377.9 0.3 finish_sources.1
  378.2 1.8 all-gather.1
  380.1 0.6 copy.4
  380.7 5.0 %all-to-all-done.4.parts_ref = f32[32,8,128]{2,1,0:T(8,128)S(1)} async-done(((f32[32,8,128]{2,1,0:T(8,128)}), f32[32,8,128]{2,1,0:T(8,128)S(1)}, u32[]{:S(2)}, u32[]{:S(2)}) %all-to-all-start.4) | async-done | bytes 131104 | tf_op jit(solution)/shard_map/all_to_all | solution.py:396
  385.6 0.7 finish_targets.1
Async XLA Ops:
  2.2 28.9 %all-to-all-start = ((bf16[16,64,128]{2,1,0:T(8,128)(2,1)}), bf16[16,64,128]{2,1,0:T(8,128)(2,1)S(1)}, u32[]{:S(2)}, u32[]{:S(2)}) async-start(bf16[16,64,128]{2,1,0:T(8,128)(2,1)} %make_copies.1), calls=%async_computation | async-start | bytes 524288 | tf_op jit(solution)/shard_map/all_to_all | solution.py:396
  372.3 13.4 %all-to-all-start.4 = ((f32[32,8,128]{2,1,0:T(8,128)}), f32[32,8,128]{2,1,0:T(8,128)S(1)}, u32[]{:S(2)}, u32[]{:S(2)}) async-start(f32[32,8,128]{2,1,0:T(8,128)} %over_sources.3), calls=%async_computation.4 | async-start | bytes 262144 | tf_op jit(solution)/shard_map/all_to_all | solution.py:396

commit v11 on v10

--- a/solution.py
+++ b/solution.py
@@ -198,16 +198,21 @@
     return (top <= HIGH) & (jnp.min(totals) >= floor)
 
 
-def row_sums(n_tgt, first, *changes):
-    return math.log2(n_tgt) + unpack(first) + sum(decode(change) for change in changes)
+def row_sums(first, change):
+    return first + decode(change)
 
 
 def over_sources(log_targets, n_parts, *refs):
     parts_refs, refs = refs[:n_parts], refs[n_parts:]
-    e_ref, yt_ref, xa_ref, part_ref, sum_ref, pot_ref, yt_buf, xa_buf = refs
+    e_ref, yt_ref, xa_ref, part_ref, *rows_ref, sum_ref, pot_ref, yt_buf, xa_buf = refs
     n_tgt, n_src = e_ref.shape
     n_blocks = n_src // LANES
-    pot = log_targets - merge(row_sums(n_tgt, *[ref[...] for ref in parts_refs]))
+    if n_parts == 1:
+        rows = math.log2(n_tgt) + unpack(parts_refs[0][...])
+        rows_ref[0][...] = rows
+    else:
+        rows = row_sums(*[ref[...] for ref in parts_refs])
+    pot = log_targets - merge(rows)
     pot_ref[...] = pot
     u = jnp.exp2(jnp.minimum(pot, HIGH))
     u = [jnp.broadcast_to(u[b : b + 1], (8, LANES)) for b in range(n_blocks)]
@@ -226,7 +231,7 @@
         if part_ref.dtype == BF16:
             value = encode(value - math.log2(n_src))
         for k in range(copies):
-            at = (k * n) % value.shape[0]
+            at = k * value.shape[0] // copies // n * n
             part_ref[k] = value[at : at + n]
 
     put(jnp.log2(totals))
@@ -254,7 +259,7 @@
     for b in range(n_blocks):
         sum_ref[b : b + 1, :] = jnp.sum(acc[b], axis=0, keepdims=True)
     totals = sum_ref[...]
-    before = row_sums(n_tgt, before_ref[0])
+    before = math.log2(n_tgt) + unpack(before_ref[0])
     send(encode(jnp.log2(totals) - before), part_ref)
 
     @pl.when(jnp.logical_not(checked(totals, pot)))
@@ -275,8 +280,8 @@
         copy.wait()
 
 
-def finish_sources(log_targets, n_tgt, first_ref, change_ref, out_ref):
-    out_ref[...] = FROM_LOG2 * (log_targets - merge(row_sums(n_tgt, first_ref[...], change_ref[...])))
+def finish_sources(log_targets, first_ref, change_ref, out_ref):
+    out_ref[...] = FROM_LOG2 * (log_targets - merge(row_sums(first_ref[...], change_ref[...])))
 
 
 def finish_targets(log_sources, parts_ref, out_ref):
@@ -316,9 +321,9 @@
     )(pltpu.with_memory_space_constraint(x, pltpu.HBM))
 
 
-def call_finish_sources(log_targets, n_tgt, first, change):
-    return pl.pallas_call(
-        functools.partial(finish_sources, log_targets, n_tgt),
+def call_finish_sources(log_targets, first, change):
+    return pl.pallas_call(
+        functools.partial(finish_sources, log_targets),
         out_shape=jax.ShapeDtypeStruct(change.shape[1:], F32),
         in_specs=[VMEM, VMEM],
         out_specs=VMEM,
@@ -358,11 +363,14 @@
 
 def call_over_sources(log_targets, e, yt, xa, part_shape, part_type, *parts):
     n_tgt, n_src = e.shape
+    out_shape = [jax.ShapeDtypeStruct(part_shape, part_type)]
+    if len(parts) == 1:
+        out_shape.append(jax.ShapeDtypeStruct((parts[0].shape[0], n_src // LANES, LANES), F32))
     return pl.pallas_call(
         functools.partial(over_sources, log_targets, len(parts)),
-        out_shape=jax.ShapeDtypeStruct(part_shape, part_type),
+        out_shape=out_shape,
         in_specs=[VMEM] * len(parts) + [VMEM, ANY, ANY],
-        out_specs=VMEM,
+        out_specs=[VMEM] * len(out_shape),
         scratch_shapes=[
             pltpu.VMEM((n_tgt // LANES, LANES), F32),
             pltpu.VMEM((n_src // LANES, LANES), F32),
@@ -407,13 +415,13 @@
     yt = call_prep(lax.all_gather(tgt_feat, "core"))
     e, xa, part = call_first(yt, x, n_z)
     first = exchange(part, "z")
-    col_part = call_over_sources(log_targets, e, yt, xa, (group, n_tgt // LANES, LANES), BF16, first)
-    col_parts = exchange(col_part, ("row", "core"))
+    col_part, first = call_over_sources(log_targets, e, yt, xa, (group, n_tgt // LANES, LANES), BF16, first)
+    col_parts = exchange(col_part, ("core", "row"))
     change = exchange(call_over_targets(log_sources, col_parts, part, e, yt, xa, n_z), "z")
-    col_part = call_over_sources(log_targets, e, yt, xa, (group, tgt_own // LANES, LANES), F32, first, change)
-    src_pot = call_finish_sources(log_targets, n_tgt, first, change)
+    (col_part,) = call_over_sources(log_targets, e, yt, xa, (group, tgt_own // LANES, LANES), F32, first, change)
+    src_pot = call_finish_sources(log_targets, first, change)
     src_pot = lax.all_gather(src_pot, "core", axis=1)
-    tgt_pot = call_finish(log_sources, exchange(col_part, ("row", "core")))
+    tgt_pot = call_finish(log_sources, exchange(col_part, ("core", "row")))
     return src_pot.reshape(n_core * n_z * src_own), tgt_pot.reshape(tgt_own)
 
 

time: 387 us -> 386 us (level)
  no operation moved by 1% of the time
where the time goes in v11:
time: 386 us
  Pallas kernels  289 us (75%)
  blocking collectives  59 us (15%)
  starting transfers between devices  21.5 us (6%)
  waiting for transfers between devices  14.9 us (4%)
    pallas_call x2, Pallas kernels, call_over_sources(): pl.pallas_call(functools.partial(over_sources, log_targets, len(parts)),...  178 us
    pallas_call x1, Pallas kernels, call_first(): pl.pallas_call(functools.partial(first_over_targets, tile), out_shape=(pl...  54.5 us
    all_to_all x3, blocking collectives, exchange(): return lax.all_to_all(value, axis, 0, 0, tiled=False)  54.3 us
    pallas_call x1, Pallas kernels, call_over_targets(): pl.pallas_call(functools.partial(over_targets, log_sources), out_shape=ja...  53.9 us
    all_to_all x2, starting transfers between devices, exchange(): return lax.all_to_all(value, axis, 0, 0, tiled=False)  21.5 us
    all_to_all x2, waiting for transfers between devices, exchange(): return lax.all_to_all(value, axis, 0, 0, tiled=False)  14.9 us
  transfers between devices with their start and end apart: 2, of which 2 were waited for; matrix products, arithmetic and copies ran while one was open for 0% of the time, Pallas kernels for 0%

profile of v11, /device:TPU:1, one launch (start us, length us, event | category | flops | bytes accessed | tf_op | source)
XLA Modules:
  0.0 385.9 jit_solution(14310627017073113407)
XLA Ops:
  0.6 1.6 make_copies.1
  2.2 15.8 %all-to-all-start = ((bf16[16,64,128]{2,1,0:T(8,128)(2,1)}), bf16[16,64,128]{2,1,0:T(8,128)(2,1)S(1)}, u32[]{:S(2)}, u32[]{:S(2)}) async-start(bf16[16,64,128]{2,1,0:T(8,128)(2,1)} %make_copies.1), calls=%async_computation | async-start | bytes 524288 | tf_op jit(solution)/shard_map/all_to_all | solution.py:404
  18.0 2.8 all-gather
  20.8 0.4 prep_targets.1.yt_ref.refs_2_.refs_3_
  21.1 10.0 %all-to-all-done.x_ref = bf16[16,64,128]{2,1,0:T(8,128)(2,1)S(1)} async-done(((bf16[16,64,128]{2,1,0:T(8,128)(2,1)}), bf16[16,64,128]{2,1,0:T(8,128)(2,1)S(1)}, u32[]{:S(2)}, u32[]{:S(2)}) %all-to-all-start) | async-done | bytes 262176 | tf_op jit(solution)/shard_map/all_to_all | solution.py:404
  31.1 54.5 %first_over_targets.1 = (f32[2048,2048]{1,0:T(8,128)S(1)}, bf16[256,2048]{1,0:T(8,128)(2,1)S(1)}, bf16[16,24,128]{2,1,0:T(8,128)(2,1)S(1)}) custom-call(bf16[2048,256]{1,0:T(8,128)(2,1)S(1)} %prep_targets.1.yt_ref.refs_2_.refs_3_, bf16[16,64,128]{2,1,0:T(8,128)(2,1)S(1)} %all-to-all-done.x_ref), custom_call_target="tpu_custom_call" | custom-call | tf_op jit(solution)/shard_map/first_over_targets/pallas_call | solution.py:349
  85.6 22.6 %all_to_all.25.refs_0_ = bf16[16,24,128]{2,1,0:T(8,128)(2,1)S(1)} all-to-all(bf16[16,24,128]{2,1,0:T(8,128)(2,1)S(1)} %get-tuple-element.7.before_ref), channel_id=1, replica_groups=mesh['row'=16,'z'=16,'core'=2] {'z'}, dimensions={0} | all-to-all | bytes 196608 | tf_op jit(solution)/shard_map/all_to_all | solution.py:404
  108.2 88.7 %over_sources.2 = (bf16[32,16,128]{2,1,0:T(8,128)(2,1)S(1)}, f32[16,16,128]{2,1,0:T(8,128)S(1)}) custom-call(bf16[16,24,128]{2,1,0:T(8,128)(2,1)S(1)} %all_to_all.25.refs_0_, f32[2048,2048]{1,0:T(8,128)S(1)} %get-tuple-element.8.refs_1_.e_ref.refs_2_, bf16[2048,256]{1,0:T(8,128)(2,1)S(1)} %prep_targets.1.yt_ref.refs_2_.refs_3_, ...), custom_call_target="tpu_custom_call" | custom-call | tf_op jit(solution)/shard_map/over_sources/pallas_call | solution.py:369
  197.0 17.1 %all_to_all.26.parts_ref = bf16[32,16,128]{2,1,0:T(8,128)(2,1)S(1)} all-to-all(bf16[32,16,128]{2,1,0:T(8,128)(2,1)S(1)} %get-tuple-element.11), channel_id=1, replica_groups=mesh['row'=16,'z'=16,'core'=2] {'core','row'}, dimensions={0} | all-to-all | bytes 262144 | tf_op jit(solution)/shard_map/all_to_all | solution.py:404
  214.1 53.9 %over_targets.1 = bf16[16,16,128]{2,1,0:T(8,128)(2,1)S(1)} custom-call(bf16[32,16,128]{2,1,0:T(8,128)(2,1)S(1)} %all_to_all.26.parts_ref, bf16[16,24,128]{2,1,0:T(8,128)(2,1)S(1)} %get-tuple-element.7.before_ref, f32[2048,2048]{1,0:T(8,128)S(1)} %get-tuple-element.8.refs_1_.e_ref.refs_2_, bf16[2048,256]{1,0:T(8,128)(2,1)S(1)} %prep_targets.1.yt_ref.refs_2_.refs_3_, ...), custom_call_target="tpu_custom_call" | custom-call | tf_op jit(solution)/shard_map/over_targets/pallas_call | solution.py:387
  268.0 14.7 %all_to_all.27.change_ref.refs_1_ = bf16[16,16,128]{2,1,0:T(8,128)(2,1)S(1)} all-to-all(bf16[16,16,128]{2,1,0:T(8,128)(2,1)S(1)} %over_targets.1), channel_id=1, replica_groups=mesh['row'=16,'z'=16,'core'=2] {'z'}, dimensions={0} | all-to-all | bytes 131072 | tf_op jit(solution)/shard_map/all_to_all | solution.py:404
  282.6 89.3 %over_sources.3 = f32[32,8,128]{2,1,0:T(8,128)} custom-call(f32[16,16,128]{2,1,0:T(8,128)S(1)} %get-tuple-element.10.first_ref.refs_0_, bf16[16,16,128]{2,1,0:T(8,128)(2,1)S(1)} %all_to_all.27.change_ref.refs_1_, f32[2048,2048]{1,0:T(8,128)S(1)} %get-tuple-element.8.refs_1_.e_ref.refs_2_, bf16[2048,256]{1,0:T(8,128)(2,1)S(1)} %prep_targets.1.yt_ref.refs_2_.refs_3_, ...), custom_call_target="tpu_custom_call" | custom-call | tf_op jit(solution)/shard_map/over_sources/pallas_call | solution.py:369
  371.9 5.8 %all-to-all-start.4 = ((f32[32,8,128]{2,1,0:T(8,128)}), f32[32,8,128]{2,1,0:T(8,128)S(1)}, u32[]{:S(2)}, u32[]{:S(2)}) async-start(f32[32,8,128]{2,1,0:T(8,128)} %over_sources.3), calls=%async_computation.4 | async-start | bytes 262144 | tf_op jit(solution)/shard_map/all_to_all | solution.py:404
  377.7 0.1 finish_sources.1
  377.9 1.8 all-gather.1
  379.7 0.6 copy.4
  380.3 5.0 %all-to-all-done.4.parts_ref = f32[32,8,128]{2,1,0:T(8,128)S(1)} async-done(((f32[32,8,128]{2,1,0:T(8,128)}), f32[32,8,128]{2,1,0:T(8,128)S(1)}, u32[]{:S(2)}, u32[]{:S(2)}) %all-to-all-start.4) | async-done | bytes 131104 | tf_op jit(solution)/shard_map/all_to_all | solution.py:404
  385.2 0.7 finish_targets.1
Async XLA Ops:
  2.2 28.9 %all-to-all-start = ((bf16[16,64,128]{2,1,0:T(8,128)(2,1)}), bf16[16,64,128]{2,1,0:T(8,128)(2,1)S(1)}, u32[]{:S(2)}, u32[]{:S(2)}) async-start(bf16[16,64,128]{2,1,0:T(8,128)(2,1)} %make_copies.1), calls=%async_computation | async-start | bytes 524288 | tf_op jit(solution)/shard_map/all_to_all | solution.py:404
  371.9 13.3 %all-to-all-start.4 = ((f32[32,8,128]{2,1,0:T(8,128)}), f32[32,8,128]{2,1,0:T(8,128)S(1)}, u32[]{:S(2)}, u32[]{:S(2)}) async-start(f32[32,8,128]{2,1,0:T(8,128)} %over_sources.3), calls=%async_computation.4 | async-start | bytes 262144 | tf_op jit(solution)/shard_map/all_to_all | solution.py:404
